TPU v7x, 32 devices: a whole 2x2x4 slice. The times are simulated.
32 devices in a mesh: dp: 16 (over z, y, core), cond: 2 (over x).
Axes of the slice: x: 2, y: 2, z: 4, core: 2. Of those that a mesh axis runs over, the one named last changes fastest.
Arguments:
- inputs: bfloat16 [1024, 16, 1152], P(('dp', 'cond')), may hold values from -6 to 6
- out_grad: bfloat16 [1024, 16, 1152], P(('dp', 'cond')), may hold values from -6 to 6
- frame_counts: int32 [4], replicated, may hold values from 8 to 16
- timesteps: int32 [4], replicated, may hold values from 0 to 999
- labels: int32 [4], replicated, may hold values from 0 to 100
- owners: int32 [7], replicated, may hold values from 0 to 1, as said below
- w_time: float32 [2, 256, 1152], P('cond', None, 'dp'), as said below
- w_table: float32 [2, 101, 1152], P('cond', None, 'dp'), as said below
- w_modulate: float32 [2, 1152, 6912], P('cond', None, 'dp'), as said below
- w_attend: float32 [2, 1152, 3456], P('cond', None, 'dp'), as said below
- w_merge: float32 [2, 1152, 1152], P('cond', None, 'dp'), as said below
- w_up: float32 [2, 1152, 4608], P('cond', None, 'dp'), as said below
- w_down: float32 [2, 4608, 1152], P('cond', None, 'dp'), as said below
- mean_time: float32 [2, 256, 1152], P('cond', None, 'dp'), as said below
- mean_table: float32 [2, 101, 1152], P('cond', None, 'dp'), as said below
- mean_modulate: float32 [2, 1152, 6912], P('cond', None, 'dp'), as said below
- mean_attend: float32 [2, 1152, 3456], P('cond', None, 'dp'), as said below
- mean_merge: float32 [2, 1152, 1152], P('cond', None, 'dp'), as said below
- mean_up: float32 [2, 1152, 4608], P('cond', None, 'dp'), as said below
- mean_down: float32 [2, 4608, 1152], P('cond', None, 'dp'), as said below
- square_time: float32 [2, 256, 1152], P('cond', None, 'dp'), as said below
- square_table: float32 [2, 101, 1152], P('cond', None, 'dp'), as said below
- square_modulate: float32 [2, 1152, 6912], P('cond', None, 'dp'), as said below
- square_attend: float32 [2, 1152, 3456], P('cond', None, 'dp'), as said below
- square_merge: float32 [2, 1152, 1152], P('cond', None, 'dp'), as said below
- square_up: float32 [2, 1152, 4608], P('cond', None, 'dp'), as said below
- square_down: float32 [2, 4608, 1152], P('cond', None, 'dp'), as said below
Outputs:
- block_out: bfloat16 [1024, 16, 1152], P(('dp', 'cond'))
- input_grad: bfloat16 [1024, 16, 1152], P(('dp', 'cond'))
- new_time: float32 [2, 256, 1152], P('cond', None, 'dp')
- new_table: float32 [2, 101, 1152], P('cond', None, 'dp')
- new_modulate: float32 [2, 1152, 6912], P('cond', None, 'dp')
- new_attend: float32 [2, 1152, 3456], P('cond', None, 'dp')
- new_merge: float32 [2, 1152, 1152], P('cond', None, 'dp')
- new_up: float32 [2, 1152, 4608], P('cond', None, 'dp')
- new_down: float32 [2, 4608, 1152], P('cond', None, 'dp')
- first_time: float32 [2, 256, 1152], P('cond', None, 'dp')
- first_table: float32 [2, 101, 1152], P('cond', None, 'dp')
- first_modulate: float32 [2, 1152, 6912], P('cond', None, 'dp')
- first_attend: float32 [2, 1152, 3456], P('cond', None, 'dp')
- first_merge: float32 [2, 1152, 1152], P('cond', None, 'dp')
- first_up: float32 [2, 1152, 4608], P('cond', None, 'dp')
- first_down: float32 [2, 4608, 1152], P('cond', None, 'dp')
- second_time: float32 [2, 256, 1152], P('cond', None, 'dp')
- second_table: float32 [2, 101, 1152], P('cond', None, 'dp')
- second_modulate: float32 [2, 1152, 6912], P('cond', None, 'dp')
- second_attend: float32 [2, 1152, 3456], P('cond', None, 'dp')
- second_merge: float32 [2, 1152, 1152], P('cond', None, 'dp')
- second_up: float32 [2, 1152, 4608], P('cond', None, 'dp')
- second_down: float32 [2, 4608, 1152], P('cond', None, 'dp')
- copy_time: bfloat16 [2, 256, 1152], P('cond', None, 'dp')
- copy_table: bfloat16 [2, 101, 1152], P('cond', None, 'dp')
- copy_modulate: bfloat16 [2, 1152, 6912], P('cond', None, 'dp')
- copy_attend: bfloat16 [2, 1152, 3456], P('cond', None, 'dp')
- copy_merge: bfloat16 [2, 1152, 1152], P('cond', None, 'dp')
- copy_up: bfloat16 [2, 1152, 4608], P('cond', None, 'dp')
- copy_down: bfloat16 [2, 4608, 1152], P('cond', None, 'dp')
Inputs may be any that keep to these rules, and one draw needn't show every extreme that they name: owners[k] is the slot of matrix k that holds it; the matrices are time, table, modulate, attend, merge, up, down in this order. `w_time`: slot owners[0] holds the matrix, the other slot zeros. `w_table`: slot owners[1] holds the matrix, the other slot zeros. `w_modulate`: slot owners[2] holds the matrix, the other slot zeros. `w_attend`: slot owners[3] holds the matrix, the other slot zeros. `w_merge`: slot owners[4] holds the matrix, the other slot zeros. `w_up`: slot owners[5] holds the matrix, the other slot zeros. `w_down`: slot owners[6] holds the matrix, the other slot zeros. `mean_time`: slot owners[0] holds the moment, the other slot zeros. `mean_table`: slot owners[1] holds the moment, the other slot zeros. `mean_modulate`: slot owners[2] holds the moment, the other slot zeros. `mean_attend`: slot owners[3] holds the moment, the other slot zeros. `mean_merge`: slot owners[4] holds the moment, the other slot zeros. `mean_up`: slot owners[5] holds the moment, the other slot zeros. `mean_down`: slot owners[6] holds the moment, the other slot zeros. `square_time`: slot owners[0] holds the moment, positive, the other slot zeros. `square_table`: slot owners[1] holds the moment, positive, the other slot zeros. `square_modulate`: slot owners[2] holds the moment, positive, the other slot zeros. `square_attend`: slot owners[3] holds the moment, positive, the other slot zeros. `square_merge`: slot owners[4] holds the moment, positive, the other slot zeros. `square_up`: slot owners[5] holds the moment, positive, the other slot zeros. `square_down`: slot owners[6] holds the moment, positive, the other slot zeros.
All inputs are finite; a program needn't handle non-finite values.
Results may differ from a plain program's by a relative error of at most 0.014.
The roundings to bfloat16 on the way count: a program that leaves them out, or rounds other values in their place, can miss the bound.
Values may be sent and summed in bfloat16 or wider, within the bound.
No kernel may reach another device: no remote copies, remote signals or barrier semaphores. Data moves between devices by JAX's collectives and lax.ppermute only.
A program may use at most 192 MiB of HBM per device.

v0:
```python
from functools import partial
import math

import jax
import jax.numpy as jnp
from jax import lax
from jax.sharding import PartitionSpec as P

D = 1152
HEADS = 16
HEAD = 72
FF = 4608
FREQ = 256
LABELS = 101
PATCHES = 256
STEP = 5


HIGHEST = lax.Precision.HIGHEST
EPSILON = 1e-06


def contract_rows(left, right, precision=None):
    return lax.dot_general(
        left,
        right,
        (((0,), (0,)), ((), ())),
        precision=precision,
        preferred_element_type=jnp.float32,
    )


def contract_cols(left, right, precision=None):
    return lax.dot_general(
        left,
        right,
        (((1,), (1,)), ((), ())),
        precision=precision,
        preferred_element_type=jnp.float32,
    )


def normalize(values):
    centre = values - jnp.mean(values, axis=-1, keepdims=True)
    spread = lax.rsqrt(jnp.mean(centre * centre, axis=-1, keepdims=True) + EPSILON)
    return (centre * spread, spread)


def normalize_back(upstream, normed, spread):
    return spread * (
        upstream
        - jnp.mean(upstream, axis=-1, keepdims=True)
        - normed * jnp.mean(upstream * normed, axis=-1, keepdims=True)
    )


def timestep_features(timesteps):
    half_count = FREQ // 2
    freqs = jnp.exp(-math.log(10000.0) * jnp.arange(half_count, dtype=jnp.float32) / half_count)
    angles = timesteps.astype(jnp.float32)[:, None] * freqs[None, :]
    return jnp.concatenate([jnp.cos(angles), jnp.sin(angles)], axis=1)


def adamw_step(master, first, second, grad, rate):
    first_new = 0.5 * first + 0.5 * grad
    second_new = 0.5 * second + 0.5 * grad * grad
    correct = 1.0 - 0.5**STEP
    update = first_new / correct / (jnp.sqrt(second_new / correct) + 1e-08)
    return (master - rate * (update + 0.01 * master), first_new, second_new)


def on_device(
    inputs,
    out_grad,
    frame_counts,
    timesteps,
    labels,
    owners,
    w_time,
    w_table,
    w_modulate,
    w_attend,
    w_merge,
    w_up,
    w_down,
    mean_time,
    mean_table,
    mean_modulate,
    mean_attend,
    mean_merge,
    mean_up,
    mean_down,
    square_time,
    square_table,
    square_modulate,
    square_attend,
    square_merge,
    square_up,
    square_down,
):
    masters = (w_time, w_table, w_modulate, w_attend, w_merge, w_up, w_down)
    means = (mean_time, mean_table, mean_modulate, mean_attend, mean_merge, mean_up, mean_down)
    squares = (
        square_time,
        square_table,
        square_modulate,
        square_attend,
        square_merge,
        square_up,
        square_down,
    )
    n_dp = lax.axis_size("dp")
    n_cond = lax.axis_size("cond")
    cond_index = lax.axis_index("cond")
    dp_index = lax.axis_index("dp")
    device = dp_index * n_cond + cond_index
    positions, frames, width = inputs.shape
    clips = timesteps.shape[0]
    clip_index = device * positions // PATCHES
    frame_count = lax.dynamic_index_in_dim(frame_counts, clip_index, 0, keepdims=False)
    both = (
        lax.all_gather(w_time.astype(jnp.bfloat16), "cond", axis=0, tiled=True),
        lax.all_gather(w_table.astype(jnp.bfloat16), "cond", axis=0, tiled=True),
        lax.all_gather(w_modulate.astype(jnp.bfloat16), "cond", axis=0, tiled=True),
        lax.all_gather(w_attend.astype(jnp.bfloat16), "cond", axis=0, tiled=True),
        lax.all_gather(w_merge.astype(jnp.bfloat16), "cond", axis=0, tiled=True),
        lax.all_gather(w_up.astype(jnp.bfloat16), "cond", axis=0, tiled=True),
        lax.all_gather(w_down.astype(jnp.bfloat16), "cond", axis=0, tiled=True),
    )
    owned = [
        lax.dynamic_index_in_dim(pair, owners[number], 0, keepdims=False)
        for number, pair in enumerate(both)
    ]
    time_w, table_w, attend_w, merge_w, up_w, down_w = (
        lax.all_gather(owned[0], "dp", axis=1, tiled=True),
        lax.all_gather(owned[1], "dp", axis=1, tiled=True),
        lax.all_gather(owned[3], "dp", axis=1, tiled=True),
        lax.all_gather(owned[4], "dp", axis=1, tiled=True),
        lax.all_gather(owned[5], "dp", axis=1, tiled=True),
        lax.all_gather(owned[6], "dp", axis=1, tiled=True),
    )
    half_width = owned[2].shape[1] // n_cond
    modulate_half = lax.dynamic_slice_in_dim(owned[2], cond_index * half_width, half_width, 1)
    features = timestep_features(timesteps).astype(jnp.bfloat16)
    time_pre = jnp.dot(features, time_w, preferred_element_type=jnp.float32)
    one_hot = (labels[:, None] == jnp.arange(LABELS)[None, :]).astype(jnp.bfloat16)
    cond_vec = jnp.dot(one_hot, table_w, preferred_element_type=jnp.float32) + jax.nn.silu(time_pre)
    cond_act, silu_back = jax.vjp(jax.nn.silu, cond_vec)
    cond_act = cond_act.astype(jnp.bfloat16)
    mod_part = jnp.dot(cond_act, modulate_half, preferred_element_type=jnp.float32)
    modulation = lax.all_gather(mod_part, ("dp", "cond"), axis=1, tiled=True)
    mod_row = lax.dynamic_index_in_dim(modulation, clip_index, 0, keepdims=False)
    shift_one, scale_one, gate_one, shift_two, scale_two, gate_two = [
        mod_row[part * width : (part + 1) * width] for part in range(6)
    ]
    rows = positions * frames
    tokens = inputs.reshape(rows, width).astype(jnp.float32)
    frame_ids = jnp.tile(jnp.arange(frames), positions)
    row_mask = (frame_ids < frame_count).astype(jnp.float32)[:, None]
    key_valid = jnp.arange(frames) < frame_count
    inv_scale = 1.0 / math.sqrt(HEAD)
    norm_one, rstd_one = normalize(tokens)
    hidden_one = (norm_one * (1.0 + scale_one) + shift_one).astype(jnp.bfloat16)
    qkv = jnp.dot(hidden_one, attend_w, preferred_element_type=jnp.float32).astype(jnp.bfloat16)
    queries = qkv[:, :width].reshape(positions, frames, HEADS, HEAD)
    key_rows = qkv[:, width : 2 * width].reshape(positions, frames, HEADS, HEAD)
    value_rows = qkv[:, 2 * width :].reshape(positions, frames, HEADS, HEAD)
    scores = (
        jnp.einsum("pfhe,pghe->phfg", queries, key_rows, preferred_element_type=jnp.float32)
        * inv_scale
    )
    scores = jnp.where(key_valid[None, None, None, :], scores, -1e30)
    top = jnp.max(scores, axis=-1, keepdims=True)
    expo = jnp.exp(scores - top)
    probs = expo / jnp.sum(expo, axis=-1, keepdims=True)
    probs_low = probs.astype(jnp.bfloat16)
    attended = jnp.einsum(
        "phfg,pghe->pfhe", probs_low, value_rows, preferred_element_type=jnp.float32
    )
    attended = attended.reshape(rows, width).astype(jnp.bfloat16)
    branch = jnp.dot(attended, merge_w, preferred_element_type=jnp.float32)
    middle = tokens + gate_one * branch
    norm_two, rstd_two = normalize(middle)
    hidden_two = (norm_two * (1.0 + scale_two) + shift_two).astype(jnp.bfloat16)
    upper = jnp.dot(hidden_two, up_w, preferred_element_type=jnp.float32)
    activ, gelu_back = jax.vjp(partial(jax.nn.gelu, approximate=True), upper)
    activ = activ.astype(jnp.bfloat16)
    mlp_out = jnp.dot(activ, down_w, preferred_element_type=jnp.float32)
    block_out = (
        (row_mask * (middle + gate_two * mlp_out))
        .reshape(positions, frames, width)
        .astype(jnp.bfloat16)
    )
    attend_b, merge_b, up_b, down_b = (
        lax.all_gather(owned[3], "dp", axis=1, tiled=True),
        lax.all_gather(owned[4], "dp", axis=1, tiled=True),
        lax.all_gather(owned[5], "dp", axis=1, tiled=True),
        lax.all_gather(owned[6], "dp", axis=1, tiled=True),
    )
    grad_out = out_grad.reshape(rows, width).astype(jnp.float32) * row_mask
    d_mlp = (grad_out * gate_two).astype(jnp.bfloat16)
    grad_down = contract_rows(activ, d_mlp)
    d_activ = contract_cols(d_mlp, down_b)
    d_upper = gelu_back(d_activ)[0].astype(jnp.bfloat16)
    grad_up = contract_rows(hidden_two, d_upper)
    d_hidden_two = contract_cols(d_upper, up_b)
    d_middle = grad_out + normalize_back(d_hidden_two * (1.0 + scale_two), norm_two, rstd_two)
    d_branch = (d_middle * gate_one).astype(jnp.bfloat16)
    grad_merge = contract_rows(attended, d_branch)
    d_attended = (
        contract_cols(d_branch, merge_b)
        .astype(jnp.bfloat16)
        .reshape(positions, frames, HEADS, HEAD)
    )
    d_probs = jnp.einsum(
        "pfhe,pghe->phfg", d_attended, value_rows, preferred_element_type=jnp.float32
    )
    d_values = jnp.einsum(
        "phfg,pfhe->pghe", probs_low, d_attended, preferred_element_type=jnp.float32
    )
    d_scores = (probs * (d_probs - jnp.sum(probs * d_probs, axis=-1, keepdims=True))).astype(
        jnp.bfloat16
    )
    d_queries = (
        jnp.einsum("phfg,pghe->pfhe", d_scores, key_rows, preferred_element_type=jnp.float32)
        * inv_scale
    )
    d_keys = (
        jnp.einsum("phfg,pfhe->pghe", d_scores, queries, preferred_element_type=jnp.float32)
        * inv_scale
    )
    d_qkv = jnp.concatenate(
        [
            d_queries.reshape(rows, width),
            d_keys.reshape(rows, width),
            d_values.reshape(rows, width),
        ],
        axis=1,
    ).astype(jnp.bfloat16)
    grad_attend = contract_rows(hidden_one, d_qkv)
    d_hidden_one = contract_cols(d_qkv, attend_b)
    d_tokens = d_middle + normalize_back(d_hidden_one * (1.0 + scale_one), norm_one, rstd_one)
    input_grad = d_tokens.reshape(positions, frames, width).astype(jnp.bfloat16)
    d_vector = jnp.concatenate(
        [
            jnp.sum(d_hidden_one, axis=0),
            jnp.sum(d_hidden_one * norm_one, axis=0),
            jnp.sum(d_middle * branch, axis=0),
            jnp.sum(d_hidden_two, axis=0),
            jnp.sum(d_hidden_two * norm_two, axis=0),
            jnp.sum(grad_out * mlp_out, axis=0),
        ]
    )
    clip_pick = (jnp.arange(clips) == clip_index).astype(jnp.float32)
    d_mod_local = clip_pick[:, None] * d_vector[None, :]
    d_mod_half = lax.psum_scatter(d_mod_local, ("dp", "cond"), scatter_dimension=1, tiled=True)
    grad_mod_half = contract_rows(cond_act.astype(jnp.float32), d_mod_half, HIGHEST)
    d_cond_part = contract_cols(d_mod_half, modulate_half.astype(jnp.float32), HIGHEST)
    d_cond_act = lax.psum(d_cond_part, ("dp", "cond"))
    d_cond = silu_back(d_cond_act)[0]
    grad_table = contract_rows(one_hot.astype(jnp.float32), d_cond, HIGHEST)
    d_time_pre = jax.vjp(jax.nn.silu, time_pre)[1](d_cond)[0]
    grad_time = contract_rows(features.astype(jnp.float32), d_time_pre, HIGHEST)
    span = width // n_dp
    grad_time_block = lax.dynamic_slice_in_dim(grad_time, dp_index * span, span, 1)
    grad_table_block = lax.dynamic_slice_in_dim(grad_table, dp_index * span, span, 1)
    blocks = (
        lax.psum_scatter(grad_attend, "dp", scatter_dimension=1, tiled=True),
        lax.psum_scatter(grad_merge, "dp", scatter_dimension=1, tiled=True),
        lax.psum_scatter(grad_up, "dp", scatter_dimension=1, tiled=True),
        lax.psum_scatter(grad_down, "dp", scatter_dimension=1, tiled=True),
    )
    placed = lax.dynamic_update_slice_in_dim(
        jnp.zeros((width, half_width * n_cond), jnp.float32),
        grad_mod_half,
        cond_index * half_width,
        1,
    )
    row_halves = (
        lax.psum_scatter(
            blocks[0].astype(jnp.bfloat16), "cond", scatter_dimension=0, tiled=True
        ).astype(jnp.float32),
        lax.psum_scatter(
            blocks[1].astype(jnp.bfloat16), "cond", scatter_dimension=0, tiled=True
        ).astype(jnp.float32),
        lax.psum_scatter(
            blocks[2].astype(jnp.bfloat16), "cond", scatter_dimension=0, tiled=True
        ).astype(jnp.float32),
        lax.psum_scatter(
            blocks[3].astype(jnp.bfloat16), "cond", scatter_dimension=0, tiled=True
        ).astype(jnp.float32),
        lax.psum_scatter(
            placed.astype(jnp.bfloat16), "cond", scatter_dimension=0, tiled=True
        ).astype(jnp.float32),
    )
    joined = (
        lax.all_gather(row_halves[0].astype(jnp.bfloat16), "cond", axis=0, tiled=True).astype(
            jnp.float32
        ),
        lax.all_gather(row_halves[1].astype(jnp.bfloat16), "cond", axis=0, tiled=True).astype(
            jnp.float32
        ),
        lax.all_gather(row_halves[2].astype(jnp.bfloat16), "cond", axis=0, tiled=True).astype(
            jnp.float32
        ),
        lax.all_gather(row_halves[3].astype(jnp.bfloat16), "cond", axis=0, tiled=True).astype(
            jnp.float32
        ),
        lax.all_gather(row_halves[4].astype(jnp.bfloat16), "cond", axis=0, tiled=True).astype(
            jnp.float32
        ),
    )
    grads = (
        grad_time_block,
        grad_table_block,
        joined[4],
        joined[0],
        joined[1],
        joined[2],
        joined[3],
    )
    rates = [
        0.5 * FREQ ** (-0.5),
        0.5,
        0.5 * D ** (-0.5),
        0.5 * D ** (-0.5),
        D ** (-0.5),
        0.5 * D ** (-0.5),
        0.5 * FF ** (-0.5),
    ]
    new_list, first_list, second_list, copy_list = ([], [], [], [])
    for number in range(7):
        fresh, first, second = adamw_step(
            masters[number][0], means[number][0], squares[number][0], grads[number], rates[number]
        )
        is_owner = cond_index == owners[number]
        fresh = jnp.where(is_owner, fresh, 0.0)[None]
        new_list.append(fresh)
        first_list.append(jnp.where(is_owner, first, 0.0)[None])
        second_list.append(jnp.where(is_owner, second, 0.0)[None])
        copy_list.append(fresh.astype(jnp.bfloat16))
    return (block_out, input_grad, *new_list, *first_list, *second_list, *copy_list)


def solution(mesh):
    return jax.shard_map(
        on_device,
        mesh=mesh,
        in_specs=(
            P(("dp", "cond"), None, None),
            P(("dp", "cond"), None, None),
            P(),
            P(),
            P(),
            P(),
            P("cond", None, "dp"),
            P("cond", None, "dp"),
            P("cond", None, "dp"),
            P("cond", None, "dp"),
            P("cond", None, "dp"),
            P("cond", None, "dp"),
            P("cond", None, "dp"),
            P("cond", None, "dp"),
            P("cond", None, "dp"),
            P("cond", None, "dp"),
            P("cond", None, "dp"),
            P("cond", None, "dp"),
            P("cond", None, "dp"),
            P("cond", None, "dp"),
            P("cond", None, "dp"),
            P("cond", None, "dp"),
            P("cond", None, "dp"),
            P("cond", None, "dp"),
            P("cond", None, "dp"),
            P("cond", None, "dp"),
            P("cond", None, "dp"),
        ),
        out_specs=(
            P(("dp", "cond"), None, None),
            P(("dp", "cond"), None, None),
            P("cond", None, "dp"),
            P("cond", None, "dp"),
            P("cond", None, "dp"),
            P("cond", None, "dp"),
            P("cond", None, "dp"),
            P("cond", None, "dp"),
            P("cond", None, "dp"),
            P("cond", None, "dp"),
            P("cond", None, "dp"),
            P("cond", None, "dp"),
            P("cond", None, "dp"),
            P("cond", None, "dp"),
            P("cond", None, "dp"),
            P("cond", None, "dp"),
            P("cond", None, "dp"),
            P("cond", None, "dp"),
            P("cond", None, "dp"),
            P("cond", None, "dp"),
            P("cond", None, "dp"),
            P("cond", None, "dp"),
            P("cond", None, "dp"),
            P("cond", None, "dp"),
            P("cond", None, "dp"),
            P("cond", None, "dp"),
            P("cond", None, "dp"),
            P("cond", None, "dp"),
            P("cond", None, "dp"),
            P("cond", None, "dp"),
        ),
        check_vma=False,
    )
```

profile of v0, /device:TPU:0, one launch (start us, length us, event | category | flops | bytes accessed | tf_op | source)
XLA Modules:
  0.0 1444.1 jit_solution(16215230211614687318)
XLA Ops:
  14.7 23.5 %all_gather.67 = bf16[2,1152,216]{1,2,0:T(8,128)(2,1)S(1)} all-gather(bf16[1,1152,216]{1,2,0:T(8,128)(2,1)S(1)} %convert_element_type.211), channel_id=1, replica_groups=mesh['dp'=16,'cond'=2] {'cond'}, dimensions={0}, use_global_device_ids=true | all-gather | bytes 1492992 | tf_op jit(solution)/shard_map/all_gather | solution.py:125
  41.1 6.5 all_gather.69
  54.3 18.9 %all-gather.23.cloned.1.call-done = bf16[2,4608,72]{1,2,0:T(8,128)(2,1)} async-done(((bf16[1,4608,72]{1,2,0:T(8,128)(2,1)}), bf16[2,4608,72]{1,2,0:T(8,128)(2,1)}) %all-gather.23.cloned.1.call-update) | async-done | bytes 1327120 | tf_op jit(solution)/shard_map/all_gather | solution.py:128
  83.3 4.8 all_gather.61
  88.1 5.4 all_gather.63
  93.5 22.1 %all-gather = bf16[1,101,1152]{1,2,0:T(8,128)(2,1)S(1)} all-gather(bf16[1,101,72]{1,2,0:T(8,128)(2,1)S(1)} %constant_dynamic-slice_fusion.5), channel_id=2, replica_groups=mesh['dp'=16,'cond'=2] {'dp'}, dimensions={2}, use_global_device_ids=true | all-gather | bytes 247248 | tf_op jit(solution)/shard_map/all_gather | solution.py:136
  117.4 20.9 %all-gather.1 = bf16[1,256,1152]{1,2,0:T(8,128)(2,1)S(1)} all-gather(bf16[1,256,72]{1,2,0:T(8,128)(2,1)S(1)} %constant_dynamic-slice_fusion.4), channel_id=3, replica_groups=mesh['dp'=16,'cond'=2] {'dp'}, dimensions={2}, use_global_device_ids=true | all-gather | bytes 626688 | tf_op jit(solution)/shard_map/all_gather | solution.py:135
  140.8 66.9 %all-gather.6 = f32[32,216,4]{1,2,0:T(4,128)S(1)} all-gather(f32[1,216,4]{1,2,0:T(4,128)S(1)} %convolution_bitcast_fusion), channel_id=1, replica_groups=mesh['dp'=16,'cond'=2] {'dp','cond'}, dimensions={0}, use_global_device_ids=true | all-gather | bytes 114048 | tf_op jit(solution)/shard_map/all_gather | solution.py:151
  211.5 8.5 fusion.22
  221.7 4.7 reshape.232
  226.3 5.0 reshape.234
  231.3 5.7 reshape.233
  246.0 4.7 convert_element_type.216
  250.8 5.4 fusion.147
  258.6 61.4 %all-gather.29.cloned.1.call-done = bf16[1,1152,4608]{1,2,0:T(8,128)(2,1)} async-done(((bf16[1,1152,288]{1,2,0:T(8,128)(2,1)}), bf16[1,1152,4608]{1,2,0:T(8,128)(2,1)}) %all-gather.29.cloned.1.call-update) | async-done | bytes 10616848 | tf_op jit(solution)/shard_map/all_gather | solution.py:139
  320.1 12.3 fusion.7
  332.4 77.5 %all-gather.31.cloned.1.call-done = bf16[1,4608,1152]{1,2,0:T(8,128)(2,1)} async-done(((bf16[1,4608,72]{1,2,0:T(8,128)(2,1)}), bf16[1,4608,1152]{1,2,0:T(8,128)(2,1)}) %all-gather.31.cloned.1.call-update) | async-done | bytes 10616848 | tf_op jit(solution)/shard_map/all_gather | solution.py:140
  409.8 15.2 %fusion.15 = bf16[512,4608]{1,0:T(8,128)(2,1)S(1)} fusion(f32[512,4608]{1,0:T(8,128)} %fusion.7, bf16[512,1152]{1,0:T(8,128)(2,1)} %fusion.32, bf16[1,4608,1152]{1,2,0:T(8,128)(2,1)} %all-gather.31.cloned.1.call-done), kind=kOutput, calls=%fused_computation.17 | convolution fusion | flops 5483003904 | bytes 25952256 | tf_op jit(solution)/shard_map/dot_general | solution.py:34
  425.1 8.7 multiply_reduce_fusion.1
  434.4 17.1 %fusion.33 = (f32[1152]{0:T(1024)}, bf16[512,1152]{1,0:T(8,128)(2,1)}, f32[1152]{0:T(1024)}, f32[512,1152]{1,0:T(8,128)}) fusion(bf16[32,16,1152]{2,1,0:T(8,128)(2,1)} %param.28, f32[512]{0:T(512)} %copy-done.50, f32[512,1152]{1,0:T(8,128)} %copy-done.13, f32[1152]{0:T(1024)} %copy-done.31, f32[512,1152]{1,0:T(8,128)} %get-tuple-element.94, ...), kind=kOutput, calls=%fused_computation.43 | convolution fusion | flops 5467666432 | bytes 31879168 | tf_op jit(solution)/shard_map/dot_general | solution.py:188
  451.5 5.3 convolution_convert_fusion
  456.8 6.1 reshape.235
  462.9 5.3 multiply_reduce_fusion
  476.5 4.6 reshape.236
  485.5 4.6 reshape.237
  492.2 3.6 reshape.238
  499.5 11.5 fusion.48
  511.9 5.3 fusion.91
  517.4 12.7 fusion.151
  530.2 100.6 %all-reduce.5.cloned.1.call-done = f32[4,6912]{1,0:T(4,128)} async-done(((f32[4,6912]{1,0:T(4,128)}), f32[4,6912]{1,0:T(4,128)}) %all-reduce.5.cloned.1.call-update) | async-done | bytes 110608
  636.5 14.5 %fusion.137 = f32[1152,4608]{0,1:T(8,128)} fusion(bf16[512,4608]{1,0:T(8,128)(2,1)} %copy-done.59, f32[512,1152]{1,0:T(8,128)} %copy-done.13, f32[1152]{0:T(1024)} %get-tuple-element.39, f32[1152]{0:T(1024)} %get-tuple-element.40, f32[512]{0:T(512)S(1)} %copy-done.52, f32[512]{0:T(512)S(1)} %copy-done.44), kind=kOutput, calls=%fused_computation.250 | convolution fusion | flops 5438767104 | bytes 28324864 | tf_op jit(solution)/shard_map/dot_general | solution.py:24
  651.0 64.1 %reduce-scatter.39.cloned.1.call-done = f32[1152,72]{0,1:T(8,128)} async-done(((f32[1152,1152]{0,1:T(8,128)}), f32[1152,72]{0,1:T(8,128)}) %reduce-scatter.39.cloned.1.call-update) | async-done | bytes 331792
  718.7 171.3 %reduce-scatter.37.cloned.1.call-done = f32[1152,216]{0,1:T(8,128)} async-done(((f32[1152,3456]{0,1:T(8,128)}), f32[1152,216]{0,1:T(8,128)}) %reduce-scatter.37.cloned.1.call-update) | async-done | bytes 995344
  894.2 13.0 fusion.138
  918.1 39.5 %psum.7 = f32[4,1152]{1,0:T(4,128)S(1)} all-reduce(f32[4,1152]{1,0:T(4,128)S(1)} %fusion.88), channel_id=1, replica_groups=mesh['dp'=16,'cond'=2] {'dp','cond'}, use_global_device_ids=true, to_apply=%region_18.19 | all-reduce | flops 4608 | bytes 36864 | tf_op jit(solution)/shard_map/psum | solution.py:259
  964.2 14.4 all-gather.7
  981.9 149.3 %reduce-scatter.23.cloned.1.call-done = f32[1152,288]{0,1:T(8,128)} async-done(((f32[1152,4608]{0,1:T(8,128)}), f32[1152,288]{0,1:T(8,128)}) %reduce-scatter.23.cloned.1.call-update) | async-done | bytes 1327120 | tf_op jit(solution)/shard_map/reduce_scatter | solution.py:270
  1133.9 7.8 convert_bitcast_fusion.2
  1146.1 5.2 all-gather.9
  1153.2 9.9 reduce-scatter.31.cloned.1.call-done
  1164.2 9.0 all-gather.8
  1174.4 206.1 %reduce-scatter.25.cloned.1.call-done = f32[4608,72]{0,1:T(8,128)} async-done(((f32[4608,1152]{0,1:T(8,128)}), f32[4608,72]{0,1:T(8,128)}) %reduce-scatter.25.cloned.1.call-update) | async-done | bytes 1327120 | tf_op jit(solution)/shard_map/reduce_scatter | solution.py:271
  1382.8 4.1 convert_bitcast_fusion.5
  1386.9 14.0 reduce-scatter.35.cloned.1.call-done
  1402.1 13.6 all-gather.10
  1418.3 5.8 convert_bitcast_fusion.4
  1424.1 8.0 all_gather.79
  1432.1 5.3 convert_bitcast_fusion.3
  (256 shorter events, 101.7 us)
Async XLA Ops:
  7.2 43.1 %all-gather.21.cloned.1.call-start = ((), (), s32[]{:S(2)}) async-start(), calls=%async_computation.10 | async-start | bytes 1990656 | tf_op jit(solution)/shard_map/all_gather | solution.py:127
  9.7 63.5 %all-gather.23.cloned.1.call-start = ((), (), s32[]{:S(2)}) async-start(), calls=%async_computation.11 | async-start | bytes 1990656 | tf_op jit(solution)/shard_map/all_gather | solution.py:128
  10.7 128.8 %all-gather.19.cloned.1.call-start = ((), (), s32[]{:S(2)}) async-start(), calls=%async_computation.9 | async-start | bytes 2985984 | tf_op jit(solution)/shard_map/all_gather | solution.py:124
  11.8 28.6 %copy-start.17 = (f32[1,1152,72]{1,2,0:T(8,128)S(1)}, f32[1,1152,72]{1,2,0:T(8,128)}, u32[]{:S(2)}) copy-start(f32[1,1152,72]{1,2,0:T(8,128)} %param.37) | copy-start | bytes 995332
  11.8 198.7 %all-gather.25.cloned.1.call-start = ((), (), s32[]{:S(2)}) async-start(), calls=%async_computation.15 | async-start | bytes 8460288 | tf_op jit(solution)/shard_map/all_gather | solution.py:137
  39.1 211.7 %all-gather.27.cloned.1.call-start = ((), (), s32[]{:S(2)}) async-start(), calls=%async_computation.16 | async-start | bytes 2820096 | tf_op jit(solution)/shard_map/all_gather | solution.py:138
  47.6 31.5 %copy-start.56 = (s32[4]{0:T(128)S(1)}, s32[4]{0:T(128)}, u32[]{:S(2)}) copy-start(s32[4]{0:T(128)} %param.29) | copy-start | bytes 52
  47.6 33.5 %copy-start.28 = (f32[1,101,72]{1,2,0:T(8,128)S(1)}, f32[1,101,72]{1,2,0:T(8,128)}, u32[]{:S(2)}) copy-start(f32[1,101,72]{1,2,0:T(8,128)} %param.34) | copy-start | bytes 87268
  47.6 33.6 %copy-start.24 = (f32[1,256,72]{1,2,0:T(8,128)S(1)}, f32[1,256,72]{1,2,0:T(8,128)}, u32[]{:S(2)}) copy-start(f32[1,256,72]{1,2,0:T(8,128)} %param.33) | copy-start | bytes 221188
  47.6 33.6 %copy-start.57 = (s32[4]{0:T(128)S(1)}, s32[4]{0:T(128)}, u32[]{:S(2)}) copy-start(s32[4]{0:T(128)} %param.30) | copy-start | bytes 52
  47.6 33.6 %copy-start = (bf16[32,16,1152]{2,1,0:T(8,128)(2,1)S(1)}, bf16[32,16,1152]{2,1,0:T(8,128)(2,1)}, u32[]{:S(2)}) copy-start(bf16[32,16,1152]{2,1,0:T(8,128)(2,1)} %param.27) | copy-start | bytes 3538948
  48.3 271.7 %all-gather.29.cloned.1.call-start = ((), (), s32[]{:S(2)}) async-start(), calls=%async_computation.17 | async-start | bytes 11280384 | tf_op jit(solution)/shard_map/all_gather | solution.py:139
  52.4 357.5 %all-gather.31.cloned.1.call-start = ((), (), s32[]{:S(2)}) async-start(), calls=%async_computation.18 | async-start | bytes 11280384 | tf_op jit(solution)/shard_map/all_gather | solution.py:140
  75.2 64.0 %copy-start.53 = (s32[4]{0:T(128)S(1)}, s32[4]{0:T(128)}, u32[]{:S(2)}) copy-start(s32[4]{0:T(128)} %param.31) | copy-start | bytes 52
  75.2 555.5 %all-reduce.5.cloned.1.call-start = ((), (), s32[]{:S(2)}) async-start(), calls=%async_computation.23 | async-start | bytes 221184
  80.4 128.2 %copy-start.50 = (f32[512]{0:T(512)}, f32[512]{0:T(512)S(1)}, u32[]{:S(2)}) copy-start(f32[512]{0:T(512)S(1)} %reshape.239) | copy-start | bytes 6148
  81.5 128.5 %copy-start.34 = (f32[512]{0:T(512)}, f32[512]{0:T(512)S(1)}, u32[]{:S(2)}) copy-start(f32[512]{0:T(512)S(1)} %div.129) | copy-start | bytes 6148
  81.5 127.1 %copy-start.20 = (bf16[32,16,1152]{2,1,0:T(8,128)(2,1)S(1)}, bf16[32,16,1152]{2,1,0:T(8,128)(2,1)}, u32[]{:S(2)}) copy-start(bf16[32,16,1152]{2,1,0:T(8,128)(2,1)} %param.28) | copy-start | bytes 3538948
  82.1 127.9 %copy-start.37 = (f32[512]{0:T(512)}, f32[512]{0:T(512)S(1)}, u32[]{:S(2)}) copy-start(f32[512]{0:T(512)S(1)} %rsqrt.20) | copy-start | bytes 6148
  117.4 20.9 %copy-start.40 = (bf16[4,128]{1,0:T(4,128)(2,1)}, bf16[4,128]{1,0:T(4,128)(2,1)S(1)}, u32[]{:S(2)}) copy-start(bf16[4,128]{1,0:T(4,128)(2,1)S(1)} %get-tuple-element.83) | copy-start | bytes 3076
  117.4 20.9 %copy-start.41 = (bf16[4,128]{1,0:T(4,128)(2,1)}, bf16[4,128]{1,0:T(4,128)(2,1)S(1)}, u32[]{:S(2)}) copy-start(bf16[4,128]{1,0:T(4,128)(2,1)S(1)} %get-tuple-element.84) | copy-start | bytes 3076
  409.8 15.2 %copy-start.14 = (f32[512,1152]{1,0:T(8,128)S(1)}, f32[512,1152]{1,0:T(8,128)}, u32[]{:S(2)}) copy-start(f32[512,1152]{1,0:T(8,128)} %copy-done.13) | copy-start | bytes 7077892
  409.8 15.2 %copy-start.43 = (f32[512]{0:T(512)S(1)}, f32[512]{0:T(512)}, u32[]{:S(2)}) copy-start(f32[512]{0:T(512)} %copy-done.42) | copy-start | bytes 6148
  409.8 15.2 %copy-start.45 = (f32[1152]{0:T(1024)S(1)}, f32[1152]{0:T(1024)}, u32[]{:S(2)}) copy-start(f32[1152]{0:T(1024)} %get-tuple-element.40) | copy-start | bytes 13828
  409.8 15.3 %copy-start.51 = (f32[512]{0:T(512)S(1)}, f32[512]{0:T(512)}, u32[]{:S(2)}) copy-start(f32[512]{0:T(512)} %add_rsqrt_fusion.1) | copy-start | bytes 6148
  409.8 15.3 %copy-start.55 = (bf16[1,1152,4608]{1,2,0:T(8,128)(2,1)S(1)}, bf16[1,1152,4608]{1,2,0:T(8,128)(2,1)}, u32[]{:S(2)}) copy-start(bf16[1,1152,4608]{1,2,0:T(8,128)(2,1)} %all-gather.29.cloned.1.call-done) | copy-start | bytes 31850500
  499.5 11.6 copy-start.48
  499.5 11.6 copy-start.54
  499.5 12.4 copy-start.2
  511.9 203.3 %reduce-scatter.39.cloned.1.call-start = ((), (), s32[]{:S(2)}) async-start(), calls=%async_computation.25 | async-start | bytes 5640192
  517.3 372.7 %reduce-scatter.37.cloned.1.call-start = ((), (), s32[]{:S(2)}) async-start(), calls=%async_computation.24 | async-start | bytes 16920576
  530.1 432.8 %reduce-scatter.29.cloned.1.call-start = ((), (), s32[]{:S(2)}) async-start(), calls=%async_computation.19 | async-start | bytes 1769472
  636.4 494.7 %reduce-scatter.23.cloned.1.call-start = ((), (), s32[]{:S(2)}) async-start(), calls=%async_computation.12 | async-start | bytes 22560768 | tf_op jit(solution)/shard_map/reduce_scatter | solution.py:270
  651.0 494.1 %reduce-scatter.33.cloned.1.call-start = ((), (), s32[]{:S(2)}) async-start(), calls=%async_computation.21 | async-start | bytes 442368
  718.6 444.4 %reduce-scatter.31.cloned.1.call-start = ((), (), s32[]{:S(2)}) async-start(), calls=%async_computation.20 | async-start | bytes 884736
  894.1 486.4 %reduce-scatter.25.cloned.1.call-start = ((), (), s32[]{:S(2)}) async-start(), calls=%async_computation.13 | async-start | bytes 22560768 | tf_op jit(solution)/shard_map/reduce_scatter | solution.py:271
  907.2 493.7 %reduce-scatter.35.cloned.1.call-start = ((), (), s32[]{:S(2)}) async-start(), calls=%async_computation.22 | async-start | bytes 1327104
  916.6 45.5 %copy-start.25 = (f32[1,256,72]{1,2,0:T(8,128)S(1)}, f32[1,256,72]{1,2,0:T(8,128)}, u32[]{:S(2)}) copy-start(f32[1,256,72]{1,2,0:T(8,128)} %param.33) | copy-start | bytes 221188
  916.6 45.5 %copy-start.29 = (f32[1,256,72]{1,2,0:T(8,128)S(1)}, f32[1,256,72]{1,2,0:T(8,128)}, u32[]{:S(2)}) copy-start(f32[1,256,72]{1,2,0:T(8,128)} %param.47) | copy-start | bytes 221188
  916.6 45.5 %copy-start.30 = (f32[1,256,72]{1,2,0:T(8,128)S(1)}, f32[1,256,72]{1,2,0:T(8,128)}, u32[]{:S(2)}) copy-start(f32[1,256,72]{1,2,0:T(8,128)} %param.40) | copy-start | bytes 221188
  981.9 152.0 %copy-start.4 = (f32[1,1152,432]{1,2,0:T(8,128)S(1)}, f32[1,1152,432]{1,2,0:T(8,128)}, u32[]{:S(2)}) copy-start(f32[1,1152,432]{1,2,0:T(8,128)} %param.35) | copy-start | bytes 5971972
  1133.8 18.0 %copy-start.18 = (f32[1,1152,72]{1,2,0:T(8,128)S(1)}, f32[1,1152,72]{1,2,0:T(8,128)}, u32[]{:S(2)}) copy-start(f32[1,1152,72]{1,2,0:T(8,128)} %param.37) | copy-start | bytes 995332
  1133.8 18.0 %copy-start.22 = (f32[1,1152,72]{1,2,0:T(8,128)S(1)}, f32[1,1152,72]{1,2,0:T(8,128)}, u32[]{:S(2)}) copy-start(f32[1,1152,72]{1,2,0:T(8,128)} %param.51) | copy-start | bytes 995332
  1133.8 18.0 %copy-start.23 = (f32[1,1152,72]{1,2,0:T(8,128)S(1)}, f32[1,1152,72]{1,2,0:T(8,128)}, u32[]{:S(2)}) copy-start(f32[1,1152,72]{1,2,0:T(8,128)} %param.44) | copy-start | bytes 995332
  1133.8 290.3 %reduce-scatter.27.cloned.1.call-start = ((), (), s32[]{:S(2)}) async-start(), calls=%async_computation.14 | async-start | bytes 995328 | tf_op jit(solution)/shard_map/reduce_scatter | solution.py:289
  1173.7 209.1 %copy-start.12 = (f32[1,1152,216]{1,2,0:T(8,128)S(1)}, f32[1,1152,216]{1,2,0:T(8,128)}, u32[]{:S(2)}) copy-start(f32[1,1152,216]{1,2,0:T(8,128)} %param.36) | copy-start | bytes 2985988
  1174.4 208.4 %copy-start.21 = (f32[1,1152,216]{1,2,0:T(8,128)S(1)}, f32[1,1152,216]{1,2,0:T(8,128)}, u32[]{:S(2)}) copy-start(f32[1,1152,216]{1,2,0:T(8,128)} %param.50) | copy-start | bytes 2985988
  1418.3 13.8 copy-start.6
  (29 other events, 121.4 us)
Sparse Core Ops, SparseCore 0:
  10.2 34.9 all-gather.20
  47.3 25.8 all-gather.22
  75.3 33.0 all-gather.18
  111.1 74.5 all-gather.24
  188.2 41.8 all-gather.26
  232.8 87.2 all-gather.28
  322.9 86.8 all-gather.30
  512.0 118.6 all-reduce.4
  634.8 80.3 reduce-scatter.38
  719.1 170.8 reduce-scatter.36
  892.8 20.8 reduce-scatter.28
  918.2 212.8 reduce-scatter.22
  1133.9 11.1 reduce-scatter.32
  1147.8 15.2 reduce-scatter.30
  1167.6 212.8 reduce-scatter.24
  1383.2 17.5 reduce-scatter.34
  1403.5 17.6 reduce-scatter.26
where the time goes:
time: 1450 us; the launch traced here: 1440 us
  waiting for transfers between devices  877 us (60%)
  blocking collectives  240 us (17%)
  matrix products  152 us (10%)
  local copies, waits for them, and re-layouts  87.7 us (6%)
  other arithmetic  54.5 us (4%)
  between operations  33 us (2%)
    unnamed x24, waiting for transfers between devices  364 us
    reduce_scatter x1, waiting for transfers between devices, on_device(): lax.psum_scatter(grad_down, 'dp', scatter_dimension=1, tiled=True)  206 us
    reduce_scatter x1, waiting for transfers between devices, on_device(): lax.psum_scatter(grad_up, 'dp', scatter_dimension=1, tiled=True)  149 us
    all_gather x1, waiting for transfers between devices, on_device(): lax.all_gather(owned[6], 'dp', axis=1, tiled=True)  77.5 us
    all_gather x1, blocking collectives, on_device(): modulation = lax.all_gather(mod_part, ('dp', 'cond'), axis=1, tiled=True)  66.9 us
    all_gather x1, waiting for transfers between devices, on_device(): lax.all_gather(owned[5], 'dp', axis=1, tiled=True)  61.4 us
    dot_general x7, matrix products, contract_rows(): lax.dot_general(left, right, (((0,), (0,)), ((), ())), precision=precisio...  50.7 us
    dot_general x5, matrix products, contract_cols(): lax.dot_general(left, right, (((1,), (1,)), ((), ())), precision=precisio...  42.1 us
  transfers between devices with their start and end apart: 17, of which 11 were waited for; matrix products, arithmetic and copies ran while one was open for 12% of the time, Pallas kernels for 0%

commit v1 on v0

--- a/solution.py
+++ b/solution.py
@@ -4,7 +4,9 @@
 import jax
 import jax.numpy as jnp
 from jax import lax
-from jax.sharding import PartitionSpec as P
+from jax.experimental import pallas as pl
+from jax.experimental.pallas import tpu as pltpu
+from jax.sharding import Mesh, PartitionSpec as P
 
 D = 1152
 HEADS = 16
@@ -12,6 +14,7 @@
 FF = 4608
 FREQ = 256
 LABELS = 101
+FRAMES = 16
 PATCHES = 256
 STEP = 5
 
@@ -67,6 +70,807 @@
     correct = 1.0 - 0.5**STEP
     update = first_new / correct / (jnp.sqrt(second_new / correct) + 1e-08)
     return (master - rate * (update + 0.01 * master), first_new, second_new)
+
+
+BF16, F32 = jnp.bfloat16, jnp.float32
+SLAB = 16
+GROUP = 128
+WIDE = 256
+
+
+def vmem(*shape, dtype=BF16):
+    return pltpu.VMEM(shape, dtype)
+
+
+def any_spec():
+    return pl.BlockSpec(memory_space=pl.ANY)
+
+
+def smem_spec():
+    return pl.BlockSpec(memory_space=pltpu.SMEM)
+
+
+def vmem_spec():
+    return pl.BlockSpec(memory_space=pltpu.VMEM)
+
+
+def dot_nn(left, right):
+    return lax.dot_general(left, right, (((1,), (0,)), ((), ())), preferred_element_type=F32)
+
+
+def dot_nt(left, right):
+    return lax.dot_general(left, right, (((1,), (1,)), ((), ())), preferred_element_type=F32)
+
+
+def run_kernel(body, operands, outs, scratch, ordered_after=(), mib=56, **kw):
+    arrays = [array for array, _ in operands] + list(ordered_after)
+    specs = [spec for _, spec in operands] + [any_spec() for _ in ordered_after]
+    n_in, n_dep = len(operands), len(ordered_after)
+
+    def kernel(*refs):
+        body(*refs[:n_in], *refs[n_in + n_dep :])
+
+    return pl.pallas_call(
+        kernel,
+        out_shape=[jax.ShapeDtypeStruct(shape, dtype) for shape, dtype in outs],
+        in_specs=specs,
+        out_specs=[vmem_spec() for _ in outs],
+        scratch_shapes=scratch,
+        compiler_params=pltpu.CompilerParams(vmem_limit_bytes=mib * 2**20),
+        cost_estimate=pl.CostEstimate(flops=1000, bytes_accessed=1000, transcendentals=0),
+        **kw,
+    )(*arrays)
+
+
+def block_order(place):
+    y, c = place[1], place[2]
+    for dc in range(2):
+        for dy in range(2):
+            yy = y if dy == 0 else 1 - y
+            cc = c if dc == 0 else 1 - c
+            for zz in range(4):
+                yield dc * 2 + dy, zz, (zz * 2 + yy) * 2 + cc
+
+
+def start_all(copies, sems):
+    made = [pltpu.make_async_copy(src, dst, sems.at[i]) for i, (src, dst) in enumerate(copies)]
+    for copy in made:
+        copy.start()
+    return made
+
+
+def attend_copies(pieces, place, wide):
+    x = place[3]
+    for pair, zz, b in block_order(place):
+        main, late = pieces[2 * pair], pieces[2 * pair + 1]
+        yield main.at[zz, 0], wide.at[b * 3]
+        yield main.at[zz, 2], wide.at[b * 3 + 1 + x]
+        yield late.at[zz], wide.at[b * 3 + 2 - x]
+
+
+def merge_copies(pieces, place, wide):
+    for pair, zz, b in block_order(place):
+        yield pieces[2 * pair].at[zz, 1], wide.at[b]
+
+
+UP_E, UP_L = 128, 80
+
+
+def up_copies(pieces, place, wide):
+    x = place[3]
+    size = UP_E + 2 * UP_L
+    for pair, zz, b in block_order(place):
+        main, late = pieces[2 * pair], pieces[2 * pair + 1]
+        row = pl.multiple_of(b * size, 16)
+        near = pl.multiple_of(b * size + UP_E + UP_L * x, 16)
+        other = pl.multiple_of(b * size + UP_E + UP_L - UP_L * x, 16)
+        yield main.at[zz, pl.ds(0, UP_E)], wide.at[pl.ds(row, UP_E)]
+        yield main.at[zz, pl.ds(UP_E, UP_L)], wide.at[pl.ds(near, UP_L)]
+        yield late.at[zz], wide.at[pl.ds(other, UP_L)]
+
+
+DOWN_E, DOWN_L = 2048, 1280
+
+
+def down_copies(pieces, place, wide):
+    x = place[3]
+    near = pl.multiple_of(DOWN_E + DOWN_L * x, 128)
+    other = pl.multiple_of(DOWN_E + DOWN_L - DOWN_L * x, 128)
+    for pair, zz, b in block_order(place):
+        main, late = pieces[2 * pair], pieces[2 * pair + 1]
+        yield main.at[zz, :, pl.ds(0, DOWN_E)], wide.at[b, :, pl.ds(0, DOWN_E)]
+        yield main.at[zz, :, pl.ds(DOWN_E, DOWN_L)], wide.at[b, :, pl.ds(near, DOWN_L)]
+        yield late.at[zz], wide.at[b, :, pl.ds(other, DOWN_L)]
+
+
+def rows_of(wide, first, count, cols=None):
+    value = wide[pl.ds(first, count)] if cols is None else wide[pl.ds(first, count), :, cols]
+    return value.astype(F32).reshape(count * HEAD, value.shape[-1]).astype(BF16)
+
+
+def norm_slab(values):
+    mean = jnp.sum(values, axis=1, keepdims=True) * (1.0 / D)
+    centre = values - mean
+    spread = lax.rsqrt(jnp.sum(centre * centre, axis=1, keepdims=True) * (1.0 / D) + EPSILON)
+    return centre * spread, spread
+
+
+def back_slab(upstream, normed, spread):
+    first = jnp.sum(upstream, axis=1, keepdims=True) * (1.0 / D)
+    second = jnp.sum(upstream * normed, axis=1, keepdims=True) * (1.0 / D)
+    return spread * (upstream - first - normed * second)
+
+
+def slabs(rows, size, body):
+    @pl.loop(0, rows // size)
+    def _(i):
+        body(pl.ds(pl.multiple_of(i * size, size), size))
+
+
+def fold(ref, value):
+    ref[...] += jnp.sum(value.reshape(value.shape[0] // 8, 8, value.shape[1]), axis=0)
+
+
+def turn(src, dst):
+    @pl.loop(0, src.shape[0] // GROUP)
+    def _(i):
+        at = pl.ds(pl.multiple_of(i * GROUP, GROUP), GROUP)
+        dst[:, at] = src[at].astype(F32).T
+
+
+def store_relative(ref, turned, y, c):
+    for b in range(16):
+        zz, yy, cc = b // 4, (b // 2) % 2, b % 2
+        dy = y if yy == 0 else 1 - y
+        dc = c if cc == 0 else 1 - c
+        ref[dc, dy * 4 + zz] = turned[b * HEAD : (b + 1) * HEAD].astype(BF16)
+
+
+def frame_mask(count):
+    keys = lax.broadcasted_iota(jnp.int32, (GROUP, GROUP), 0)
+    asks = lax.broadcasted_iota(jnp.int32, (GROUP, GROUP), 1)
+    return (keys // FRAMES == asks // FRAMES) & (keys % FRAMES < count)
+
+
+def probs_of(key, query, mask):
+    scores = dot_nn(key.astype(F32).T.astype(BF16), query) * (1.0 / math.sqrt(HEAD))
+    scores = jnp.where(mask, scores, -1e30)
+    top = jnp.max(scores, axis=0, keepdims=True)
+    expo = jnp.where(mask, jnp.exp(scores - top), 0.0)
+    return expo / jnp.sum(expo, axis=0, keepdims=True)
+
+
+def first_half_kernel(place, tokens, mods, *rest):
+    pieces, rest = rest[:8], rest[8:]
+    h1, qkv, attended, branch, h2, wide, merge, turned, sems = rest
+    copies = list(attend_copies(pieces, place, wide)) + list(merge_copies(pieces, place, merge))
+    copies = start_all(copies, sems)
+    rows = tokens.shape[0]
+
+    def norm_one(at):
+        normed, _ = norm_slab(tokens[at].astype(F32))
+        h1[at] = (normed * (1.0 + mods[1:2]) + mods[0:1]).astype(BF16)
+
+    slabs(rows, SLAB, norm_one)
+    for copy in copies:
+        copy.wait()
+
+    @pl.loop(0, 12)
+    def _(i):
+        value = dot_nt(rows_of(wide, i * 4, 4), h1[...])
+        for j in range(4):
+            qkv[i * 4 + j] = value[j * HEAD : (j + 1) * HEAD].astype(BF16)
+
+    mask = frame_mask(place[4])
+
+    @pl.loop(0, HEADS)
+    def _(head):
+        for group in range(rows // GROUP):
+            at = pl.ds(group * GROUP, GROUP)
+            probs = probs_of(qkv[HEADS + head, :, at], qkv[head, :, at], mask)
+            turned[head, :, at] = dot_nn(qkv[2 * HEADS + head, :, at], probs.astype(BF16))
+
+    for group in range(rows // GROUP):
+        at = pl.ds(group * GROUP, GROUP)
+        attended[at] = turned[:, :, at].reshape(D, GROUP).T.astype(BF16)
+    branch[...] = dot_nt(attended[...], rows_of(merge, 0, 16))
+
+    def norm_two(at):
+        middle = tokens[at].astype(F32) + mods[2:3] * branch[at]
+        normed, _ = norm_slab(middle)
+        h2[at] = (normed * (1.0 + mods[4:5]) + mods[3:4]).astype(BF16)
+
+    slabs(rows, SLAB, norm_two)
+
+
+def up_kernel(place, h2, *rest):
+    pieces, rest = rest[:8], rest[8:]
+    act, slope, wide, upper, sems = rest
+    for copy in start_all(list(up_copies(pieces, place, wide)), sems):
+        copy.wait()
+    rows = h2.shape[0]
+    root = math.sqrt(2.0 / math.pi)
+
+    @pl.loop(0, FF // WIDE)
+    def _(i):
+        cols = pl.ds(pl.multiple_of(i * WIDE, WIDE), WIDE)
+        upper[...] = dot_nt(h2[...], wide[cols])
+
+        def gelu(at):
+            u = upper[at]
+            square = u * u
+            bent = jnp.tanh(root * u * (1.0 + 0.044715 * square))
+            half = 0.5 * (1.0 + bent)
+            act[at, cols] = (u * half).astype(BF16)
+            rise = root * (1.0 + 3.0 * 0.044715 * square)
+            slope[at, cols] = (half + 0.5 * u * (1.0 - bent * bent) * rise).astype(BF16)
+
+        slabs(rows, 32, gelu)
+
+
+def start_back_kernel(place, out_grad, mods, d_mlp, relative, turned):
+    rows = out_grad.shape[0]
+
+    def scale(at):
+        frame = lax.broadcasted_iota(jnp.int32, (SLAB, 1), 0) % FRAMES
+        dy = jnp.where(frame < place[4], out_grad[at].astype(F32), 0.0)
+        d_mlp[at] = (dy * mods[5:6]).astype(BF16)
+
+    slabs(rows, SLAB, scale)
+    turn(d_mlp, turned)
+    store_relative(relative, turned, place[1], place[2])
+
+
+def d_upper_kernel(place, d_mlp, slope, *rest):
+    pieces, rest = rest[:8], rest[8:]
+    d_upper, d_upper_t, wide, value, sems = rest
+    for copy in start_all(list(down_copies(pieces, place, wide)), sems):
+        copy.wait()
+    rows = d_mlp.shape[0]
+
+    @pl.loop(0, FF // WIDE)
+    def _(i):
+        cols = pl.ds(pl.multiple_of(i * WIDE, WIDE), WIDE)
+        value[...] = dot_nn(d_mlp[...], rows_of(wide, 0, 16, cols))
+
+        @pl.loop(0, rows // GROUP)
+        def _(j):
+            at = pl.ds(pl.multiple_of(j * GROUP, GROUP), GROUP)
+            part = value[at] * slope[at, cols].astype(F32)
+            d_upper[at, cols] = part.astype(BF16)
+            d_upper_t[cols, at] = part.T.astype(BF16)
+
+
+def middle_back_kernel(place, d_upper, tokens, out_grad, branch, mods, *rest):
+    ups, firsts, rest = rest[:8], rest[8:16], rest[16:]
+    d_middle, d_branch, relative, d_att, sums, wide, merge, value, turned, fold_a, fold_b, fold_c, sems = rest
+    copies = list(up_copies(ups, place, wide)) + list(merge_copies(firsts, place, merge))
+    copies = start_all(copies, sems)
+    for copy in copies:
+        copy.wait()
+    rows = tokens.shape[0]
+    value[...] = dot_nn(d_upper[...], wide[...])
+    for ref in (fold_a, fold_b, fold_c):
+        ref[...] = jnp.zeros_like(ref)
+
+    def back(at):
+        d_h2 = value[at]
+        arm = branch[at]
+        normed, spread = norm_slab(tokens[at].astype(F32) + mods[2:3] * arm)
+        frame = lax.broadcasted_iota(jnp.int32, (SLAB, 1), 0) % FRAMES
+        dy = jnp.where(frame < place[4], out_grad[at].astype(F32), 0.0)
+        d_mid = dy + back_slab(d_h2 * (1.0 + mods[4:5]), normed, spread)
+        d_middle[at] = d_mid
+        d_branch[at] = (d_mid * mods[2:3]).astype(BF16)
+        fold(fold_a, d_mid * arm)
+        fold(fold_b, d_h2)
+        fold(fold_c, d_h2 * normed)
+
+    slabs(rows, SLAB, back)
+    sums[...] = jnp.zeros_like(sums)
+    sums[0:1] = jnp.sum(fold_a[...], axis=0, keepdims=True)
+    sums[1:2] = jnp.sum(fold_b[...], axis=0, keepdims=True)
+    sums[2:3] = jnp.sum(fold_c[...], axis=0, keepdims=True)
+    turn(d_branch, turned)
+    store_relative(relative, turned, place[1], place[2])
+    value[...] = dot_nn(d_branch[...], rows_of(merge, 0, 16))
+    turn(value, turned)
+    for head in range(HEADS):
+        d_att[head] = turned[head * HEAD : (head + 1) * HEAD].astype(BF16)
+
+
+def attend_back_kernel(place, qkv, d_att, d_qkv, relative, d_q, d_k, d_v):
+    rows = qkv.shape[2]
+    y, c = place[1], place[2]
+    mask = frame_mask(place[4])
+    scale = 1.0 / math.sqrt(HEAD)
+
+    @pl.loop(0, HEADS)
+    def _(head):
+        for group in range(rows // GROUP):
+            at = pl.ds(group * GROUP, GROUP)
+            query, key = qkv[head, :, at], qkv[HEADS + head, :, at]
+            val, grad = qkv[2 * HEADS + head, :, at], d_att[head, :, at]
+            probs = probs_of(key, query, mask)
+            d_probs = dot_nn(val.astype(F32).T.astype(BF16), grad)
+            d_v[head, :, at] = dot_nt(grad, probs.astype(BF16))
+            inner = jnp.sum(probs * d_probs, axis=0, keepdims=True)
+            d_scores = (probs * (d_probs - inner)).astype(BF16)
+            d_q[head, :, at] = dot_nn(key, d_scores) * scale
+            d_k[head, :, at] = dot_nt(query, d_scores) * scale
+
+    for part, ref in enumerate((d_q, d_k, d_v)):
+        for group in range(rows // GROUP):
+            at = pl.ds(group * GROUP, GROUP)
+            d_qkv[at, part * D : (part + 1) * D] = ref[:, :, at].reshape(D, GROUP).T.astype(BF16)
+        for head in range(HEADS):
+            number = part * HEADS + head
+            b, tile = number // 3, number % 3
+            zz, yy, cc = b // 4, (b // 2) % 2, b % 2
+            dy = y if yy == 0 else 1 - y
+            dc = c if cc == 0 else 1 - c
+            relative[dc, dy * 4 + zz, tile] = ref[head].astype(BF16)
+
+
+def input_back_kernel(place, d_qkv, tokens, d_middle, mods, *rest):
+    pieces, rest = rest[:8], rest[8:]
+    input_grad, sums, wide, value, fold_a, fold_b, sems = rest
+    for copy in start_all(list(attend_copies(pieces, place, wide)), sems):
+        copy.wait()
+    rows = tokens.shape[0]
+    for part in range(3):
+        add = dot_nn(d_qkv[:, part * D : (part + 1) * D], rows_of(wide, part * 16, 16))
+        if part == 0:
+            value[...] = add
+        else:
+            value[...] += add
+    for ref in (fold_a, fold_b):
+        ref[...] = jnp.zeros_like(ref)
+
+    def back(at):
+        d_h1 = value[at]
+        normed, spread = norm_slab(tokens[at].astype(F32))
+        d_token = d_middle[at] + back_slab(d_h1 * (1.0 + mods[1:2]), normed, spread)
+        input_grad[at] = d_token.astype(BF16)
+        fold(fold_a, d_h1)
+        fold(fold_b, d_h1 * normed)
+
+    slabs(rows, SLAB, back)
+    sums[...] = jnp.zeros_like(sums)
+    sums[0:1] = jnp.sum(fold_a[...], axis=0, keepdims=True)
+    sums[1:2] = jnp.sum(fold_b[...], axis=0, keepdims=True)
+
+
+def output_kernel(place, act, tokens, branch, out_grad, mods, *rest):
+    pieces, rest = rest[:8], rest[8:]
+    block_out, sums, wide, value, fold_a, sems = rest
+    for copy in start_all(list(down_copies(pieces, place, wide)), sems):
+        copy.wait()
+    rows = tokens.shape[0]
+    value[...] = jnp.zeros_like(value)
+
+    @pl.loop(0, FF // WIDE)
+    def _(i):
+        cols = pl.ds(pl.multiple_of(i * WIDE, WIDE), WIDE)
+        value[...] += dot_nt(act[:, cols], rows_of(wide, 0, 16, cols))
+
+    fold_a[...] = jnp.zeros_like(fold_a)
+
+    def finish(at):
+        mlp = value[at]
+        frame = lax.broadcasted_iota(jnp.int32, (SLAB, 1), 0) % FRAMES
+        keep = frame < place[4]
+        middle = tokens[at].astype(F32) + mods[2:3] * branch[at]
+        block_out[at] = jnp.where(keep, middle + mods[5:6] * mlp, 0.0).astype(BF16)
+        fold(fold_a, jnp.where(keep, out_grad[at].astype(F32), 0.0) * mlp)
+
+    slabs(rows, SLAB, finish)
+    sums[...] = jnp.zeros_like(sums)
+    sums[0:1] = jnp.sum(fold_a[...], axis=0, keepdims=True)
+
+
+def pair_grads(left, right, ordered_after=(), row_block=288):
+    _, rows, depth = left.shape
+    cols = right.shape[1]
+    n_dep = len(ordered_after)
+
+    def kernel(keep_l, send_l, right_ref, *rest):
+        keep, send = rest[n_dep:]
+        send[...] = dot_nn(send_l[0], right_ref[...]).astype(BF16)
+        keep[...] = dot_nn(keep_l[0], right_ref[...]).astype(BF16)
+
+    col_block = WIDE * 5 if cols > D else cols
+    col_block = cols // 4 if cols > D else cols
+    grid = (cols // col_block, rows // row_block)
+    return pl.pallas_call(
+        kernel,
+        grid=grid,
+        out_shape=[jax.ShapeDtypeStruct((rows, cols), BF16)] * 2,
+        in_specs=[
+            pl.BlockSpec((1, row_block, depth), lambda j, i: (0, i, 0)),
+            pl.BlockSpec((1, row_block, depth), lambda j, i: (1, i, 0)),
+            pl.BlockSpec((depth, col_block), lambda j, i: (0, j)),
+        ]
+        + [any_spec()] * n_dep,
+        out_specs=[pl.BlockSpec((row_block, col_block), lambda j, i: (i, j))] * 2,
+        compiler_params=pltpu.CompilerParams(vmem_limit_bytes=40 * 2**20),
+        cost_estimate=pl.CostEstimate(flops=1000, bytes_accessed=1000, transcendentals=0),
+    )(left, left, right, *ordered_after)
+
+
+def up_grads(place, left, right, ordered_after=()):
+    depth, cols = right.shape
+    size = left.shape[0] // 16
+    n_dep = len(ordered_after)
+
+    def kernel(place_ref, keep_l, send_l, right_ref, *rest):
+        keep, send = rest[n_dep:]
+        send[0] = dot_nn(send_l[...], right_ref[...]).astype(BF16)
+        keep[0] = dot_nn(keep_l[...], right_ref[...]).astype(BF16)
+
+    def index(dc):
+        def block(i, place_ref):
+            yy = (place_ref[1] + i // 4) % 2
+            return ((i % 4 * 2 + yy) * 2 + (place_ref[2] + dc) % 2, 0)
+
+        return block
+
+    return pl.pallas_call(
+        kernel,
+        out_shape=[jax.ShapeDtypeStruct((8, size, cols), BF16)] * 2,
+        grid_spec=pltpu.PrefetchScalarGridSpec(
+            num_scalar_prefetch=1,
+            grid=(8,),
+            in_specs=[
+                pl.BlockSpec((size, depth), index(0)),
+                pl.BlockSpec((size, depth), index(1)),
+                pl.BlockSpec((depth, cols), lambda i, place_ref: (0, 0)),
+            ]
+            + [any_spec()] * n_dep,
+            out_specs=[pl.BlockSpec((1, size, cols), lambda i, place_ref: (i, 0, 0))] * 2,
+        ),
+        compiler_params=pltpu.CompilerParams(vmem_limit_bytes=40 * 2**20),
+        cost_estimate=pl.CostEstimate(flops=1000, bytes_accessed=1000, transcendentals=0),
+    )(place, left, left, right, *ordered_after)
+
+
+def flat_mesh(mesh):
+    n_dp, n_cond = mesh.shape["dp"], mesh.shape["cond"]
+    return Mesh(mesh.devices.reshape(n_dp // 4, 2, 2, n_cond), ("z", "y", "c", "x"))
+
+
+def swap(value, axis):
+    return lax.ppermute(value, axis, [(0, 1), (1, 0)])
+
+
+def sum_all(value):
+    for axis in ("c", "x", "y"):
+        value = value + swap(value, axis)
+    for step in (1, 2):
+        value = value + lax.ppermute(value, "z", [(i, i ^ step) for i in range(4)])
+    return value
+
+
+def add_low(*terms):
+    total = terms[0].astype(F32)
+    for term in terms[1:]:
+        total = total + term.astype(F32)
+    return total.astype(BF16)
+
+
+def gather_pieces(early, late, flag_early, flag_late, axis, cut, x):
+    first = x == 0
+    near_late, far_late = jnp.where(first, late[0], late[1]), jnp.where(first, late[1], late[0])
+    flag = jnp.concatenate(
+        [
+            jnp.broadcast_to(flag_early, early.shape),
+            jnp.broadcast_to(jnp.where(first, flag_late[0], flag_late[1]), near_late.shape),
+        ],
+        axis=axis,
+    )
+    got = swap(jnp.concatenate([early, far_late], axis=axis), "x")
+    mine = jnp.where(flag, jnp.concatenate([early, near_late], axis=axis), got)
+    near = lax.all_gather(mine, "z", axis=0, tiled=False)
+    far = swap(near, "y")
+    pieces = [near, swap(cut(near), "x"), far, swap(cut(far), "x")]
+    return pieces + [swap(piece, "c") for piece in pieces]
+
+
+def split_sum(keep, send, cut, x):
+    got = swap(send, "c")
+    first = x == 0
+    (ke, k0, k1), (ge, g0, g1) = cut(keep), cut(got)
+    late_send = add_low(jnp.where(first, k1, k0), jnp.where(first, g1, g0))
+    late_got = swap(late_send, "x")
+    kl, gl = jnp.where(first, k0, k1), jnp.where(first, g0, g1)
+    early = [add_low(ke[i], ge[i]) for i in range(2)]
+    late = [add_low(kl[i], gl[i], late_got[i]) for i in range(2)]
+    return early, late
+
+
+def over_y(halves):
+    return add_low(halves[0], swap(halves[1], "y"))
+
+
+def over_z(value):
+    flat = value.reshape(value.shape[0] * value.shape[1], -1)
+    part = lax.psum_scatter(flat, "z", scatter_dimension=0, tiled=True)
+    return part.reshape(value.shape[1:])
+
+
+def on_grid(inputs, out_grad, frame_counts, timesteps, labels, owners, *matrices):
+    masters, means, squares = matrices[:7], matrices[7:14], matrices[14:]
+    z, y, c, x = (lax.axis_index(axis) for axis in ("z", "y", "c", "x"))
+    block = (z * 2 + y) * 2 + c
+    device = block * 2 + x
+    positions, frames, width = inputs.shape
+    rows = positions * frames
+    span = width // 16
+    clips = timesteps.shape[0]
+    clip_index = device * positions // PATCHES
+    frame_count = lax.dynamic_index_in_dim(frame_counts, clip_index, 0, keepdims=False)
+    place = jnp.stack([z, y, c, x, frame_count, z, z, z]).astype(jnp.int32)
+    own = [owners[number] == x for number in range(7)]
+    own_low = [master[0].T.astype(BF16) for master in masters]
+
+    attend_t, merge_t, up_t, down_t = own_low[3:]
+    tiles = attend_t.reshape(3, span, width)
+    flags = jnp.stack([own[3], own[4]])[:, None, None]
+    firsts = gather_pieces(
+        jnp.stack([tiles[0], merge_t]),
+        (tiles[1:2], tiles[2:3]),
+        flags,
+        (own[3], own[3]),
+        0,
+        lambda main: main[:, 2],
+        x,
+    )
+    ups = gather_pieces(
+        up_t[:UP_E],
+        (up_t[UP_E : UP_E + UP_L], up_t[UP_E + UP_L :]),
+        own[5],
+        (own[5], own[5]),
+        0,
+        lambda main: main[:, UP_E:],
+        x,
+    )
+    downs = gather_pieces(
+        down_t[:, :DOWN_E],
+        (down_t[:, DOWN_E : DOWN_E + DOWN_L], down_t[:, DOWN_E + DOWN_L :]),
+        own[6],
+        (own[6], own[6]),
+        1,
+        lambda main: main[:, :, DOWN_E:],
+        x,
+    )
+
+    features = timestep_features(timesteps).astype(BF16)
+    one_hot = (labels[:, None] == jnp.arange(LABELS)[None, :]).astype(BF16)
+    time_part = jnp.where(own[0], contract_cols(features, own_low[0]), 0.0)
+    table_part = jnp.where(own[1], contract_cols(one_hot, own_low[1]), 0.0)
+    parts = lax.dynamic_update_slice_in_dim(
+        jnp.zeros((2, clips, width), F32), jnp.stack([time_part, table_part]), block * span, 2
+    )
+    parts = sum_all(parts)
+    time_pre = parts[0]
+    cond_vec = parts[1] + jax.nn.silu(time_pre)
+    cond_act, silu_back = jax.vjp(jax.nn.silu, cond_vec)
+    cond_act = cond_act.astype(BF16)
+    mod_part = jnp.where(own[2], contract_cols(cond_act, own_low[2]), 0.0)
+    mod_span = mod_part.shape[1]
+    modulation = sum_all(
+        lax.dynamic_update_slice_in_dim(
+            jnp.zeros((clips, 6 * width), F32), mod_part, block * mod_span, 1
+        )
+    )
+    mod_row = lax.dynamic_index_in_dim(modulation, clip_index, 0, keepdims=False)
+    mods = jnp.concatenate([mod_row.reshape(6, width), jnp.zeros((2, width), F32)])
+
+    tokens = inputs.reshape(rows, width)
+    grad_out = out_grad.reshape(rows, width)
+    spot = (place, smem_spec())
+    whole = vmem_spec()
+    in_vmem = lambda *arrays: [(array, whole) for array in arrays]
+    in_place = lambda arrays: [(array, any_spec()) for array in arrays]
+    sems = lambda count: pltpu.SemaphoreType.DMA((count,))
+    d_mlp, d_mlp_rel = run_kernel(
+        start_back_kernel,
+        [spot] + in_vmem(grad_out, mods),
+        [((rows, width), BF16), ((2, 8, span, rows), BF16)],
+        [vmem(width, rows, dtype=F32)],
+    )
+    h1, qkv, attended, branch, h2 = run_kernel(
+        first_half_kernel,
+        [spot] + in_vmem(tokens, mods) + in_place(firsts),
+        [
+            ((rows, width), BF16),
+            ((48, span, rows), BF16),
+            ((rows, width), BF16),
+            ((rows, width), F32),
+            ((rows, width), BF16),
+        ],
+        [
+            vmem(48, span, width),
+            vmem(16, span, width),
+            vmem(16, span, rows, dtype=F32),
+            sems(64),
+        ],
+    )
+    act, slope = run_kernel(
+        up_kernel,
+        [spot] + in_vmem(h2) + in_place(ups),
+        [((rows, FF), BF16)] * 2,
+        [vmem(FF, width), vmem(rows, WIDE, dtype=F32), sems(48)],
+    )
+    down_keep, down_send = pair_grads(d_mlp_rel.reshape(2, 8 * span, rows), act)
+    cut_down = lambda v: (
+        v[..., :DOWN_E],
+        v[..., DOWN_E : DOWN_E + DOWN_L],
+        v[..., DOWN_E + DOWN_L :],
+    )
+    shape = (2, 4, span, FF)
+    early, late = split_sum(down_keep.reshape(shape), down_send.reshape(shape), cut_down, x)
+    down_part = over_z(jnp.concatenate([over_y(early), over_y(late)], axis=-1))
+    down_got = swap(down_part, "x")
+
+    d_upper, d_upper_t = run_kernel(
+        d_upper_kernel,
+        [spot] + in_vmem(d_mlp, slope) + in_place(downs),
+        [((rows, FF), BF16), ((FF, rows), BF16)],
+        [vmem(16, span, FF), vmem(rows, WIDE, dtype=F32), sems(48)],
+    )
+    up_keep, up_send = up_grads(place, d_upper_t, h2)
+    cut_up = lambda v: (v[:, :, :UP_E], v[:, :, UP_E : UP_E + UP_L], v[:, :, UP_E + UP_L :])
+    shape = (2, 4, 4 * span, width)
+    early, late = split_sum(up_keep.reshape(shape), up_send.reshape(shape), cut_up, x)
+    up_total = jnp.concatenate([over_y(early), over_y(late)], axis=1)
+    up_total, _ = lax.optimization_barrier((up_total, down_part))
+    up_part = over_z(up_total)
+    up_got = swap(up_part, "x")
+
+    d_middle, d_branch, d_branch_rel, d_att, sums_two = run_kernel(
+        middle_back_kernel,
+        [spot] + in_vmem(d_upper, tokens, grad_out, branch, mods) + in_place(ups + firsts),
+        [
+            ((rows, width), F32),
+            ((rows, width), BF16),
+            ((2, 8, span, rows), BF16),
+            ((16, span, rows), BF16),
+            ((8, width), F32),
+        ],
+        [
+            vmem(FF, width),
+            vmem(16, span, width),
+            vmem(rows, width, dtype=F32),
+            vmem(width, rows, dtype=F32),
+        ]
+        + [vmem(8, width, dtype=F32)] * 3
+        + [sems(64)],
+    )
+    merge_keep, merge_send = pair_grads(d_branch_rel.reshape(2, 8 * span, rows), attended)
+    shape = (2, 4, span, width)
+    merge_keep = merge_keep.reshape(shape)
+    merge_got = swap(merge_send.reshape(shape), "c")
+    merge_total = over_y([add_low(merge_keep[i], merge_got[i]) for i in range(2)])
+
+    d_qkv, d_qkv_rel = run_kernel(
+        attend_back_kernel,
+        [spot] + in_vmem(qkv, d_att),
+        [((rows, 3 * width), BF16), ((2, 8, 3, span, rows), BF16)],
+        [vmem(16, span, rows, dtype=F32)] * 3,
+    )
+    attend_keep, attend_send = pair_grads(d_qkv_rel.reshape(2, 24 * span, rows), h1)
+    cut_attend = lambda v: (v[:, :, 0], v[:, :, 1], v[:, :, 2])
+    shape = (2, 4, 3, span, width)
+    early, late = split_sum(attend_keep.reshape(shape), attend_send.reshape(shape), cut_attend, x)
+    first_total = jnp.concatenate([over_y(early), merge_total, over_y(late)], axis=2)
+    first_total, _ = lax.optimization_barrier((first_total, up_part))
+    first_part = over_z(first_total).reshape(span, 3, width).transpose(1, 0, 2)
+    first_got = swap(first_part, "x")
+
+    input_grad, sums_one = run_kernel(
+        input_back_kernel,
+        [spot] + in_vmem(d_qkv, tokens, d_middle, mods) + in_place(firsts),
+        [((rows, width), BF16), ((8, width), F32)],
+        [vmem(48, span, width), vmem(rows, width, dtype=F32)]
+        + [vmem(8, width, dtype=F32)] * 2
+        + [sems(48)],
+    )
+    block_out, sums_out = run_kernel(
+        output_kernel,
+        [spot] + in_vmem(act, tokens, branch, grad_out, mods) + in_place(downs),
+        [((rows, width), BF16), ((8, width), F32)],
+        [
+            vmem(16, span, FF),
+            vmem(rows, width, dtype=F32),
+            vmem(8, width, dtype=F32),
+            sems(48),
+        ],
+    )
+
+    d_vector = jnp.concatenate([sums_one[:2], sums_two[:3], sums_out[:1]]).reshape(6 * width)
+    clip_pick = (jnp.arange(clips) == clip_index).astype(F32)
+    d_mod = sum_all(clip_pick[:, None] * d_vector[None, :])
+    d_mod = lax.dynamic_slice_in_dim(d_mod, block * mod_span, mod_span, 1)
+    grad_mod = contract_rows(d_mod, cond_act.astype(F32), HIGHEST)
+    d_cond_part = jnp.dot(
+        d_mod, own_low[2].astype(F32), precision=HIGHEST, preferred_element_type=F32
+    )
+    d_cond_act = sum_all(jnp.where(own[2], d_cond_part, 0.0))
+    d_cond = silu_back(d_cond_act)[0]
+    d_time_pre = jax.vjp(jax.nn.silu, time_pre)[1](d_cond)[0]
+    d_cond_block = lax.dynamic_slice_in_dim(d_cond, block * span, span, 1)
+    d_time_block = lax.dynamic_slice_in_dim(d_time_pre, block * span, span, 1)
+    grad_table = contract_rows(d_cond_block, one_hot.astype(F32), HIGHEST)
+    grad_time = contract_rows(d_time_block, features.astype(F32), HIGHEST)
+
+    def joined(early, part, got, axis):
+        first = x == 0
+        halves = [jnp.where(first, part, got), jnp.where(first, got, part)]
+        return jnp.concatenate([early.astype(BF16)] + halves, axis=axis).astype(F32)
+
+    def both(part, got):
+        return part.astype(F32) + got.astype(F32)
+
+    grads = (
+        grad_time,
+        grad_table,
+        grad_mod,
+        jnp.concatenate(
+            [
+                both(first_part[0], first_got[0]),
+                jnp.where(x == 0, first_part[2], first_got[2]).astype(F32),
+                jnp.where(x == 0, first_got[2], first_part[2]).astype(F32),
+            ]
+        ),
+        both(first_part[1], first_got[1]),
+        jnp.concatenate(
+            [
+                both(up_part[:UP_E], up_got[:UP_E]),
+                jnp.where(x == 0, up_part[UP_E:], up_got[UP_E:]).astype(F32),
+                jnp.where(x == 0, up_got[UP_E:], up_part[UP_E:]).astype(F32),
+            ]
+        ),
+        jnp.concatenate(
+            [
+                both(down_part[:, :DOWN_E], down_got[:, :DOWN_E]),
+                jnp.where(x == 0, down_part[:, DOWN_E:], down_got[:, DOWN_E:]).astype(F32),
+                jnp.where(x == 0, down_got[:, DOWN_E:], down_part[:, DOWN_E:]).astype(F32),
+            ],
+            axis=1,
+        ),
+    )
+    rates = [
+        0.5 * FREQ ** (-0.5),
+        0.5,
+        0.5 * D ** (-0.5),
+        0.5 * D ** (-0.5),
+        D ** (-0.5),
+        0.5 * D ** (-0.5),
+        0.5 * FF ** (-0.5),
+    ]
+    new_list, first_list, second_list, copy_list = ([], [], [], [])
+    for number in range(7):
+        fresh, mean, square = adamw_step(
+            masters[number][0].T,
+            means[number][0].T,
+            squares[number][0].T,
+            grads[number],
+            rates[number],
+        )
+        fresh = jnp.where(own[number], fresh, 0.0).T[None]
+        new_list.append(fresh)
+        first_list.append(jnp.where(own[number], mean, 0.0).T[None])
+        second_list.append(jnp.where(own[number], square, 0.0).T[None])
+        copy_list.append(fresh.astype(BF16))
+    return (
+        block_out.reshape(inputs.shape),
+        input_grad.reshape(inputs.shape),
+        *new_list,
+        *first_list,
+        *second_list,
+        *copy_list,
+    )
 
 
 def on_device(
@@ -343,69 +1147,23 @@
 
 
 def solution(mesh):
+    n_dp, n_cond = mesh.shape["dp"], mesh.shape["cond"]
+    if (n_dp, n_cond) == (16, 2):
+        token_spec = P(("z", "y", "c", "x"), None, None)
+        matrix_spec = P("x", None, ("z", "y", "c"))
+        return jax.shard_map(
+            on_grid,
+            mesh=flat_mesh(mesh),
+            in_specs=(token_spec,) * 2 + (P(),) * 4 + (matrix_spec,) * 21,
+            out_specs=(token_spec,) * 2 + (matrix_spec,) * 28,
+            check_vma=False,
+        )
+    token_spec = P(("dp", "cond"), None, None)
+    matrix_spec = P("cond", None, "dp")
     return jax.shard_map(
         on_device,
         mesh=mesh,
-        in_specs=(
-            P(("dp", "cond"), None, None),
-            P(("dp", "cond"), None, None),
-            P(),
-            P(),
-            P(),
-            P(),
-            P("cond", None, "dp"),
-            P("cond", None, "dp"),
-            P("cond", None, "dp"),
-            P("cond", None, "dp"),
-            P("cond", None, "dp"),
-            P("cond", None, "dp"),
-            P("cond", None, "dp"),
-            P("cond", None, "dp"),
-            P("cond", None, "dp"),
-            P("cond", None, "dp"),
-            P("cond", None, "dp"),
-            P("cond", None, "dp"),
-            P("cond", None, "dp"),
-            P("cond", None, "dp"),
-            P("cond", None, "dp"),
-            P("cond", None, "dp"),
-            P("cond", None, "dp"),
-            P("cond", None, "dp"),
-            P("cond", None, "dp"),
-            P("cond", None, "dp"),
-            P("cond", None, "dp"),
-        ),
-        out_specs=(
-            P(("dp", "cond"), None, None),
-            P(("dp", "cond"), None, None),
-            P("cond", None, "dp"),
-            P("cond", None, "dp"),
-            P("cond", None, "dp"),
-            P("cond", None, "dp"),
-            P("cond", None, "dp"),
-            P("cond", None, "dp"),
-            P("cond", None, "dp"),
-            P("cond", None, "dp"),
-            P("cond", None, "dp"),
-            P("cond", None, "dp"),
-            P("cond", None, "dp"),
-            P("cond", None, "dp"),
-            P("cond", None, "dp"),
-            P("cond", None, "dp"),
-            P("cond", None, "dp"),
-            P("cond", None, "dp"),
-            P("cond", None, "dp"),
-            P("cond", None, "dp"),
-            P("cond", None, "dp"),
-            P("cond", None, "dp"),
-            P("cond", None, "dp"),
-            P("cond", None, "dp"),
-            P("cond", None, "dp"),
-            P("cond", None, "dp"),
-            P("cond", None, "dp"),
-            P("cond", None, "dp"),
-            P("cond", None, "dp"),
-            P("cond", None, "dp"),
-        ),
+        in_specs=(token_spec,) * 2 + (P(),) * 4 + (matrix_spec,) * 21,
+        out_specs=(token_spec,) * 2 + (matrix_spec,) * 28,
         check_vma=False,
     )

time: 1450 us -> 772 us (0.53)
  waiting for transfers between devices: 877 us -> 359 us
  blocking collectives: 240 us -> 0 us
  Pallas kernels: 0 us -> 221 us
  matrix products: 152 us -> 9.48 us
  starting transfers between devices: 0.71 us -> 61.5 us
  local copies, waits for them, and re-layouts: 87.7 us -> 32.3 us
    reduce_scatter x3 -> x2, waiting for transfers between devices: 355 us -> 7.12 us  [over_z(): part = lax.psum_scatter(flat, 'z', scatter_dimension=0, tiled=True)]
    unnamed x24 -> x7, waiting for transfers between devices: 364 us -> 28.2 us
    ppermute x0 -> x61, waiting for transfers between devices: none -> 286 us  [the longest x53 276 us: swap(): return lax.ppermute(value, axis, [(0, 1), (1, 0)])]
    pallas_call x0 -> x12, Pallas kernels: none -> 221 us  [the longest x8 196 us: run_kernel(): pl.pallas_call(kernel, out_shape=[jax.ShapeDtypeStruct(shape, dtype) for...]
    all_gather x12 -> x0, blocking collectives: 200 us -> none  [the longest x1 66.9 us: on_device(): modulation = lax.all_gather(mod_part, ('dp', 'cond'), axis=1, tiled=True)]
    all_gather x7 -> x3, waiting for transfers between devices: 158 us -> 37.6 us  [gather_pieces(): near = lax.all_gather(mine, 'z', axis=0, tiled=False)]
    ppermute x0 -> x61, starting transfers between devices: none -> 61 us  [the longest x53 48.4 us: swap(): return lax.ppermute(value, axis, [(0, 1), (1, 0)])]
    dot_general x13 -> x1, matrix products: 58.7 us -> 1.07 us  [on_grid(): jnp.dot(d_mod, own_low[2].astype(F32), precision=HIGHEST, preferred_eleme...]
  transfers between devices with their start and end apart: 17 -> 67, of which waited for: 11 -> 38; matrix products, arithmetic and copies ran while one was open for 12% -> 10% of each run, Pallas kernels for 0% -> 12%
where the time goes in v1:
time: 772 us; the launch traced here: 762 us
  waiting for transfers between devices  359 us (47%)
  Pallas kernels  221 us (29%)
  starting transfers between devices  61.5 us (8%)
  other arithmetic  58.5 us (8%)
  local copies, waits for them, and re-layouts  32.3 us (4%)
  between operations  20.4 us (3%)
  matrix products  9.48 us (1%)
    ppermute x53, waiting for transfers between devices, swap(): return lax.ppermute(value, axis, [(0, 1), (1, 0)])  276 us
    pallas_call x8, Pallas kernels, run_kernel(): pl.pallas_call(kernel, out_shape=[jax.ShapeDtypeStruct(shape, dtype) for...  196 us
    ppermute x53, starting transfers between devices, swap(): return lax.ppermute(value, axis, [(0, 1), (1, 0)])  48.4 us
    all_gather x3, waiting for transfers between devices, gather_pieces(): near = lax.all_gather(mine, 'z', axis=0, tiled=False)  37.6 us
    unnamed x7, waiting for transfers between devices  28.2 us
    convert_element_type x17, other arithmetic, add_low(): return total.astype(BF16)  26.5 us
    pallas_call x3, Pallas kernels, pair_grads(): pl.pallas_call(kernel, grid=grid, out_shape=[jax.ShapeDtypeStruct((rows,...  16.9 us
  transfers between devices with their start and end apart: 67, of which 38 were waited for; matrix products, arithmetic and copies ran while one was open for 10% of the time, Pallas kernels for 12%

profile of v1, /device:TPU:0, one launch (start us, length us, event | category | flops | bytes accessed | tf_op | source)
XLA Modules:
  0.0 762.0 jit_solution(6894460426978679657)
XLA Ops:
  8.8 3.0 collective-permute-start.18
  13.1 9.7 %collective-permute-done.18 = bf16[208,1152]{1,0:T(8,128)(2,1)S(1)} collective-permute-done((bf16[208,1152]{1,0:T(8,128)(2,1)S(1)}, bf16[208,1152]{1,0:T(8,128)(2,1)S(1)}, u32[]{:S(2)}, u32[]{:S(2)}) %collective-permute-start.18) | collective-permute-done | bytes 479264 | tf_op jit(solution)/shard_map/ppermute | solution.py:543
  26.5 9.7 %collective-permute-done.26 = bf16[72,3328]{1,0:T(8,128)(2,1)S(1)} collective-permute-done((bf16[72,3328]{1,0:T(8,128)(2,1)S(1)}, bf16[72,3328]{1,0:T(8,128)(2,1)S(1)}, u32[]{:S(2)}, u32[]{:S(2)}) %collective-permute-start.26) | collective-permute-done | bytes 479264 | tf_op jit(solution)/shard_map/ppermute | solution.py:543
  40.4 8.8 %collective-permute-done.10 = bf16[3,72,1152]{2,1,0:T(8,128)(2,1)S(1)} collective-permute-done((bf16[3,72,1152]{2,1,0:T(8,128)(2,1)S(1)}, bf16[3,72,1152]{2,1,0:T(8,128)(2,1)S(1)}, u32[]{:S(2)}, u32[]{:S(2)}) %collective-permute-start.10) | collective-permute-done | bytes 497696 | tf_op jit(solution)/shard_map/ppermute | solution.py:543
  63.5 3.7 collective-permute-done.3
  75.1 37.6 %all-gather.11.cloned.1.call-done = bf16[288,3328]{1,0:T(8,128)(2,1)} async-done(((bf16[72,3328]{1,0:T(8,128)(2,1)}), bf16[288,3328]{1,0:T(8,128)(2,1)}) %all-gather.11.cloned.1.call-update) | async-done | bytes 1916944 | tf_op jit(solution)/shard_map/all_gather | solution.py:573
  116.1 3.3 collective-permute-done.6
  122.9 38.2 %collective-permute-done.7 = f32[4,6912]{1,0:T(4,128)S(1)} collective-permute-done((f32[4,6912]{1,0:T(4,128)S(1)}, f32[4,6912]{1,0:T(4,128)S(1)}, u32[]{:S(2)}, u32[]{:S(2)}) %collective-permute-start.7) | collective-permute-done | bytes 110624 | tf_op jit(solution)/shard_map/ppermute | solution.py:543
  169.7 3.2 collective-permute-done.9
  176.1 7.6 %collective-permute-done.27.refs_7_.refs_4_ = bf16[4,72,1280]{2,1,0:T(8,128)(2,1)S(1)} collective-permute-done((bf16[4,72,1280]{2,1,0:T(8,128)(2,1)}, bf16[4,72,1280]{2,1,0:T(8,128)(2,1)S(1)}, u32[]{:S(2)}, u32[]{:S(2)}) %collective-permute-start.27) | collective-permute-done | bytes 737312 | tf_op jit(solution)/shard_map/ppermute | solution.py:543
  183.7 12.5 %collective-permute-done.11.refs_4_.refs_15_.refs_6_ = bf16[4,72,1152]{2,1,0:T(8,128)(2,1)S(1)} collective-permute-done((bf16[4,72,1152]{2,1,0:T(8,128)(2,1)S(1)}, bf16[4,72,1152]{2,1,0:T(8,128)(2,1)S(1)}, u32[]{:S(2)}, u32[]{:S(2)}) %collective-permute-start.11) | collective-permute-done | bytes 663584 | tf_op jit(solution)/shard_map/ppermute | solution.py:543
  199.2 3.1 collective-permute-done.15.refs_8_.refs_19_.refs_10_
  204.3 11.3 %collective-permute-done.12 = bf16[4,3,72,1152]{3,2,0,1:T(8,128)(2,1)S(1)} collective-permute-done((bf16[4,3,72,1152]{3,2,0,1:T(8,128)(2,1)S(1)}, bf16[4,3,72,1152]{3,2,0,1:T(8,128)(2,1)S(1)}, u32[]{:S(2)}, u32[]{:S(2)}) %collective-permute-start.12) | collective-permute-done | bytes 1990688 | tf_op jit(solution)/shard_map/ppermute | solution.py:543
  217.2 4.4 collective-permute-done.21.refs_5_.refs_9_
  223.4 14.1 %collective-permute-done.29.refs_9_.refs_6_ = bf16[4,72,1280]{2,1,0:T(8,128)(2,1)} collective-permute-done((bf16[4,72,1280]{2,1,0:T(8,128)(2,1)S(1)}, bf16[4,72,1280]{2,1,0:T(8,128)(2,1)}, u32[]{:S(2)}, u32[]{:S(2)}) %collective-permute-start.29) | collective-permute-done | bytes 737312 | tf_op jit(solution)/shard_map/ppermute | solution.py:543
  237.5 13.3 %collective-permute-done.13.refs_6_.refs_17_.refs_8_ = bf16[4,72,1152]{2,1,0:T(8,128)(2,1)S(1)} collective-permute-done((bf16[4,72,1152]{2,1,0:T(8,128)(2,1)S(1)}, bf16[4,72,1152]{2,1,0:T(8,128)(2,1)S(1)}, u32[]{:S(2)}, u32[]{:S(2)}) %collective-permute-start.13) | collective-permute-done | bytes 663584 | tf_op jit(solution)/shard_map/ppermute | solution.py:543
  251.4 4.0 collective-permute-done.17.refs_10_.refs_21_.refs_12_
  260.5 3.7 shard_map.493
  264.2 3.1 copy.90.refs_5_.refs_16_.refs_7_
  268.8 34.5 %shard_map.490 = (bf16[512,1152]{1,0:T(8,128)(2,1)}, bf16[48,72,512]{2,1,0:T(8,128)(2,1)}, bf16[512,1152]{1,0:T(8,128)(2,1)}, f32[512,1152]{1,0:T(8,128)}, bf16[512,1152]{1,0:T(8,128)(2,1)}) custom-call(s32[8]{0:T(128)} %stack.45.refs_0_.place_ref, bf16[512,1152]{1,0:T(8,128)(2,1)} %bitcast.552, f32[8,1152]{1,0:T(8,128)} %concatenate.64.refs_2_.refs_5_.refs_4_, ...), custom_call_target="tpu_custom_call" | custom-call | flops 1000 | bytes 1000 | tf_op jit(solution)/shard_map/pallas_call | solution.py:113
  304.6 27.3 %shard_map.491 = (bf16[512,4608]{1,0:T(8,128)(2,1)}, bf16[512,4608]{1,0:T(8,128)(2,1)}) custom-call(s32[8]{0:T(128)} %stack.45.refs_0_.place_ref, bf16[512,1152]{1,0:T(8,128)(2,1)} %get-tuple-element.61.refs_1_.right_ref, bf16[4,208,1152]{2,1,0:T(8,128)(2,1)} %bitcast.558, bf16[4,80,1152]{2,1,0:T(8,128)(2,1)} %copy-done.30, ...), custom_call_target="tpu_custom_call" | custom-call | flops 1000 | bytes 1000 | tf_op jit(solution)/shard_map/pallas_call | solution.py:113
  331.9 20.7 %shard_map.492 = (bf16[512,1152]{1,0:T(8,128)(2,1)}, f32[8,1152]{1,0:T(8,128)}) custom-call(s32[8]{0:T(128)} %stack.45.refs_0_.place_ref, bf16[512,4608]{1,0:T(8,128)(2,1)} %get-tuple-element.62.refs_1_.right_ref, bf16[512,1152]{1,0:T(8,128)(2,1)} %bitcast.553, f32[512,1152]{1,0:T(8,128)} %get-tuple-element.63.refs_3_.refs_4_, bf16[512,1152]{1,0:T(8,128)(2,1)} %bitcast.562, ...), custom_call_target="tpu_custom_call" | custom-call | flops 1000 | bytes 1000 | tf_op jit(solution)/shard_map/pallas_call | solution.py:113
  353.4 28.2 %shard_map.494 = (bf16[512,4608]{1,0:T(8,128)(2,1)}, bf16[4608,512]{1,0:T(8,128)(2,1)}) custom-call(s32[8]{0:T(128)} %stack.45.refs_0_.place_ref, bf16[512,1152]{1,0:T(8,128)(2,1)} %get-tuple-element.66.refs_1_, bf16[512,4608]{1,0:T(8,128)(2,1)} %get-tuple-element.67.refs_2_, bf16[4,72,3328]{2,1,0:T(8,128)(2,1)} %bitcast.38.refs_6_.refs_3_, ...), custom_call_target="tpu_custom_call" | custom-call | flops 1000 | bytes 1000 | tf_op jit(solution)/shard_map/pallas_call | solution.py:113
  381.6 33.0 %shard_map.495 = (f32[512,1152]{1,0:T(8,128)}, bf16[512,1152]{1,0:T(8,128)(2,1)}, bf16[2,8,72,512]{3,2,1,0:T(8,128)(2,1)}, bf16[16,72,512]{2,1,0:T(8,128)(2,1)}, f32[8,1152]{1,0:T(8,128)}) custom-call(s32[8]{0:T(128)} %stack.45.refs_0_.place_ref, bf16[512,4608]{1,0:T(8,128)(2,1)} %get-tuple-element.68.refs_1_, bf16[512,1152]{1,0:T(8,128)(2,1)} %bitcast.554, ...), custom_call_target="tpu_custom_call" | custom-call | flops 1000 | bytes 1000 | tf_op jit(solution)/shard_map/pallas_call | solution.py:113
  415.4 26.1 %shard_map.496 = (bf16[512,3456]{1,0:T(8,128)(2,1)}, bf16[2,8,3,72,512]{4,3,2,1,0:T(8,128)(2,1)}) custom-call(s32[8]{0:T(128)} %stack.45.refs_0_.place_ref, bf16[48,72,512]{2,1,0:T(8,128)(2,1)} %get-tuple-element.65.refs_1_, bf16[16,72,512]{2,1,0:T(8,128)(2,1)} %get-tuple-element.69.refs_2_), custom_call_target="tpu_custom_call" | custom-call | flops 1000 | bytes 1000 | tf_op jit(solution)/shard_map/pallas_call | solution.py:113
  441.5 22.1 %shard_map.497 = (bf16[512,1152]{1,0:T(8,128)(2,1)}, f32[8,1152]{1,0:T(8,128)}) custom-call(s32[8]{0:T(128)} %stack.45.refs_0_.place_ref, bf16[512,3456]{1,0:T(8,128)(2,1)} %get-tuple-element.70.refs_1_, bf16[512,1152]{1,0:T(8,128)(2,1)} %bitcast.555, f32[512,1152]{1,0:T(8,128)} %get-tuple-element.71.refs_3_, f32[8,1152]{1,0:T(8,128)} %concatenate.64.refs_2_.refs_5_.refs_4_, ...), custom_call_target="tpu_custom_call" | custom-call | flops 1000 | bytes 1000 | tf_op jit(solution)/shard_map/pallas_call | solution.py:113
  469.8 9.1 %shard_map.501 = (bf16[576,4608]{1,0:T(8,128)(2,1)S(1)}, bf16[576,4608]{1,0:T(8,128)(2,1)}) custom-call(bf16[2,576,512]{2,1,0:T(8,128)(2,1)S(1)} %bitcast.542, bf16[2,576,512]{2,1,0:T(8,128)(2,1)S(1)} %bitcast.543, bf16[512,4608]{1,0:T(8,128)(2,1)S(1)} %copy-done), custom_call_target="tpu_custom_call" | custom-call | flops 1000 | bytes 1000 | tf_op jit(solution)/shard_map/pallas_call | solution.py:485
  480.6 4.0 collective-permute-done.36
  486.2 5.6 shard_map.498
  498.0 8.7 %shard_map.500 = (bf16[8,288,1152]{2,1,0:T(8,128)(2,1)S(1)}, bf16[8,288,1152]{2,1,0:T(8,128)(2,1)}) custom-call(s32[8]{0:T(128)S(1)} %copy-done.10, bf16[4608,512]{1,0:T(8,128)(2,1)S(1)} %bitcast.525, bf16[4608,512]{1,0:T(8,128)(2,1)S(1)} %bitcast.525, bf16[512,1152]{1,0:T(8,128)(2,1)S(1)} %copy-done.5), custom_call_target="tpu_custom_call" | custom-call | flops 1000 | bytes 1000 | tf_op jit(solution)/shard_map/pallas_call | solution.py:518
  511.6 3.9 collective-permute-done.39
  516.3 3.0 collective-permute-done.40
  524.0 5.7 convert_bitcast_fusion
  541.1 24.6 %collective-permute-done.56 = bf16[2,4,72,1280]{3,2,1,0:T(8,128)(2,1)S(1)} collective-permute-done((bf16[2,4,72,1280]{3,2,1,0:T(8,128)(2,1)S(1)}, bf16[2,4,72,1280]{3,2,1,0:T(8,128)(2,1)S(1)}, u32[]{:S(2)}, u32[]{:S(2)}) %collective-permute-start.56) | collective-permute-done | bytes 1474592 | tf_op jit(solution)/shard_map/ppermute | solution.py:543
  570.2 24.4 %collective-permute-done.55 = bf16[4,72,2048]{2,1,0:T(8,128)(2,1)S(1)} collective-permute-done((bf16[4,72,2048]{2,1,0:T(8,128)(2,1)S(1)}, bf16[4,72,2048]{2,1,0:T(8,128)(2,1)S(1)}, u32[]{:S(2)}, u32[]{:S(2)}) %collective-permute-start.55) | collective-permute-done | bytes 1179680 | tf_op jit(solution)/shard_map/ppermute | solution.py:543
  596.9 8.8 %collective-permute-done.57 = bf16[4,72,1280]{2,1,0:T(8,128)(2,1)S(1)} collective-permute-done((bf16[4,72,1280]{2,1,0:T(8,128)(2,1)S(1)}, bf16[4,72,1280]{2,1,0:T(8,128)(2,1)S(1)}, u32[]{:S(2)}, u32[]{:S(2)}) %collective-permute-start.57) | collective-permute-done | bytes 737312 | tf_op jit(solution)/shard_map/ppermute | solution.py:543
  613.5 7.5 collective-permute-done.52
  624.5 3.4 fusion.16
  628.7 9.8 %collective-permute-done.51 = bf16[4,128,1152]{2,1,0:T(8,128)(2,1)S(1)} collective-permute-done((bf16[4,128,1152]{2,1,0:T(8,128)(2,1)S(1)}, bf16[4,128,1152]{2,1,0:T(8,128)(2,1)S(1)}, u32[]{:S(2)}, u32[]{:S(2)}) %collective-permute-start.51) | collective-permute-done | bytes 1179680 | tf_op jit(solution)/shard_map/ppermute | solution.py:543
  640.6 8.2 %collective-permute-done.53 = bf16[4,80,1152]{2,1,0:T(8,128)(2,1)S(1)} collective-permute-done((bf16[4,80,1152]{2,1,0:T(8,128)(2,1)S(1)}, bf16[4,80,1152]{2,1,0:T(8,128)(2,1)S(1)}, u32[]{:S(2)}, u32[]{:S(2)}) %collective-permute-start.53) | collective-permute-done | bytes 737312 | tf_op jit(solution)/shard_map/ppermute | solution.py:543
  659.5 11.9 %collective-permute-done.45 = bf16[4,72,1152]{2,1,0:T(8,128)(2,1)S(1)} collective-permute-done((bf16[4,72,1152]{2,1,0:T(8,128)(2,1)S(1)}, bf16[4,72,1152]{2,1,0:T(8,128)(2,1)S(1)}, u32[]{:S(2)}, u32[]{:S(2)}) %collective-permute-start.45) | collective-permute-done | bytes 663584 | tf_op jit(solution)/shard_map/ppermute | solution.py:543
  673.0 6.5 collective-permute-done.49
  684.0 7.1 reduce-scatter.8.cloned.1.call-done
  695.0 3.6 fusion.48
  698.6 7.5 collective-permute-done.59
  706.2 28.1 %reduce-scatter.10.cloned.1.call-done = bf16[72,3456]{1,0:T(8,128)(2,1)} async-done(((bf16[288,3456]{1,0:T(8,128)(2,1)}), bf16[72,3456]{1,0:T(8,128)(2,1)}) %reduce-scatter.10.cloned.1.call-update) | async-done | bytes 497680
  737.5 5.3 fusion.47
  742.8 6.2 collective-permute-done.58
  (355 shorter events, 152.2 us)
Async XLA Ops:
  7.2 65.8 %all-gather.9.cloned.1.call-start = ((), (), s32[]{:S(2)}) async-start(), calls=%async_computation.6 | async-start | bytes 2396160 | tf_op jit(solution)/shard_map/all_gather | solution.py:573
  8.8 14.0 %collective-permute-start.18 = (bf16[208,1152]{1,0:T(8,128)(2,1)S(1)}, bf16[208,1152]{1,0:T(8,128)(2,1)S(1)}, u32[]{:S(2)}, u32[]{:S(2)}) collective-permute-start(bf16[208,1152]{1,0:T(8,128)(2,1)S(1)} %pad_maximum_fusion.6), channel_id=1, source_target_pairs={{0,1},{1,0},{2,3},{3,2},{4,5},{5,4},{6,7},{7,6},{8,9},{9,8},{10,11... | collective-permute-start | bytes 1437704 | tf_op jit(solution)/shard_map/ppermute | solution.py:543
  23.8 89.0 %all-gather.11.cloned.1.call-start = ((), (), s32[]{:S(2)}) async-start(), calls=%async_computation.7 | async-start | bytes 2396160 | tf_op jit(solution)/shard_map/all_gather | solution.py:573
  24.0 12.2 %collective-permute-start.26 = (bf16[72,3328]{1,0:T(8,128)(2,1)S(1)}, bf16[72,3328]{1,0:T(8,128)(2,1)S(1)}, u32[]{:S(2)}, u32[]{:S(2)}) collective-permute-start(bf16[72,3328]{1,0:T(8,128)(2,1)S(1)} %pad_maximum_fusion.8), channel_id=1, source_target_pairs={{0,1},{1,0},{2,3},{3,2},{4,5},{5,4},{6,7},{7,6},{8,9},{9,8},{10,11... | collective-permute-start | bytes 1437704 | tf_op jit(solution)/shard_map/ppermute | solution.py:543
  37.2 130.6 %all-gather.7.cloned.1.call-start = ((), (), s32[]{:S(2)}) async-start(), calls=%async_computation.5 | async-start | bytes 2488320 | tf_op jit(solution)/shard_map/all_gather | solution.py:573
  37.5 11.7 %collective-permute-start.10 = (bf16[3,72,1152]{2,1,0:T(8,128)(2,1)S(1)}, bf16[3,72,1152]{2,1,0:T(8,128)(2,1)S(1)}, u32[]{:S(2)}, u32[]{:S(2)}) collective-permute-start(bf16[3,72,1152]{2,1,0:T(8,128)(2,1)S(1)} %pad_maximum_fusion.11), channel_id=1, source_target_pairs={{0,1},{1,0},{2,3},{3,2},{4,5},{5,4},{6,7},{7,6},{8,9},{9,8},{10,11... | collective-permute-start | bytes 1493000 | tf_op jit(solution)/shard_map/ppermute | solution.py:543
  50.1 601.6 %reduce-scatter.6.cloned.1.call-start = ((), (), s32[]{:S(2)}) async-start(), calls=%async_computation.3 | async-start | bytes 2396160 | tf_op jit(solution)/shard_map/reduce_scatter | solution.py:597
  72.9 41.3 %collective-permute-start.5 = (f32[4,6912]{1,0:T(4,128)S(1)}, f32[4,6912]{1,0:T(4,128)S(1)}, u32[]{:S(2)}, u32[]{:S(2)}) collective-permute-start(f32[4,6912]{1,0:T(4,128)S(1)} %dynamic_update_slice.12), channel_id=1, source_target_pairs={{0,2},{2,0},{1,3},{3,1},{4,6},{6,4},{5,7},{7,5},{8,10},{10,8},{9,1... | collective-permute-start | bytes 331784 | tf_op jit(solution)/shard_map/ppermute | solution.py:543
  73.1 123.2 %collective-permute-start.20 = (bf16[4,208,1152]{2,1,0:T(8,128)(2,1)}, bf16[4,208,1152]{2,1,0:T(8,128)(2,1)}, u32[]{:S(2)}, u32[]{:S(2)}) collective-permute-start(bf16[4,208,1152]{2,1,0:T(8,128)(2,1)} %bitcast.556), channel_id=1, source_target_pairs={{0,4},{4,0},{1,5},{5,1},{2,6},{6,2},{3,7},{7,3},{8,12},{12,8},{9,1... | collective-permute-start | bytes 5750792 | tf_op jit(solution)/shard_map/ppermute | solution.py:543
  112.7 84.1 %collective-permute-start.28 = (bf16[4,72,3328]{2,1,0:T(8,128)(2,1)}, bf16[4,72,3328]{2,1,0:T(8,128)(2,1)}, u32[]{:S(2)}, u32[]{:S(2)}) collective-permute-start(bf16[4,72,3328]{2,1,0:T(8,128)(2,1)} %bitcast.38.refs_6_.refs_3_), channel_id=1, source_target_pairs={{0,4},{4,0},{1,5},{5,1},{2,6},{6,2},{3,7},{7,3},{8,12},{12,8},{9,1... | collective-permute-start | bytes 5750792 | tf_op jit(solution)/shard_map/ppermute | solution.py:543
  119.4 41.7 %collective-permute-start.7 = (f32[4,6912]{1,0:T(4,128)S(1)}, f32[4,6912]{1,0:T(4,128)S(1)}, u32[]{:S(2)}, u32[]{:S(2)}) collective-permute-start(f32[4,6912]{1,0:T(4,128)S(1)} %add.388), channel_id=1, source_target_pairs={{0,4},{4,0},{1,5},{5,1},{2,6},{6,2},{3,7},{7,3},{8,12},{12,8},{9,1... | collective-permute-start | bytes 331784 | tf_op jit(solution)/shard_map/ppermute | solution.py:543
  121.4 53.4 %collective-permute-start.19 = (bf16[4,80,1152]{2,1,0:T(8,128)(2,1)S(1)}, bf16[4,80,1152]{2,1,0:T(8,128)(2,1)S(1)}, u32[]{:S(2)}, u32[]{:S(2)}) collective-permute-start(bf16[4,80,1152]{2,1,0:T(8,128)(2,1)S(1)} %slice.398), channel_id=1, source_target_pairs={{0,1},{1,0},{2,3},{3,2},{4,5},{5,4},{6,7},{7,6},{8,9},{9,8},{10,11... | collective-permute-start | bytes 2211848 | tf_op jit(solution)/shard_map/ppermute | solution.py:543
  164.1 19.6 %collective-permute-start.27 = (bf16[4,72,1280]{2,1,0:T(8,128)(2,1)}, bf16[4,72,1280]{2,1,0:T(8,128)(2,1)S(1)}, u32[]{:S(2)}, u32[]{:S(2)}) collective-permute-start(bf16[4,72,1280]{2,1,0:T(8,128)(2,1)} %slice.403), channel_id=1, source_target_pairs={{0,1},{1,0},{2,3},{3,2},{4,5},{5,4},{6,7},{7,6},{8,9},{9,8},{10,11... | collective-permute-start | bytes 2211848 | tf_op jit(solution)/shard_map/ppermute | solution.py:543
  172.9 42.7 %collective-permute-start.12 = (bf16[4,3,72,1152]{3,2,0,1:T(8,128)(2,1)S(1)}, bf16[4,3,72,1152]{3,2,0,1:T(8,128)(2,1)S(1)}, u32[]{:S(2)}, u32[]{:S(2)}) collective-permute-start(bf16[4,3,72,1152]{3,2,0,1:T(8,128)(2,1)S(1)} %copy.88), channel_id=1, source_target_pairs={{0,4},{4,0},{1,5},{5,1},{2,6},{6,2},{3,7},{7,3},{8,12},{12,8},{9,1... | collective-permute-start | bytes 5971976 | tf_op jit(solution)/shard_map/ppermute | solution.py:543
  174.7 21.5 %collective-permute-start.11 = (bf16[4,72,1152]{2,1,0:T(8,128)(2,1)S(1)}, bf16[4,72,1152]{2,1,0:T(8,128)(2,1)S(1)}, u32[]{:S(2)}, u32[]{:S(2)}) collective-permute-start(bf16[4,72,1152]{2,1,0:T(8,128)(2,1)S(1)} %slice_bitcast_fusion.7), channel_id=1, source_target_pairs={{0,1},{1,0},{2,3},{3,2},{4,5},{5,4},{6,7},{7,6},{8,9},{9,8},{10,11... | collective-permute-start | bytes 1990664 | tf_op jit(solution)/shard_map/ppermute | solution.py:543
  183.7 32.0 %collective-permute-start.22 = (bf16[4,208,1152]{2,1,0:T(8,128)(2,1)S(1)}, bf16[4,208,1152]{2,1,0:T(8,128)(2,1)S(1)}, u32[]{:S(2)}, u32[]{:S(2)}) collective-permute-start(bf16[4,208,1152]{2,1,0:T(8,128)(2,1)S(1)} %bitcast.560), channel_id=1, source_target_pairs={{0,2},{2,0},{1,3},{3,1},{4,6},{6,4},{5,7},{7,5},{8,10},{10,8},{9,1... | collective-permute-start | bytes 5750792 | tf_op jit(solution)/shard_map/ppermute | solution.py:543
  196.3 25.4 %collective-permute-start.14 = (bf16[4,3,72,1152]{3,2,1,0:T(8,128)(2,1)S(1)}, bf16[4,3,72,1152]{3,2,1,0:T(8,128)(2,1)S(1)}, u32[]{:S(2)}, u32[]{:S(2)}) collective-permute-start(bf16[4,3,72,1152]{3,2,1,0:T(8,128)(2,1)S(1)} %bitcast.551), channel_id=1, source_target_pairs={{0,2},{2,0},{1,3},{3,1},{4,6},{6,4},{5,7},{7,5},{8,10},{10,8},{9,1... | collective-permute-start | bytes 5971976 | tf_op jit(solution)/shard_map/ppermute | solution.py:543
  202.3 19.3 %collective-permute-start.21 = (bf16[4,80,1152]{2,1,0:T(8,128)(2,1)S(1)}, bf16[4,80,1152]{2,1,0:T(8,128)(2,1)S(1)}, u32[]{:S(2)}, u32[]{:S(2)}) collective-permute-start(bf16[4,80,1152]{2,1,0:T(8,128)(2,1)S(1)} %slice.399), channel_id=1, source_target_pairs={{0,1},{1,0},{2,3},{3,2},{4,5},{5,4},{6,7},{7,6},{8,9},{9,8},{10,11... | collective-permute-start | bytes 2211848 | tf_op jit(solution)/shard_map/ppermute | solution.py:543
  203.6 34.0 %collective-permute-start.29 = (bf16[4,72,1280]{2,1,0:T(8,128)(2,1)S(1)}, bf16[4,72,1280]{2,1,0:T(8,128)(2,1)}, u32[]{:S(2)}, u32[]{:S(2)}) collective-permute-start(bf16[4,72,1280]{2,1,0:T(8,128)(2,1)S(1)} %slice.404), channel_id=1, source_target_pairs={{0,1},{1,0},{2,3},{3,2},{4,5},{5,4},{6,7},{7,6},{8,9},{9,8},{10,11... | collective-permute-start | bytes 2211848 | tf_op jit(solution)/shard_map/ppermute | solution.py:543
  215.7 40.9 %collective-permute-start.16 = (bf16[4,3,72,1152]{3,2,0,1:T(8,128)(2,1)S(1)}, bf16[4,3,72,1152]{3,2,0,1:T(8,128)(2,1)S(1)}, u32[]{:S(2)}, u32[]{:S(2)}) collective-permute-start(bf16[4,3,72,1152]{3,2,0,1:T(8,128)(2,1)S(1)} %collective-permute-done.12), channel_id=1, source_target_pairs={{0,2},{2,0},{1,3},{3,1},{4,6},{6,4},{5,7},{7,5},{8,10},{10,8},{9,1... | collective-permute-start | bytes 5971976 | tf_op jit(solution)/shard_map/ppermute | solution.py:543
  215.8 35.1 %collective-permute-start.13 = (bf16[4,72,1152]{2,1,0:T(8,128)(2,1)S(1)}, bf16[4,72,1152]{2,1,0:T(8,128)(2,1)S(1)}, u32[]{:S(2)}, u32[]{:S(2)}) collective-permute-start(bf16[4,72,1152]{2,1,0:T(8,128)(2,1)S(1)} %slice_bitcast_fusion.6), channel_id=1, source_target_pairs={{0,1},{1,0},{2,3},{3,2},{4,5},{5,4},{6,7},{7,6},{8,9},{9,8},{10,11... | collective-permute-start | bytes 1990664 | tf_op jit(solution)/shard_map/ppermute | solution.py:543
  221.6 29.2 %collective-permute-start.25 = (bf16[4,80,1152]{2,1,0:T(8,128)(2,1)S(1)}, bf16[4,80,1152]{2,1,0:T(8,128)(2,1)S(1)}, u32[]{:S(2)}, u32[]{:S(2)}) collective-permute-start(bf16[4,80,1152]{2,1,0:T(8,128)(2,1)S(1)} %collective-permute-done.21.refs_5_.refs_9_), channel_id=1, source_target_pairs={{0,2},{2,0},{1,3},{3,1},{4,6},{6,4},{5,7},{7,5},{8,10},{10,8},{9,1... | collective-permute-start | bytes 2211848 | tf_op jit(solution)/shard_map/ppermute | solution.py:543
  222.9 80.3 %collective-permute-start.24 = (bf16[4,208,1152]{2,1,0:T(8,128)(2,1)}, bf16[4,208,1152]{2,1,0:T(8,128)(2,1)S(1)}, u32[]{:S(2)}, u32[]{:S(2)}) collective-permute-start(bf16[4,208,1152]{2,1,0:T(8,128)(2,1)} %collective-permute-done.20.refs_4_.refs_8_), channel_id=1, source_target_pairs={{0,2},{2,0},{1,3},{3,1},{4,6},{6,4},{5,7},{7,5},{8,10},{10,8},{9,1... | collective-permute-start | bytes 5750792 | tf_op jit(solution)/shard_map/ppermute | solution.py:543
  237.5 94.4 %collective-permute-start.30 = (bf16[4,72,3328]{2,1,0:T(8,128)(2,1)}, bf16[4,72,3328]{2,1,0:T(8,128)(2,1)}, u32[]{:S(2)}, u32[]{:S(2)}) collective-permute-start(bf16[4,72,3328]{2,1,0:T(8,128)(2,1)} %bitcast.38.refs_6_.refs_3_), channel_id=1, source_target_pairs={{0,2},{2,0},{1,3},{3,1},{4,6},{6,4},{5,7},{7,5},{8,10},{10,8},{9,1... | collective-permute-start | bytes 5750792 | tf_op jit(solution)/shard_map/ppermute | solution.py:543
  250.8 81.1 %collective-permute-start.32 = (bf16[4,72,3328]{2,1,0:T(8,128)(2,1)}, bf16[4,72,3328]{2,1,0:T(8,128)(2,1)}, u32[]{:S(2)}, u32[]{:S(2)}) collective-permute-start(bf16[4,72,3328]{2,1,0:T(8,128)(2,1)} %collective-permute-done.28.refs_8_.refs_5_), channel_id=1, source_target_pairs={{0,2},{2,0},{1,3},{3,1},{4,6},{6,4},{5,7},{7,5},{8,10},{10,8},{9,1... | collective-permute-start | bytes 5750792 | tf_op jit(solution)/shard_map/ppermute | solution.py:543
  256.1 75.8 %collective-permute-start.31 = (bf16[4,72,1280]{2,1,0:T(8,128)(2,1)}, bf16[4,72,1280]{2,1,0:T(8,128)(2,1)}, u32[]{:S(2)}, u32[]{:S(2)}) collective-permute-start(bf16[4,72,1280]{2,1,0:T(8,128)(2,1)} %copy-done.34), channel_id=1, source_target_pairs={{0,2},{2,0},{1,3},{3,1},{4,6},{6,4},{5,7},{7,5},{8,10},{10,8},{9,1... | collective-permute-start | bytes 2211848 | tf_op jit(solution)/shard_map/ppermute | solution.py:543
  257.8 74.1 %collective-permute-start.33 = (bf16[4,72,1280]{2,1,0:T(8,128)(2,1)}, bf16[4,72,1280]{2,1,0:T(8,128)(2,1)}, u32[]{:S(2)}, u32[]{:S(2)}) collective-permute-start(bf16[4,72,1280]{2,1,0:T(8,128)(2,1)} %collective-permute-done.29.refs_9_.refs_6_), channel_id=1, source_target_pairs={{0,2},{2,0},{1,3},{3,1},{4,6},{6,4},{5,7},{7,5},{8,10},{10,8},{9,1... | collective-permute-start | bytes 2211848 | tf_op jit(solution)/shard_map/ppermute | solution.py:543
  466.1 12.9 %collective-permute-start.35 = (f32[4,6912]{1,0:T(4,128)S(1)}, f32[4,6912]{1,0:T(4,128)S(1)}, u32[]{:S(2)}, u32[]{:S(2)}) collective-permute-start(f32[4,6912]{1,0:T(4,128)S(1)} %fusion.92), channel_id=1, source_target_pairs={{0,1},{1,0},{2,3},{3,2},{4,5},{5,4},{6,7},{7,6},{8,9},{9,8},{10,11... | collective-permute-start | bytes 331784 | tf_op jit(solution)/shard_map/ppermute | solution.py:543
  478.9 52.7 %collective-permute-start.54 = (bf16[2,4,72,4608]{3,2,1,0:T(8,128)(2,1)}, bf16[2,4,72,4608]{3,2,1,0:T(8,128)(2,1)}, u32[]{:S(2)}, u32[]{:S(2)}) collective-permute-start(bf16[2,4,72,4608]{3,2,1,0:T(8,128)(2,1)} %bitcast.575), channel_id=1, source_target_pairs={{0,2},{2,0},{1,3},{3,1},{4,6},{6,4},{5,7},{7,5},{8,10},{10,8},{9,1... | collective-permute-start | bytes 15925256 | tf_op jit(solution)/shard_map/ppermute | solution.py:543
  494.2 130.3 %collective-permute-start.44 = (bf16[2,4,3,72,1152]{4,3,1,2,0:T(8,128)(2,1)}, bf16[2,4,3,72,1152]{4,3,1,2,0:T(8,128)(2,1)}, u32[]{:S(2)}, u32[]{:S(2)}) collective-permute-start(bf16[2,4,3,72,1152]{4,3,1,2,0:T(8,128)(2,1)} %copy.97), channel_id=1, source_target_pairs={{0,2},{2,0},{1,3},{3,1},{4,6},{6,4},{5,7},{7,5},{8,10},{10,8},{9,1... | collective-permute-start | bytes 11943944 | tf_op jit(solution)/shard_map/ppermute | solution.py:543
  494.2 14.6 %collective-permute-start.38 = (f32[4,6912]{1,0:T(4,128)S(1)}, f32[4,6912]{1,0:T(4,128)S(1)}, u32[]{:S(2)}, u32[]{:S(2)}) collective-permute-start(f32[4,6912]{1,0:T(4,128)S(1)} %add.395), channel_id=1, source_target_pairs={{0,16},{8,24},{16,0},{24,8},{1,17},{9,25},{17,1},{25,9},{2,18},{10... | collective-permute-start | bytes 331784 | tf_op jit(solution)/shard_map/ppermute | solution.py:550
  506.7 60.7 %collective-permute-start.50 = (bf16[2,4,288,1152]{3,2,1,0:T(8,128)(2,1)}, bf16[2,4,288,1152]{3,2,1,0:T(8,128)(2,1)S(1)}, u32[]{:S(2)}, u32[]{:S(2)}) collective-permute-start(bf16[2,4,288,1152]{3,2,1,0:T(8,128)(2,1)} %bitcast.576), channel_id=1, source_target_pairs={{0,2},{2,0},{1,3},{3,1},{4,6},{6,4},{5,7},{7,5},{8,10},{10,8},{9,1... | collective-permute-start | bytes 15925256 | tf_op jit(solution)/shard_map/ppermute | solution.py:543
  511.3 23.5 %collective-permute-start.46 = (bf16[2,4,72,1152]{3,2,1,0:T(8,128)(2,1)S(1)}, bf16[2,4,72,1152]{3,2,1,0:T(8,128)(2,1)S(1)}, u32[]{:S(2)}, u32[]{:S(2)}) collective-permute-start(bf16[2,4,72,1152]{3,2,1,0:T(8,128)(2,1)S(1)} %bitcast.545), channel_id=1, source_target_pairs={{0,2},{2,0},{1,3},{3,1},{4,6},{6,4},{5,7},{7,5},{8,10},{10,8},{9,1... | collective-permute-start | bytes 3981320 | tf_op jit(solution)/shard_map/ppermute | solution.py:543
  529.7 161.4 %collective-permute-start.43 = (f32[4,1152]{1,0:T(4,128)S(1)}, f32[4,1152]{1,0:T(4,128)S(1)}, u32[]{:S(2)}, u32[]{:S(2)}) collective-permute-start(f32[4,1152]{1,0:T(4,128)S(1)} %add.400), channel_id=1, source_target_pairs={{0,16},{8,24},{16,0},{24,8},{1,17},{9,25},{17,1},{25,9},{2,18},{10... | collective-permute-start | bytes 55304 | tf_op jit(solution)/shard_map/ppermute | solution.py:550
  534.2 31.5 %collective-permute-start.56 = (bf16[2,4,72,1280]{3,2,1,0:T(8,128)(2,1)S(1)}, bf16[2,4,72,1280]{3,2,1,0:T(8,128)(2,1)S(1)}, u32[]{:S(2)}, u32[]{:S(2)}) collective-permute-start(bf16[2,4,72,1280]{3,2,1,0:T(8,128)(2,1)S(1)} %add_convert_fusion), channel_id=1, source_target_pairs={{0,1},{1,0},{2,3},{3,2},{4,5},{5,4},{6,7},{7,6},{8,9},{9,8},{10,11... | collective-permute-start | bytes 4423688 | tf_op jit(solution)/shard_map/ppermute | solution.py:543
  536.0 123.2 %collective-permute-start.47 = (bf16[4,72,1152]{2,1,0:T(8,128)(2,1)}, bf16[4,72,1152]{2,1,0:T(8,128)(2,1)S(1)}, u32[]{:S(2)}, u32[]{:S(2)}) collective-permute-start(bf16[4,72,1152]{2,1,0:T(8,128)(2,1)} %fusion.18), channel_id=1, source_target_pairs={{0,4},{4,0},{1,5},{5,1},{2,6},{6,2},{3,7},{7,3},{8,12},{12,8},{9,1... | collective-permute-start | bytes 1990664 | tf_op jit(solution)/shard_map/ppermute | solution.py:543
  565.7 28.9 %collective-permute-start.55 = (bf16[4,72,2048]{2,1,0:T(8,128)(2,1)S(1)}, bf16[4,72,2048]{2,1,0:T(8,128)(2,1)S(1)}, u32[]{:S(2)}, u32[]{:S(2)}) collective-permute-start(bf16[4,72,2048]{2,1,0:T(8,128)(2,1)S(1)} %fusion.32), channel_id=1, source_target_pairs={{0,4},{4,0},{1,5},{5,1},{2,6},{6,2},{3,7},{7,3},{8,12},{12,8},{9,1... | collective-permute-start | bytes 3538952 | tf_op jit(solution)/shard_map/ppermute | solution.py:543
  567.5 38.3 %collective-permute-start.57 = (bf16[4,72,1280]{2,1,0:T(8,128)(2,1)S(1)}, bf16[4,72,1280]{2,1,0:T(8,128)(2,1)S(1)}, u32[]{:S(2)}, u32[]{:S(2)}) collective-permute-start(bf16[4,72,1280]{2,1,0:T(8,128)(2,1)S(1)} %fusion.42), channel_id=1, source_target_pairs={{0,4},{4,0},{1,5},{5,1},{2,6},{6,2},{3,7},{7,3},{8,12},{12,8},{9,1... | collective-permute-start | bytes 2211848 | tf_op jit(solution)/shard_map/ppermute | solution.py:543
  594.6 26.3 %collective-permute-start.52 = (bf16[2,4,80,1152]{3,2,1,0:T(8,128)(2,1)}, bf16[2,4,80,1152]{3,2,1,0:T(8,128)(2,1)}, u32[]{:S(2)}, u32[]{:S(2)}) collective-permute-start(bf16[2,4,80,1152]{3,2,1,0:T(8,128)(2,1)} %add_convert_fusion.1), channel_id=1, source_target_pairs={{0,1},{1,0},{2,3},{3,2},{4,5},{5,4},{6,7},{7,6},{8,9},{9,8},{10,11... | collective-permute-start | bytes 4423688 | tf_op jit(solution)/shard_map/ppermute | solution.py:543
  607.6 83.5 %reduce-scatter.8.cloned.1.call-start = ((), (), s32[]{:S(2)}) async-start(), calls=%async_computation.4 | async-start | bytes 2396160 | tf_op jit(solution)/shard_map/reduce_scatter | solution.py:597
  609.5 29.0 %collective-permute-start.51 = (bf16[4,128,1152]{2,1,0:T(8,128)(2,1)S(1)}, bf16[4,128,1152]{2,1,0:T(8,128)(2,1)S(1)}, u32[]{:S(2)}, u32[]{:S(2)}) collective-permute-start(bf16[4,128,1152]{2,1,0:T(8,128)(2,1)S(1)} %fusion.30), channel_id=1, source_target_pairs={{0,4},{4,0},{1,5},{5,1},{2,6},{6,2},{3,7},{7,3},{8,12},{12,8},{9,1... | collective-permute-start | bytes 3538952 | tf_op jit(solution)/shard_map/ppermute | solution.py:543
  622.4 26.4 %collective-permute-start.53 = (bf16[4,80,1152]{2,1,0:T(8,128)(2,1)S(1)}, bf16[4,80,1152]{2,1,0:T(8,128)(2,1)S(1)}, u32[]{:S(2)}, u32[]{:S(2)}) collective-permute-start(bf16[4,80,1152]{2,1,0:T(8,128)(2,1)S(1)} %fusion.40), channel_id=1, source_target_pairs={{0,4},{4,0},{1,5},{5,1},{2,6},{6,2},{3,7},{7,3},{8,12},{12,8},{9,1... | collective-permute-start | bytes 2211848 | tf_op jit(solution)/shard_map/ppermute | solution.py:543
  627.9 29.3 %collective-permute-start.48 = (bf16[2,4,72,1152]{3,2,1,0:T(8,128)(2,1)}, bf16[2,4,72,1152]{3,2,1,0:T(8,128)(2,1)}, u32[]{:S(2)}, u32[]{:S(2)}) collective-permute-start(bf16[2,4,72,1152]{3,2,1,0:T(8,128)(2,1)} %fusion.16), channel_id=1, source_target_pairs={{0,1},{1,0},{2,3},{3,2},{4,5},{5,4},{6,7},{7,6},{8,9},{9,8},{10,11... | collective-permute-start | bytes 3981320 | tf_op jit(solution)/shard_map/ppermute | solution.py:543
  651.7 82.6 %reduce-scatter.10.cloned.1.call-start = ((), (), s32[]{:S(2)}) async-start(), calls=%async_computation.8 | async-start | bytes 2488320
  653.5 17.9 %collective-permute-start.45 = (bf16[4,72,1152]{2,1,0:T(8,128)(2,1)S(1)}, bf16[4,72,1152]{2,1,0:T(8,128)(2,1)S(1)}, u32[]{:S(2)}, u32[]{:S(2)}) collective-permute-start(bf16[4,72,1152]{2,1,0:T(8,128)(2,1)S(1)} %fusion.44), channel_id=1, source_target_pairs={{0,4},{4,0},{1,5},{5,1},{2,6},{6,2},{3,7},{7,3},{8,12},{12,8},{9,1... | collective-permute-start | bytes 1990664 | tf_op jit(solution)/shard_map/ppermute | solution.py:543
  658.8 20.7 %collective-permute-start.49 = (bf16[4,72,1152]{2,1,0:T(8,128)(2,1)S(1)}, bf16[4,72,1152]{2,1,0:T(8,128)(2,1)S(1)}, u32[]{:S(2)}, u32[]{:S(2)}) collective-permute-start(bf16[4,72,1152]{2,1,0:T(8,128)(2,1)S(1)} %fusion.46), channel_id=1, source_target_pairs={{0,4},{4,0},{1,5},{5,1},{2,6},{6,2},{3,7},{7,3},{8,12},{12,8},{9,1... | collective-permute-start | bytes 1990664 | tf_op jit(solution)/shard_map/ppermute | solution.py:543
  693.5 12.6 %collective-permute-start.59 = (bf16[208,1152]{1,0:T(8,128)(2,1)S(1)}, bf16[208,1152]{1,0:T(8,128)(2,1)S(1)}, u32[]{:S(2)}, u32[]{:S(2)}) collective-permute-start(bf16[208,1152]{1,0:T(8,128)(2,1)S(1)} %copy-done.46), channel_id=1, source_target_pairs={{0,1},{1,0},{2,3},{3,2},{4,5},{5,4},{6,7},{7,6},{8,9},{9,8},{10,11... | collective-permute-start | bytes 1437704 | tf_op jit(solution)/shard_map/ppermute | solution.py:543
  736.0 13.0 %collective-permute-start.58 = (bf16[3,72,1152]{2,1,0:T(8,128)(2,1)S(1)}, bf16[3,72,1152]{2,1,0:T(8,128)(2,1)S(1)}, u32[]{:S(2)}, u32[]{:S(2)}) collective-permute-start(bf16[3,72,1152]{2,1,0:T(8,128)(2,1)S(1)} %copy.101), channel_id=1, source_target_pairs={{0,1},{1,0},{2,3},{3,2},{4,5},{5,4},{6,7},{7,6},{8,9},{9,8},{10,11... | collective-permute-start | bytes 1493000 | tf_op jit(solution)/shard_map/ppermute | solution.py:543
  (84 other events, 967.4 us)
Sparse Core Ops, SparseCore 0:
  23.9 44.1 all-gather.8
  70.3 42.4 all-gather.10
  114.9 42.8 all-gather.6
  607.7 39.2 reduce-scatter.5
  651.9 39.2 reduce-scatter.7
  693.3 41.0 reduce-scatter.9

commit v2 on v1

--- a/solution.py
+++ b/solution.py
@@ -74,6 +74,7 @@
 
 BF16, F32 = jnp.bfloat16, jnp.float32
 SLAB = 16
+COST_FLOPS, COST_BYTES = 6e9, 18e6
 GROUP = 128
 WIDE = 256
 
@@ -102,7 +103,11 @@
     return lax.dot_general(left, right, (((1,), (1,)), ((), ())), preferred_element_type=F32)
 
 
-def run_kernel(body, operands, outs, scratch, ordered_after=(), mib=56, **kw):
+def cost(us):
+    return pl.CostEstimate(flops=int(us * COST_FLOPS), bytes_accessed=int(us * COST_BYTES), transcendentals=0)
+
+
+def run_kernel(body, operands, outs, scratch, us, ordered_after=(), mib=56, **kw):
     arrays = [array for array, _ in operands] + list(ordered_after)
     specs = [spec for _, spec in operands] + [any_spec() for _ in ordered_after]
     n_in, n_dep = len(operands), len(ordered_after)
@@ -117,9 +122,12 @@
         out_specs=[vmem_spec() for _ in outs],
         scratch_shapes=scratch,
         compiler_params=pltpu.CompilerParams(vmem_limit_bytes=mib * 2**20),
-        cost_estimate=pl.CostEstimate(flops=1000, bytes_accessed=1000, transcendentals=0),
+        cost_estimate=cost(us),
         **kw,
     )(*arrays)
+
+
+PIECES = 8
 
 
 def block_order(place):
@@ -129,7 +137,7 @@
             yy = y if dy == 0 else 1 - y
             cc = c if dc == 0 else 1 - c
             for zz in range(4):
-                yield dc * 2 + dy, zz, (zz * 2 + yy) * 2 + cc
+                yield dc * 4 + dy * 2, zz, (zz * 2 + yy) * 2 + cc
 
 
 def start_all(copies, sems):
@@ -141,16 +149,16 @@
 
 def attend_copies(pieces, place, wide):
     x = place[3]
-    for pair, zz, b in block_order(place):
-        main, late = pieces[2 * pair], pieces[2 * pair + 1]
+    for at, zz, b in block_order(place):
+        main, other = pieces[at : at + 2]
         yield main.at[zz, 0], wide.at[b * 3]
         yield main.at[zz, 2], wide.at[b * 3 + 1 + x]
-        yield late.at[zz], wide.at[b * 3 + 2 - x]
+        yield other.at[zz], wide.at[b * 3 + 2 - x]
 
 
 def merge_copies(pieces, place, wide):
-    for pair, zz, b in block_order(place):
-        yield pieces[2 * pair].at[zz, 1], wide.at[b]
+    for at, zz, b in block_order(place):
+        yield pieces[at].at[zz, 1], wide.at[b]
 
 
 UP_E, UP_L = 128, 80
@@ -159,14 +167,14 @@
 def up_copies(pieces, place, wide):
     x = place[3]
     size = UP_E + 2 * UP_L
-    for pair, zz, b in block_order(place):
-        main, late = pieces[2 * pair], pieces[2 * pair + 1]
+    for at, zz, b in block_order(place):
+        main, other = pieces[at : at + 2]
         row = pl.multiple_of(b * size, 16)
-        near = pl.multiple_of(b * size + UP_E + UP_L * x, 16)
-        other = pl.multiple_of(b * size + UP_E + UP_L - UP_L * x, 16)
+        near_row = pl.multiple_of(b * size + UP_E + UP_L * x, 16)
+        other_row = pl.multiple_of(b * size + UP_E + UP_L - UP_L * x, 16)
         yield main.at[zz, pl.ds(0, UP_E)], wide.at[pl.ds(row, UP_E)]
-        yield main.at[zz, pl.ds(UP_E, UP_L)], wide.at[pl.ds(near, UP_L)]
-        yield late.at[zz], wide.at[pl.ds(other, UP_L)]
+        yield main.at[zz, pl.ds(UP_E, UP_L)], wide.at[pl.ds(near_row, UP_L)]
+        yield other.at[zz], wide.at[pl.ds(other_row, UP_L)]
 
 
 DOWN_E, DOWN_L = 2048, 1280
@@ -174,13 +182,13 @@
 
 def down_copies(pieces, place, wide):
     x = place[3]
-    near = pl.multiple_of(DOWN_E + DOWN_L * x, 128)
-    other = pl.multiple_of(DOWN_E + DOWN_L - DOWN_L * x, 128)
-    for pair, zz, b in block_order(place):
-        main, late = pieces[2 * pair], pieces[2 * pair + 1]
+    near_col = pl.multiple_of(DOWN_E + DOWN_L * x, 128)
+    other_col = pl.multiple_of(DOWN_E + DOWN_L - DOWN_L * x, 128)
+    for at, zz, b in block_order(place):
+        main, other = pieces[at : at + 2]
         yield main.at[zz, :, pl.ds(0, DOWN_E)], wide.at[b, :, pl.ds(0, DOWN_E)]
-        yield main.at[zz, :, pl.ds(DOWN_E, DOWN_L)], wide.at[b, :, pl.ds(near, DOWN_L)]
-        yield late.at[zz], wide.at[b, :, pl.ds(other, DOWN_L)]
+        yield main.at[zz, :, pl.ds(DOWN_E, DOWN_L)], wide.at[b, :, pl.ds(near_col, DOWN_L)]
+        yield other.at[zz], wide.at[b, :, pl.ds(other_col, DOWN_L)]
 
 
 def rows_of(wide, first, count, cols=None):
@@ -240,18 +248,16 @@
     return expo / jnp.sum(expo, axis=0, keepdims=True)
 
 
-def first_half_kernel(place, tokens, mods, *rest):
-    pieces, rest = rest[:8], rest[8:]
-    h1, qkv, attended, branch, h2, wide, merge, turned, sems = rest
-    copies = list(attend_copies(pieces, place, wide)) + list(merge_copies(pieces, place, merge))
-    copies = start_all(copies, sems)
-    rows = tokens.shape[0]
+def qkv_kernel(place, tokens, mods, *rest):
+    pieces, rest = rest[:PIECES], rest[PIECES:]
+    h1, qkv, wide, sems = rest
+    copies = start_all(list(attend_copies(pieces, place, wide)), sems)
 
     def norm_one(at):
         normed, _ = norm_slab(tokens[at].astype(F32))
         h1[at] = (normed * (1.0 + mods[1:2]) + mods[0:1]).astype(BF16)
 
-    slabs(rows, SLAB, norm_one)
+    slabs(tokens.shape[0], SLAB, norm_one)
     for copy in copies:
         copy.wait()
 
@@ -261,6 +267,12 @@
         for j in range(4):
             qkv[i * 4 + j] = value[j * HEAD : (j + 1) * HEAD].astype(BF16)
 
+
+def attend_kernel(place, qkv, tokens, mods, *rest):
+    pieces, rest = rest[:PIECES], rest[PIECES:]
+    attended, branch, h2, merge, turned, sems = rest
+    copies = start_all(list(merge_copies(pieces, place, merge)), sems)
+    rows = tokens.shape[0]
     mask = frame_mask(place[4])
 
     @pl.loop(0, HEADS)
@@ -273,6 +285,8 @@
     for group in range(rows // GROUP):
         at = pl.ds(group * GROUP, GROUP)
         attended[at] = turned[:, :, at].reshape(D, GROUP).T.astype(BF16)
+    for copy in copies:
+        copy.wait()
     branch[...] = dot_nt(attended[...], rows_of(merge, 0, 16))
 
     def norm_two(at):
@@ -284,7 +298,7 @@
 
 
 def up_kernel(place, h2, *rest):
-    pieces, rest = rest[:8], rest[8:]
+    pieces, rest = rest[:PIECES], rest[PIECES:]
     act, slope, wide, upper, sems = rest
     for copy in start_all(list(up_copies(pieces, place, wide)), sems):
         copy.wait()
@@ -322,7 +336,7 @@
 
 
 def d_upper_kernel(place, d_mlp, slope, *rest):
-    pieces, rest = rest[:8], rest[8:]
+    pieces, rest = rest[:PIECES], rest[PIECES:]
     d_upper, d_upper_t, wide, value, sems = rest
     for copy in start_all(list(down_copies(pieces, place, wide)), sems):
         copy.wait()
@@ -342,7 +356,7 @@
 
 
 def middle_back_kernel(place, d_upper, tokens, out_grad, branch, mods, *rest):
-    ups, firsts, rest = rest[:8], rest[8:16], rest[16:]
+    ups, firsts, rest = rest[:PIECES], rest[PIECES : 2 * PIECES], rest[2 * PIECES :]
     d_middle, d_branch, relative, d_att, sums, wide, merge, value, turned, fold_a, fold_b, fold_c, sems = rest
     copies = list(up_copies(ups, place, wide)) + list(merge_copies(firsts, place, merge))
     copies = start_all(copies, sems)
@@ -413,7 +427,7 @@
 
 
 def input_back_kernel(place, d_qkv, tokens, d_middle, mods, *rest):
-    pieces, rest = rest[:8], rest[8:]
+    pieces, rest = rest[:PIECES], rest[PIECES:]
     input_grad, sums, wide, value, fold_a, fold_b, sems = rest
     for copy in start_all(list(attend_copies(pieces, place, wide)), sems):
         copy.wait()
@@ -442,7 +456,7 @@
 
 
 def output_kernel(place, act, tokens, branch, out_grad, mods, *rest):
-    pieces, rest = rest[:8], rest[8:]
+    pieces, rest = rest[:PIECES], rest[PIECES:]
     block_out, sums, wide, value, fold_a, sems = rest
     for copy in start_all(list(down_copies(pieces, place, wide)), sems):
         copy.wait()
@@ -494,7 +508,7 @@
         + [any_spec()] * n_dep,
         out_specs=[pl.BlockSpec((row_block, col_block), lambda j, i: (i, j))] * 2,
         compiler_params=pltpu.CompilerParams(vmem_limit_bytes=40 * 2**20),
-        cost_estimate=pl.CostEstimate(flops=1000, bytes_accessed=1000, transcendentals=0),
+        cost_estimate=cost(rows * cols * depth / 3e8),
     )(left, left, right, *ordered_after)
 
 
@@ -530,7 +544,7 @@
             out_specs=[pl.BlockSpec((1, size, cols), lambda i, place_ref: (i, 0, 0))] * 2,
         ),
         compiler_params=pltpu.CompilerParams(vmem_limit_bytes=40 * 2**20),
-        cost_estimate=pl.CostEstimate(flops=1000, bytes_accessed=1000, transcendentals=0),
+        cost_estimate=cost(9),
     )(place, left, left, right, *ordered_after)
 
 
@@ -543,12 +557,28 @@
     return lax.ppermute(value, axis, [(0, 1), (1, 0)])
 
 
-def sum_all(value):
+def sum_plane(value):
     for axis in ("c", "x", "y"):
         value = value + swap(value, axis)
+    return value
+
+
+def sum_all(value):
+    value = sum_plane(value)
     for step in (1, 2):
         value = value + lax.ppermute(value, "z", [(i, i ^ step) for i in range(4)])
     return value
+
+
+def turn_z(value, z):
+    out = jnp.zeros_like(value)
+    own = lax.dynamic_slice_in_dim(value, z, 1, 0)
+    out = lax.dynamic_update_slice_in_dim(out, own, z, 0)
+    for step in (1, 2, 3):
+        entry = lax.dynamic_slice_in_dim(value, (z + step) % 4, 1, 0)
+        got = lax.ppermute(entry, "z", [(i, (i + step) % 4) for i in range(4)])
+        out = lax.dynamic_update_slice_in_dim(out, got, (z + 4 - step) % 4, 0)
+    return out
 
 
 def add_low(*terms):
@@ -558,7 +588,11 @@
     return total.astype(BF16)
 
 
-def gather_pieces(early, late, flag_early, flag_late, axis, cut, x):
+def after(value, *others):
+    return lax.optimization_barrier((value, *others))[0]
+
+
+def own_block(early, late, flag_early, flag_late, axis, x, before):
     first = x == 0
     near_late, far_late = jnp.where(first, late[0], late[1]), jnp.where(first, late[1], late[0])
     flag = jnp.concatenate(
@@ -568,24 +602,35 @@
         ],
         axis=axis,
     )
-    got = swap(jnp.concatenate([early, far_late], axis=axis), "x")
-    mine = jnp.where(flag, jnp.concatenate([early, near_late], axis=axis), got)
-    near = lax.all_gather(mine, "z", axis=0, tiled=False)
-    far = swap(near, "y")
-    pieces = [near, swap(cut(near), "x"), far, swap(cut(far), "x")]
+    got = swap(after(jnp.concatenate([early, far_late], axis=axis), *before), "x")
+    return jnp.where(flag, jnp.concatenate([early, near_late], axis=axis), got)
+
+
+def gather_near(mine):
+    near = lax.all_gather(mine.reshape(-1, mine.shape[-1]), "z", axis=0, tiled=False)
+    return near.reshape(near.shape[:1] + mine.shape)
+
+
+def gather_pieces(near, cut, before_far, before_late):
+    far = swap(after(near, *before_far), "y")
+    late = swap(cut(after(far, *before_late)), "x")
+    pieces = [near, swap(cut(near), "x"), far, late]
     return pieces + [swap(piece, "c") for piece in pieces]
 
 
-def split_sum(keep, send, cut, x):
+def core_sum(keep, send, cut, x):
     got = swap(send, "c")
     first = x == 0
     (ke, k0, k1), (ge, g0, g1) = cut(keep), cut(got)
+    early = [add_low(ke[i], ge[i]) for i in range(2)]
     late_send = add_low(jnp.where(first, k1, k0), jnp.where(first, g1, g0))
-    late_got = swap(late_send, "x")
-    kl, gl = jnp.where(first, k0, k1), jnp.where(first, g0, g1)
-    early = [add_low(ke[i], ge[i]) for i in range(2)]
-    late = [add_low(kl[i], gl[i], late_got[i]) for i in range(2)]
-    return early, late
+    late_keep = add_low(jnp.where(first, k0, k1), jnp.where(first, g0, g1))
+    return early, late_keep, late_send
+
+
+def late_sum(late_keep, late_send, before):
+    got = after(swap(late_send, "x"), *before)
+    return [add_low(late_keep[i], got[i]) for i in range(2)]
 
 
 def over_y(halves):
@@ -616,32 +661,32 @@
     attend_t, merge_t, up_t, down_t = own_low[3:]
     tiles = attend_t.reshape(3, span, width)
     flags = jnp.stack([own[3], own[4]])[:, None, None]
-    firsts = gather_pieces(
+    first_mine = own_block(
         jnp.stack([tiles[0], merge_t]),
         (tiles[1:2], tiles[2:3]),
-        flags,
+        jnp.stack([own[3], own[4]])[:, None, None],
         (own[3], own[3]),
         0,
-        lambda main: main[:, 2],
         x,
-    )
-    ups = gather_pieces(
+        (),
+    )
+    up_mine = own_block(
         up_t[:UP_E],
         (up_t[UP_E : UP_E + UP_L], up_t[UP_E + UP_L :]),
         own[5],
         (own[5], own[5]),
         0,
-        lambda main: main[:, UP_E:],
         x,
-    )
-    downs = gather_pieces(
+        (first_mine,),
+    )
+    down_mine = own_block(
         down_t[:, :DOWN_E],
         (down_t[:, DOWN_E : DOWN_E + DOWN_L], down_t[:, DOWN_E + DOWN_L :]),
         own[6],
         (own[6], own[6]),
         1,
-        lambda main: main[:, :, DOWN_E:],
         x,
+        (up_mine,),
     )
 
     features = timestep_features(timesteps).astype(BF16)
@@ -658,13 +703,17 @@
     cond_act = cond_act.astype(BF16)
     mod_part = jnp.where(own[2], contract_cols(cond_act, own_low[2]), 0.0)
     mod_span = mod_part.shape[1]
-    modulation = sum_all(
-        lax.dynamic_update_slice_in_dim(
-            jnp.zeros((clips, 6 * width), F32), mod_part, block * mod_span, 1
-        )
-    )
-    mod_row = lax.dynamic_index_in_dim(modulation, clip_index, 0, keepdims=False)
+    mod_row = lax.dynamic_update_slice(
+        jnp.zeros((4, 4, mod_span), F32), turn_z(mod_part, z)[:, None], (0, y * 2 + c, 0)
+    )
+    mod_row = sum_plane(mod_row)
     mods = jnp.concatenate([mod_row.reshape(6, width), jnp.zeros((2, width), F32)])
+
+    first_near, up_near, down_near = (
+        gather_near(mine) for mine in (first_mine, up_mine, down_mine)
+    )
+    firsts = gather_pieces(first_near, lambda main: main[:, 2], (mods,), ())
+    ups = gather_pieces(up_near, lambda main: main[:, UP_E:], firsts[:1], ())
 
     tokens = inputs.reshape(rows, width)
     grad_out = out_grad.reshape(rows, width)
@@ -678,56 +727,54 @@
         [spot] + in_vmem(grad_out, mods),
         [((rows, width), BF16), ((2, 8, span, rows), BF16)],
         [vmem(width, rows, dtype=F32)],
-    )
-    h1, qkv, attended, branch, h2 = run_kernel(
-        first_half_kernel,
+        us=4,
+    )
+    h1, qkv = run_kernel(
+        qkv_kernel,
         [spot] + in_vmem(tokens, mods) + in_place(firsts),
-        [
-            ((rows, width), BF16),
-            ((48, span, rows), BF16),
-            ((rows, width), BF16),
-            ((rows, width), F32),
-            ((rows, width), BF16),
-        ],
-        [
-            vmem(48, span, width),
-            vmem(16, span, width),
-            vmem(16, span, rows, dtype=F32),
-            sems(64),
-        ],
-    )
+        [((rows, width), BF16), ((48, span, rows), BF16)],
+        [vmem(48, span, width), sems(48)],
+        us=18,
+        ordered_after=[down_near],
+    )
+    attended, branch, h2 = run_kernel(
+        attend_kernel,
+        [spot] + in_vmem(qkv, tokens, mods) + in_place(firsts),
+        [((rows, width), BF16), ((rows, width), F32), ((rows, width), BF16)],
+        [vmem(16, span, width), vmem(16, span, rows, dtype=F32), sems(16)],
+        us=20,
+    )
+    downs = gather_pieces(down_near, lambda main: main[:, :, DOWN_E:], ups[:1], (h2,))
     act, slope = run_kernel(
         up_kernel,
         [spot] + in_vmem(h2) + in_place(ups),
         [((rows, FF), BF16)] * 2,
         [vmem(FF, width), vmem(rows, WIDE, dtype=F32), sems(48)],
-    )
-    down_keep, down_send = pair_grads(d_mlp_rel.reshape(2, 8 * span, rows), act)
+        us=27,
+    )
+    down_keep, down_send = pair_grads(d_mlp_rel.reshape(2, 8 * span, rows), act, downs[3:4])
     cut_down = lambda v: (
         v[..., :DOWN_E],
         v[..., DOWN_E : DOWN_E + DOWN_L],
         v[..., DOWN_E + DOWN_L :],
     )
     shape = (2, 4, span, FF)
-    early, late = split_sum(down_keep.reshape(shape), down_send.reshape(shape), cut_down, x)
-    down_part = over_z(jnp.concatenate([over_y(early), over_y(late)], axis=-1))
-    down_got = swap(down_part, "x")
+    down_early, *down_late = core_sum(down_keep.reshape(shape), down_send.reshape(shape), cut_down, x)
 
     d_upper, d_upper_t = run_kernel(
         d_upper_kernel,
         [spot] + in_vmem(d_mlp, slope) + in_place(downs),
         [((rows, FF), BF16), ((FF, rows), BF16)],
         [vmem(16, span, FF), vmem(rows, WIDE, dtype=F32), sems(48)],
+        us=28,
+        ordered_after=[down_early[1], down_late[1]],
     )
     up_keep, up_send = up_grads(place, d_upper_t, h2)
     cut_up = lambda v: (v[:, :, :UP_E], v[:, :, UP_E : UP_E + UP_L], v[:, :, UP_E + UP_L :])
     shape = (2, 4, 4 * span, width)
-    early, late = split_sum(up_keep.reshape(shape), up_send.reshape(shape), cut_up, x)
-    up_total = jnp.concatenate([over_y(early), over_y(late)], axis=1)
-    up_total, _ = lax.optimization_barrier((up_total, down_part))
-    up_part = over_z(up_total)
-    up_got = swap(up_part, "x")
-
+    up_early, *up_late = core_sum(up_keep.reshape(shape), up_send.reshape(shape), cut_up, x)
+
+    down_late = late_sum(*down_late, (up_keep,))
     d_middle, d_branch, d_branch_rel, d_att, sums_two = run_kernel(
         middle_back_kernel,
         [spot] + in_vmem(d_upper, tokens, grad_out, branch, mods) + in_place(ups + firsts),
@@ -746,6 +793,8 @@
         ]
         + [vmem(8, width, dtype=F32)] * 3
         + [sems(64)],
+        ordered_after=[down_late[1]],
+        us=33,
     )
     merge_keep, merge_send = pair_grads(d_branch_rel.reshape(2, 8 * span, rows), attended)
     shape = (2, 4, span, width)
@@ -753,20 +802,27 @@
     merge_got = swap(merge_send.reshape(shape), "c")
     merge_total = over_y([add_low(merge_keep[i], merge_got[i]) for i in range(2)])
 
+    down_total = jnp.concatenate(
+        [over_y(down_early), after(over_y(down_late), d_middle)], axis=-1
+    )
     d_qkv, d_qkv_rel = run_kernel(
         attend_back_kernel,
         [spot] + in_vmem(qkv, d_att),
         [((rows, 3 * width), BF16), ((2, 8, 3, span, rows), BF16)],
         [vmem(16, span, rows, dtype=F32)] * 3,
-    )
-    attend_keep, attend_send = pair_grads(d_qkv_rel.reshape(2, 24 * span, rows), h1)
+        ordered_after=[up_early[1], up_late[1], down_total],
+        us=26,
+    )
+    up_late = late_sum(*up_late, (d_qkv,))
+    attend_keep, attend_send = pair_grads(
+        d_qkv_rel.reshape(2, 24 * span, rows), h1, [up_late[1]]
+    )
     cut_attend = lambda v: (v[:, :, 0], v[:, :, 1], v[:, :, 2])
     shape = (2, 4, 3, span, width)
-    early, late = split_sum(attend_keep.reshape(shape), attend_send.reshape(shape), cut_attend, x)
-    first_total = jnp.concatenate([over_y(early), merge_total, over_y(late)], axis=2)
-    first_total, _ = lax.optimization_barrier((first_total, up_part))
-    first_part = over_z(first_total).reshape(span, 3, width).transpose(1, 0, 2)
-    first_got = swap(first_part, "x")
+    first_early, *first_late = core_sum(
+        attend_keep.reshape(shape), attend_send.reshape(shape), cut_attend, x
+    )
+    down_part = over_z(down_total)
 
     input_grad, sums_one = run_kernel(
         input_back_kernel,
@@ -775,7 +831,10 @@
         [vmem(48, span, width), vmem(rows, width, dtype=F32)]
         + [vmem(8, width, dtype=F32)] * 2
         + [sems(48)],
-    )
+        ordered_after=[attend_keep],
+        us=22,
+    )
+    up_total = jnp.concatenate([over_y(up_early), after(over_y(up_late), input_grad)], axis=1)
     block_out, sums_out = run_kernel(
         output_kernel,
         [spot] + in_vmem(act, tokens, branch, grad_out, mods) + in_place(downs),
@@ -786,12 +845,20 @@
             vmem(8, width, dtype=F32),
             sems(48),
         ],
-    )
+        ordered_after=[up_total, first_early[1], first_late[1], down_part],
+        us=21,
+    )
+    first_late = late_sum(*first_late, (block_out,))
+    up_part = over_z(after(up_total, down_part))
+    first_total = jnp.concatenate([over_y(first_early), merge_total, over_y(first_late)], axis=2)
+    first_part = over_z(after(first_total, up_part))
+    first_part = first_part.reshape(span, 3, width).transpose(1, 0, 2)
+    down_got, up_got, first_got = swap(down_part, "x"), swap(up_part, "x"), swap(first_part, "x")
 
     d_vector = jnp.concatenate([sums_one[:2], sums_two[:3], sums_out[:1]]).reshape(6 * width)
-    clip_pick = (jnp.arange(clips) == clip_index).astype(F32)
-    d_mod = sum_all(clip_pick[:, None] * d_vector[None, :])
-    d_mod = lax.dynamic_slice_in_dim(d_mod, block * mod_span, mod_span, 1)
+    d_mod = sum_plane(after(d_vector, up_part).reshape(4, 4, mod_span))
+    d_mod = lax.dynamic_index_in_dim(d_mod, y * 2 + c, 1, keepdims=False)
+    d_mod = turn_z(d_mod, z)
     grad_mod = contract_rows(d_mod, cond_act.astype(F32), HIGHEST)
     d_cond_part = jnp.dot(
         d_mod, own_low[2].astype(F32), precision=HIGHEST, preferred_element_type=F32

time: 772 us -> 635 us (0.82)
  waiting for transfers between devices: 359 us -> 194 us
  other arithmetic: 58.5 us -> 72.3 us
  local copies, waits for them, and re-layouts: 32.3 us -> 41.9 us
    ppermute x53, waiting for transfers between devices: 276 us -> 116 us  [swap(): return lax.ppermute(value, axis, [(0, 1), (1, 0)])]
    convert_element_type x17, other arithmetic: 26.5 us -> 43.3 us  [add_low(): return total.astype(BF16)]
    ppermute x0 -> x6, starting transfers between devices: none -> 11 us  [turn_z(): got = lax.ppermute(entry, 'z', [(i, (i + step) % 4) for i in range(4)])]
    select_n x12 -> x6, other arithmetic: 11 us -> 2.89 us  [the longest x3 2.78 us: own_block(): return jnp.where(flag, jnp.concatenate([early, near_late], axis=axis), got)]
    pallas_call x8 -> x9, Pallas kernels: 196 us -> 199 us  [run_kernel(): pl.pallas_call(kernel, out_shape=[jax.ShapeDtypeStruct(shape, dtype) for...]
  transfers between devices with their start and end apart: 67 -> 69, of which waited for: 38 -> 25; matrix products, arithmetic and copies ran while one was open for 10% -> 16% of each run, Pallas kernels for 12% -> 34%
where the time goes in v2:
time: 635 us; the launch traced here: 630 us
  Pallas kernels  224 us (35%)
  waiting for transfers between devices  194 us (31%)
  other arithmetic  72.3 us (11%)
  starting transfers between devices  68.3 us (11%)
  local copies, waits for them, and re-layouts  41.9 us (7%)
  between operations  20.7 us (3%)
  matrix products  9.41 us (1%)
    pallas_call x9, Pallas kernels, run_kernel(): pl.pallas_call(kernel, out_shape=[jax.ShapeDtypeStruct(shape, dtype) for...  199 us
    ppermute x53, waiting for transfers between devices, swap(): return lax.ppermute(value, axis, [(0, 1), (1, 0)])  116 us
    ppermute x53, starting transfers between devices, swap(): return lax.ppermute(value, axis, [(0, 1), (1, 0)])  49.3 us
    convert_element_type x17, other arithmetic, add_low(): return total.astype(BF16)  43.3 us
    all_gather x3, waiting for transfers between devices, gather_near(): lax.all_gather(mine.reshape(-1, mine.shape[-1]), 'z', axis=0, tiled=False)  36.3 us
    unnamed x7, waiting for transfers between devices  22.9 us
    pallas_call x3, Pallas kernels, pair_grads(): pl.pallas_call(kernel, grid=grid, out_shape=[jax.ShapeDtypeStruct((rows,...  16.7 us
    convert_element_type x4, other arithmetic, on_grid(): copy_list.append(fresh.astype(BF16))  15 us
  transfers between devices with their start and end apart: 69, of which 25 were waited for; matrix products, arithmetic and copies ran while one was open for 16% of the time, Pallas kernels for 34%

profile of v2, /device:TPU:0, one launch (start us, length us, event | category | flops | bytes accessed | tf_op | source)
XLA Modules:
  0.0 630.3 jit_solution(9518306150804343839)
XLA Ops:
  8.8 3.0 collective-permute-start.11
  15.9 7.3 %collective-permute-done.11 = bf16[3,72,1152]{2,1,0:T(8,128)(2,1)S(1)} collective-permute-done((bf16[3,72,1152]{2,1,0:T(8,128)(2,1)S(1)}, bf16[3,72,1152]{2,1,0:T(8,128)(2,1)S(1)}, u32[]{:S(2)}, u32[]{:S(2)}) %collective-permute-start.11) | collective-permute-done | bytes 497696 | tf_op jit(solution)/shard_map/ppermute | solution.py:557
  34.7 3.1 collective-permute-done.3
  37.8 2.6 collective-permute-start.4
  44.3 2.7 collective-permute-start.5
  47.0 3.7 collective-permute-start.6
  55.0 4.5 collective-permute-done.19
  71.1 3.1 copy.93
  80.4 34.8 %all-gather.10.cloned.1.call-done = bf16[832,1152]{1,0:T(8,128)(2,1)} async-done(((bf16[208,1152]{1,0:T(8,128)(2,1)}), bf16[832,1152]{1,0:T(8,128)(2,1)}) %all-gather.10.cloned.1.call-update) | async-done | bytes 1916944 | tf_op jit(solution)/shard_map/all_gather | solution.py:610
  116.6 4.1 collective-permute-done.13
  129.6 31.3 %collective-permute-done.22.refs_4_.refs_8_ = bf16[4,208,1152]{2,1,0:T(8,128)(2,1)} collective-permute-done((bf16[4,208,1152]{2,1,0:T(8,128)(2,1)}, bf16[4,208,1152]{2,1,0:T(8,128)(2,1)}, u32[]{:S(2)}, u32[]{:S(2)}) %collective-permute-start.22) | collective-permute-done | bytes 1916960 | tf_op jit(solution)/shard_map/ppermute | solution.py:557
  163.9 3.7 shard_map.493
  167.6 3.0 copy.94.refs_5_.refs_6_.refs_16_.refs_7_
  170.6 3.0 copy.95.refs_9_.refs_10_.refs_20_.refs_11_
  175.3 5.9 collective-permute-done.23.refs_5_.refs_9_
  181.7 16.7 %shard_map.490 = (bf16[512,1152]{1,0:T(8,128)(2,1)}, bf16[48,72,512]{2,1,0:T(8,128)(2,1)}) custom-call(s32[8]{0:T(128)} %stack.45.refs_0_.place_ref, bf16[512,1152]{1,0:T(8,128)(2,1)} %bitcast.581, f32[8,1152]{1,0:T(8,128)} %concatenate.64.refs_2_.refs_3_.refs_5_.refs_4_, bf16[4,3,72,1152]{3,2,1,0:T(8,128)(2,1)} %bitcast.566, ...), custom_call_target="tpu_custom_call" | custom-call | flops 108000002048 | bytes 324000000 | tf_op jit(solution)/shard_map/pallas_call | solution.py:118
  198.4 20.8 %shard_map.491 = (bf16[512,1152]{1,0:T(8,128)(2,1)}, f32[512,1152]{1,0:T(8,128)}, bf16[512,1152]{1,0:T(8,128)(2,1)}) custom-call(s32[8]{0:T(128)} %stack.45.refs_0_.place_ref, bf16[48,72,512]{2,1,0:T(8,128)(2,1)} %get-tuple-element.76.refs_1_, bf16[512,1152]{1,0:T(8,128)(2,1)} %bitcast.582, f32[8,1152]{1,0:T(8,128)} %concatenate.64.refs_2_.refs_3_.refs_5_.refs_4_, ...), custom_call_target="tpu_custom_call" | custom-call | flops 120000004096 | bytes 360000000 | tf_op jit(solution)/shard_map/pallas_call | solution.py:118
  222.7 27.3 %shard_map.492 = (bf16[512,4608]{1,0:T(8,128)(2,1)}, bf16[512,4608]{1,0:T(8,128)(2,1)}) custom-call(s32[8]{0:T(128)} %stack.45.refs_0_.place_ref, bf16[512,1152]{1,0:T(8,128)(2,1)} %get-tuple-element.77.refs_1_.right_ref, bf16[4,208,1152]{2,1,0:T(8,128)(2,1)} %bitcast.42.refs_2_.refs_6_, bf16[4,80,1152]{2,1,0:T(8,128)(2,1)} %collective-permute-done.21.refs_3_.refs_7_, ...), custom_call_target="tpu_custom_call" | custom-call | flops 161999994880 | bytes 486000000 | tf_op jit(solution)/shard_map/pallas_call | solution.py:118
  252.4 9.2 %shard_map.494 = (bf16[576,4608]{1,0:T(8,128)(2,1)S(1)}, bf16[576,4608]{1,0:T(8,128)(2,1)}) custom-call(bf16[2,576,512]{2,1,0:T(8,128)(2,1)S(1)} %bitcast.556, bf16[2,576,512]{2,1,0:T(8,128)(2,1)S(1)} %bitcast.557, bf16[512,4608]{1,0:T(8,128)(2,1)S(1)} %copy-done.8, bf16[4,72,1280]{2,1,0:T(8,128)(2,1)} %collective-permute-done.30.rest_0_.refs_6_.refs_9_), custom_call_target="tpu_custom_call" | custom-call | flops 27179089920 | bytes 81537272 | tf_op jit(solution)/shard_map/pallas_call | solution.py:499
  264.5 17.8 %collective-permute-done.28.refs_4_.refs_7_ = bf16[4,72,1280]{2,1,0:T(8,128)(2,1)S(1)} collective-permute-done((bf16[4,72,1280]{2,1,0:T(8,128)(2,1)S(1)}, bf16[4,72,1280]{2,1,0:T(8,128)(2,1)S(1)}, u32[]{:S(2)}, u32[]{:S(2)}) %collective-permute-start.28) | collective-permute-done | bytes 737312 | tf_op jit(solution)/shard_map/ppermute | solution.py:557
  285.9 2.7 add_convert_fusion
  291.5 28.0 %shard_map.495 = (bf16[512,4608]{1,0:T(8,128)(2,1)}, bf16[4608,512]{1,0:T(8,128)(2,1)}) custom-call(s32[8]{0:T(128)} %stack.45.refs_0_.place_ref, bf16[512,1152]{1,0:T(8,128)(2,1)} %get-tuple-element.83.refs_1_, bf16[512,4608]{1,0:T(8,128)(2,1)} %get-tuple-element.84.refs_2_, bf16[4,72,3328]{2,1,0:T(8,128)(2,1)} %bitcast.41.refs_11_.refs_3_.refs_6_, ...), custom_call_target="tpu_custom_call" | custom-call | flops 167999995904 | bytes 504000000 | tf_op jit(solution)/shard_map/pallas_call | solution.py:118
  319.6 2.3 copy-done.10
  321.9 8.9 %shard_map.496 = (bf16[8,288,1152]{2,1,0:T(8,128)(2,1)S(1)}, bf16[8,288,1152]{2,1,0:T(8,128)(2,1)}) custom-call(s32[8]{0:T(128)S(1)} %copy-done.3, bf16[4608,512]{1,0:T(8,128)(2,1)S(1)} %copy-done.10, bf16[4608,512]{1,0:T(8,128)(2,1)S(1)} %copy-done.10, bf16[512,1152]{1,0:T(8,128)(2,1)S(1)} %copy-done.11), custom_call_target="tpu_custom_call" | custom-call | flops 54000001024 | bytes 162000000 | tf_op jit(solution)/shard_map/pallas_call | solution.py:532
  330.8 2.4 copy-done
  333.2 3.8 fusion
  339.7 33.1 %shard_map.497 = (f32[512,1152]{1,0:T(8,128)}, bf16[512,1152]{1,0:T(8,128)(2,1)}, bf16[2,8,72,512]{3,2,1,0:T(8,128)(2,1)}, bf16[16,72,512]{2,1,0:T(8,128)(2,1)}, f32[8,1152]{1,0:T(8,128)}) custom-call(s32[8]{0:T(128)} %stack.45.refs_0_.place_ref, bf16[512,4608]{1,0:T(8,128)(2,1)} %get-tuple-element.91.refs_1_, bf16[512,1152]{1,0:T(8,128)(2,1)} %bitcast.583, ...), custom_call_target="tpu_custom_call" | custom-call | flops 198000001024 | bytes 594000000 | tf_op jit(solution)/shard_map/pallas_call | solution.py:118
  383.8 2.9 fusion.31.refs_3_
  387.2 5.4 add_convert_fusion.1
  394.1 26.3 %shard_map.498 = (bf16[512,3456]{1,0:T(8,128)(2,1)}, bf16[2,8,3,72,512]{4,3,2,1,0:T(8,128)(2,1)}) custom-call(s32[8]{0:T(128)} %stack.45.refs_0_.place_ref, bf16[48,72,512]{2,1,0:T(8,128)(2,1)} %get-tuple-element.76.refs_1_, bf16[16,72,512]{2,1,0:T(8,128)(2,1)} %get-tuple-element.93.refs_2_, bf16[4,128,1152]{2,1,0:T(8,128)(2,1)} %fusion.31.refs_3_, ...), custom_call_target="tpu_custom_call" | custom-call | flops 155999993856 | bytes 468000000 | tf_op jit(solution)/shard_map/pallas_call | solution.py:118
  420.3 4.8 collective-permute-done.37
  425.1 3.6 fusion.1
  432.5 5.6 shard_map.499
  438.1 2.5 copy.103
  441.2 22.1 %shard_map.500 = (bf16[512,1152]{1,0:T(8,128)(2,1)}, f32[8,1152]{1,0:T(8,128)}) custom-call(s32[8]{0:T(128)} %stack.45.refs_0_.place_ref, bf16[512,3456]{1,0:T(8,128)(2,1)} %get-tuple-element.96.refs_1_, bf16[512,1152]{1,0:T(8,128)(2,1)} %bitcast.584, f32[512,1152]{1,0:T(8,128)} %get-tuple-element.94.refs_3_, ...), custom_call_target="tpu_custom_call" | custom-call | flops 131999997952 | bytes 396000000 | tf_op jit(solution)/shard_map/pallas_call | solution.py:118
  469.6 4.9 add_convert_fusion.4
  474.5 20.7 %shard_map.501 = (bf16[512,1152]{1,0:T(8,128)(2,1)}, f32[8,1152]{1,0:T(8,128)}) custom-call(s32[8]{0:T(128)} %stack.45.refs_0_.place_ref, bf16[512,4608]{1,0:T(8,128)(2,1)} %get-tuple-element.79.right_ref.refs_1_, bf16[512,1152]{1,0:T(8,128)(2,1)} %bitcast.585, f32[512,1152]{1,0:T(8,128)} %get-tuple-element.80.refs_4_.refs_3_, bf16[512,1152]{1,0:T(8,128)(2,1)} %bitcast.588, ...), custom_call_target="tpu_custom_call" | custom-call | flops 125999996928 | bytes 378000000 | tf_op jit(solution)/shard_map/pallas_call | solution.py:118
  496.1 10.6 %reduce-scatter.8.cloned.1.call-done = bf16[208,1152]{1,0:T(8,128)(2,1)} async-done(((bf16[832,1152]{1,0:T(8,128)(2,1)}), bf16[208,1152]{1,0:T(8,128)(2,1)}) %reduce-scatter.8.cloned.1.call-update) | async-done | bytes 479248 | tf_op jit(solution)/shard_map/reduce_scatter | solution.py:642
  513.5 2.4 collective-permute-done.46
  520.6 2.6 add_convert_fusion.14
  528.2 13.7 %collective-permute-done.58 = bf16[2,4,72,1152]{3,2,1,0:T(8,128)(2,1)} collective-permute-done((bf16[2,4,72,1152]{3,2,1,0:T(8,128)(2,1)}, bf16[2,4,72,1152]{3,2,1,0:T(8,128)(2,1)}, u32[]{:S(2)}, u32[]{:S(2)}) %collective-permute-start.58) | collective-permute-done | bytes 1327136 | tf_op jit(solution)/shard_map/ppermute | solution.py:557
  544.7 6.3 %collective-permute-done.62 = bf16[72,3328]{1,0:T(8,128)(2,1)} collective-permute-done((bf16[72,3328]{1,0:T(8,128)(2,1)}, bf16[72,3328]{1,0:T(8,128)(2,1)}, u32[]{:S(2)}, u32[]{:S(2)}) %collective-permute-start.62) | collective-permute-done | bytes 479264 | tf_op jit(solution)/shard_map/ppermute | solution.py:557
  563.2 5.5 fusion.46
  571.6 5.6 convert_bitcast_fusion
  579.6 22.8 %reduce-scatter.10.cloned.1.call-done = bf16[72,3456]{1,0:T(8,128)(2,1)} async-done(((bf16[288,3456]{1,0:T(8,128)(2,1)}), bf16[72,3456]{1,0:T(8,128)(2,1)}) %reduce-scatter.10.cloned.1.call-update) | async-done | bytes 497680
  605.8 5.3 fusion.45
  611.1 6.1 collective-permute-done.60
  620.1 2.9 fusion.49
  (363 shorter events, 138.4 us)
Async XLA Ops:
  7.2 63.9 %all-gather.6.cloned.1.call-start = ((), (), s32[]{:S(2)}) async-start(), calls=%async_computation.3 | async-start | bytes 2488320 | tf_op jit(solution)/shard_map/all_gather | solution.py:610
  8.8 14.4 %collective-permute-start.11 = (bf16[3,72,1152]{2,1,0:T(8,128)(2,1)S(1)}, bf16[3,72,1152]{2,1,0:T(8,128)(2,1)S(1)}, u32[]{:S(2)}, u32[]{:S(2)}) collective-permute-start(bf16[3,72,1152]{2,1,0:T(8,128)(2,1)S(1)} %pad_maximum_fusion.11), channel_id=1, source_target_pairs={{0,1},{1,0},{2,3},{3,2},{4,5},{5,4},{6,7},{7,6},{8,9},{9,8},{10,11... | collective-permute-start | bytes 1493000 | tf_op jit(solution)/shard_map/ppermute | solution.py:557
  14.4 9.7 %collective-permute-start = (f32[2,4,1152]{2,1,0:T(4,128)S(1)}, f32[2,4,1152]{2,1,0:T(4,128)S(1)}, u32[]{:S(2)}, u32[]{:S(2)}) collective-permute-start(f32[2,4,1152]{2,1,0:T(4,128)S(1)} %dynamic_update_slice.38), channel_id=1, source_target_pairs={{0,2},{2,0},{1,3},{3,1},{4,6},{6,4},{5,7},{7,5},{8,10},{10,8},{9,1... | collective-permute-start | bytes 110600 | tf_op jit(solution)/shard_map/ppermute | solution.py:557
  24.1 91.0 %all-gather.10.cloned.1.call-start = ((), (), s32[]{:S(2)}) async-start(), calls=%async_computation.7 | async-start | bytes 2396160 | tf_op jit(solution)/shard_map/all_gather | solution.py:610
  50.7 8.8 %collective-permute-start.19 = (bf16[208,1152]{1,0:T(8,128)(2,1)S(1)}, bf16[208,1152]{1,0:T(8,128)(2,1)S(1)}, u32[]{:S(2)}, u32[]{:S(2)}) collective-permute-start(bf16[208,1152]{1,0:T(8,128)(2,1)S(1)} %pad_maximum_fusion.8), channel_id=1, source_target_pairs={{0,1},{1,0},{2,3},{3,2},{4,5},{5,4},{6,7},{7,6},{8,9},{9,8},{10,11... | collective-permute-start | bytes 1437704 | tf_op jit(solution)/shard_map/ppermute | solution.py:557
  60.6 107.0 %all-gather.8.cloned.1.call-start = ((), (), s32[]{:S(2)}) async-start(), calls=%async_computation.6 | async-start | bytes 2396160 | tf_op jit(solution)/shard_map/all_gather | solution.py:610
  74.2 46.5 %collective-permute-start.13 = (bf16[4,3,72,1152]{3,2,0,1:T(8,128)(2,1)}, bf16[4,3,72,1152]{3,2,0,1:T(8,128)(2,1)}, u32[]{:S(2)}, u32[]{:S(2)}) collective-permute-start(bf16[4,3,72,1152]{3,2,0,1:T(8,128)(2,1)} %copy.93), channel_id=1, source_target_pairs={{0,4},{4,0},{1,5},{5,1},{2,6},{6,2},{3,7},{7,3},{8,12},{12,8},{9,1... | collective-permute-start | bytes 5971976 | tf_op jit(solution)/shard_map/ppermute | solution.py:557
  77.5 46.7 %collective-permute-start.20 = (bf16[72,3328]{1,0:T(8,128)(2,1)}, bf16[72,3328]{1,0:T(8,128)(2,1)S(1)}, u32[]{:S(2)}, u32[]{:S(2)}) collective-permute-start(bf16[72,3328]{1,0:T(8,128)(2,1)} %pad_maximum_fusion.6), channel_id=1, source_target_pairs={{0,1},{1,0},{2,3},{3,2},{4,5},{5,4},{6,7},{7,6},{8,9},{9,8},{10,11... | collective-permute-start | bytes 1437704 | tf_op jit(solution)/shard_map/ppermute | solution.py:557
  79.8 49.2 %collective-permute-start.12 = (bf16[4,72,1152]{2,1,0:T(8,128)(2,1)}, bf16[4,72,1152]{2,1,0:T(8,128)(2,1)}, u32[]{:S(2)}, u32[]{:S(2)}) collective-permute-start(bf16[4,72,1152]{2,1,0:T(8,128)(2,1)} %slice_bitcast_fusion.9), channel_id=1, source_target_pairs={{0,1},{1,0},{2,3},{3,2},{4,5},{5,4},{6,7},{7,6},{8,9},{9,8},{10,11... | collective-permute-start | bytes 1990664 | tf_op jit(solution)/shard_map/ppermute | solution.py:557
  115.1 45.8 %collective-permute-start.22 = (bf16[4,208,1152]{2,1,0:T(8,128)(2,1)}, bf16[4,208,1152]{2,1,0:T(8,128)(2,1)}, u32[]{:S(2)}, u32[]{:S(2)}) collective-permute-start(bf16[4,208,1152]{2,1,0:T(8,128)(2,1)} %bitcast.42.refs_2_.refs_6_), channel_id=1, source_target_pairs={{0,4},{4,0},{1,5},{5,1},{2,6},{6,2},{3,7},{7,3},{8,12},{12,8},{9,1... | collective-permute-start | bytes 5750792 | tf_op jit(solution)/shard_map/ppermute | solution.py:557
  120.7 42.9 %collective-permute-start.17 = (bf16[4,3,72,1152]{3,2,0,1:T(8,128)(2,1)}, bf16[4,3,72,1152]{3,2,0,1:T(8,128)(2,1)}, u32[]{:S(2)}, u32[]{:S(2)}) collective-permute-start(bf16[4,3,72,1152]{3,2,0,1:T(8,128)(2,1)} %collective-permute-done.13), channel_id=1, source_target_pairs={{0,2},{2,0},{1,3},{3,1},{4,6},{6,4},{5,7},{7,5},{8,10},{10,8},{9,1... | collective-permute-start | bytes 5971976 | tf_op jit(solution)/shard_map/ppermute | solution.py:557
  122.7 39.4 %collective-permute-start.14 = (bf16[4,72,1152]{2,1,0:T(8,128)(2,1)}, bf16[4,72,1152]{2,1,0:T(8,128)(2,1)}, u32[]{:S(2)}, u32[]{:S(2)}) collective-permute-start(bf16[4,72,1152]{2,1,0:T(8,128)(2,1)} %slice_bitcast_fusion.8), channel_id=1, source_target_pairs={{0,1},{1,0},{2,3},{3,2},{4,5},{5,4},{6,7},{7,6},{8,9},{9,8},{10,11... | collective-permute-start | bytes 1990664 | tf_op jit(solution)/shard_map/ppermute | solution.py:557
  125.1 342.2 %reduce-scatter.6.cloned.1.call-start = ((), (), s32[]{:S(2)}) async-start(), calls=%async_computation.4 | async-start | bytes 2396160 | tf_op jit(solution)/shard_map/reduce_scatter | solution.py:642
  127.6 47.7 %collective-permute-start.15 = (bf16[4,3,72,1152]{3,2,1,0:T(8,128)(2,1)S(1)}, bf16[4,3,72,1152]{3,2,1,0:T(8,128)(2,1)}, u32[]{:S(2)}, u32[]{:S(2)}) collective-permute-start(bf16[4,3,72,1152]{3,2,1,0:T(8,128)(2,1)S(1)} %bitcast.571), channel_id=1, source_target_pairs={{0,2},{2,0},{1,3},{3,1},{4,6},{6,4},{5,7},{7,5},{8,10},{10,8},{9,1... | collective-permute-start | bytes 5971976 | tf_op jit(solution)/shard_map/ppermute | solution.py:557
  129.0 44.6 %collective-permute-start.21 = (bf16[4,80,1152]{2,1,0:T(8,128)(2,1)S(1)}, bf16[4,80,1152]{2,1,0:T(8,128)(2,1)}, u32[]{:S(2)}, u32[]{:S(2)}) collective-permute-start(bf16[4,80,1152]{2,1,0:T(8,128)(2,1)S(1)} %slice.381), channel_id=1, source_target_pairs={{0,1},{1,0},{2,3},{3,2},{4,5},{5,4},{6,7},{7,6},{8,9},{9,8},{10,11... | collective-permute-start | bytes 2211848 | tf_op jit(solution)/shard_map/ppermute | solution.py:557
  160.9 12.9 %collective-permute-start.16 = (bf16[4,72,1152]{2,1,0:T(8,128)(2,1)}, bf16[4,72,1152]{2,1,0:T(8,128)(2,1)}, u32[]{:S(2)}, u32[]{:S(2)}) collective-permute-start(bf16[4,72,1152]{2,1,0:T(8,128)(2,1)} %collective-permute-done.12.refs_4_.refs_5_.refs_15_.refs_6_), channel_id=1, source_target_pairs={{0,2},{2,0},{1,3},{3,1},{4,6},{6,4},{5,7},{7,5},{8,10},{10,8},{9,1... | collective-permute-start | bytes 1990664 | tf_op jit(solution)/shard_map/ppermute | solution.py:557
  162.1 19.1 %collective-permute-start.23 = (bf16[4,80,1152]{2,1,0:T(8,128)(2,1)S(1)}, bf16[4,80,1152]{2,1,0:T(8,128)(2,1)}, u32[]{:S(2)}, u32[]{:S(2)}) collective-permute-start(bf16[4,80,1152]{2,1,0:T(8,128)(2,1)S(1)} %slice.382), channel_id=1, source_target_pairs={{0,1},{1,0},{2,3},{3,2},{4,5},{5,4},{6,7},{7,6},{8,9},{9,8},{10,11... | collective-permute-start | bytes 2211848 | tf_op jit(solution)/shard_map/ppermute | solution.py:557
  163.7 17.5 %collective-permute-start.18 = (bf16[4,72,1152]{2,1,0:T(8,128)(2,1)}, bf16[4,72,1152]{2,1,0:T(8,128)(2,1)}, u32[]{:S(2)}, u32[]{:S(2)}) collective-permute-start(bf16[4,72,1152]{2,1,0:T(8,128)(2,1)} %collective-permute-done.14.refs_6_.refs_7_.refs_17_.refs_8_), channel_id=1, source_target_pairs={{0,2},{2,0},{1,3},{3,1},{4,6},{6,4},{5,7},{7,5},{8,10},{10,8},{9,1... | collective-permute-start | bytes 1990664 | tf_op jit(solution)/shard_map/ppermute | solution.py:557
  173.6 49.2 %collective-permute-start.24 = (bf16[4,208,1152]{2,1,0:T(8,128)(2,1)}, bf16[4,208,1152]{2,1,0:T(8,128)(2,1)}, u32[]{:S(2)}, u32[]{:S(2)}) collective-permute-start(bf16[4,208,1152]{2,1,0:T(8,128)(2,1)} %bitcast.42.refs_2_.refs_6_), channel_id=1, source_target_pairs={{0,2},{2,0},{1,3},{3,1},{4,6},{6,4},{5,7},{7,5},{8,10},{10,8},{9,1... | collective-permute-start | bytes 5750792 | tf_op jit(solution)/shard_map/ppermute | solution.py:557
  173.8 45.3 %collective-permute-start.29 = (bf16[4,72,3328]{2,1,0:T(8,128)(2,1)}, bf16[4,72,3328]{2,1,0:T(8,128)(2,1)}, u32[]{:S(2)}, u32[]{:S(2)}) collective-permute-start(bf16[4,72,3328]{2,1,0:T(8,128)(2,1)} %bitcast.41.refs_11_.refs_3_.refs_6_), channel_id=1, source_target_pairs={{0,4},{4,0},{1,5},{5,1},{2,6},{6,2},{3,7},{7,3},{8,12},{12,8},{9,1... | collective-permute-start | bytes 5750792 | tf_op jit(solution)/shard_map/ppermute | solution.py:557
  175.3 47.4 %collective-permute-start.25 = (bf16[4,80,1152]{2,1,0:T(8,128)(2,1)}, bf16[4,80,1152]{2,1,0:T(8,128)(2,1)}, u32[]{:S(2)}, u32[]{:S(2)}) collective-permute-start(bf16[4,80,1152]{2,1,0:T(8,128)(2,1)} %collective-permute-done.21.refs_3_.refs_7_), channel_id=1, source_target_pairs={{0,2},{2,0},{1,3},{3,1},{4,6},{6,4},{5,7},{7,5},{8,10},{10,8},{9,1... | collective-permute-start | bytes 2211848 | tf_op jit(solution)/shard_map/ppermute | solution.py:557
  181.2 41.6 %collective-permute-start.26 = (bf16[4,208,1152]{2,1,0:T(8,128)(2,1)}, bf16[4,208,1152]{2,1,0:T(8,128)(2,1)}, u32[]{:S(2)}, u32[]{:S(2)}) collective-permute-start(bf16[4,208,1152]{2,1,0:T(8,128)(2,1)} %collective-permute-done.22.refs_4_.refs_8_), channel_id=1, source_target_pairs={{0,2},{2,0},{1,3},{3,1},{4,6},{6,4},{5,7},{7,5},{8,10},{10,8},{9,1... | collective-permute-start | bytes 5750792 | tf_op jit(solution)/shard_map/ppermute | solution.py:557
  181.2 41.6 %collective-permute-start.27 = (bf16[4,80,1152]{2,1,0:T(8,128)(2,1)}, bf16[4,80,1152]{2,1,0:T(8,128)(2,1)}, u32[]{:S(2)}, u32[]{:S(2)}) collective-permute-start(bf16[4,80,1152]{2,1,0:T(8,128)(2,1)} %collective-permute-done.23.refs_5_.refs_9_), channel_id=1, source_target_pairs={{0,2},{2,0},{1,3},{3,1},{4,6},{6,4},{5,7},{7,5},{8,10},{10,8},{9,1... | collective-permute-start | bytes 2211848 | tf_op jit(solution)/shard_map/ppermute | solution.py:557
  221.2 28.8 %collective-permute-start.30 = (bf16[4,72,1280]{2,1,0:T(8,128)(2,1)}, bf16[4,72,1280]{2,1,0:T(8,128)(2,1)}, u32[]{:S(2)}, u32[]{:S(2)}) collective-permute-start(bf16[4,72,1280]{2,1,0:T(8,128)(2,1)} %slice.308), channel_id=1, source_target_pairs={{0,1},{1,0},{2,3},{3,2},{4,5},{5,4},{6,7},{7,6},{8,9},{9,8},{10,11... | collective-permute-start | bytes 2211848 | tf_op jit(solution)/shard_map/ppermute | solution.py:557
  261.6 21.2 %collective-permute-start.35 = (bf16[2,4,72,4608]{3,2,1,0:T(8,128)(2,1)}, bf16[2,4,72,4608]{3,2,1,0:T(8,128)(2,1)S(1)}, u32[]{:S(2)}, u32[]{:S(2)}) collective-permute-start(bf16[2,4,72,4608]{3,2,1,0:T(8,128)(2,1)} %bitcast.580), channel_id=1, source_target_pairs={{0,2},{2,0},{1,3},{3,1},{4,6},{6,4},{5,7},{7,5},{8,10},{10,8},{9,1... | collective-permute-start | bytes 15925256 | tf_op jit(solution)/shard_map/ppermute | solution.py:557
  263.3 19.0 %collective-permute-start.28 = (bf16[4,72,1280]{2,1,0:T(8,128)(2,1)S(1)}, bf16[4,72,1280]{2,1,0:T(8,128)(2,1)S(1)}, u32[]{:S(2)}, u32[]{:S(2)}) collective-permute-start(bf16[4,72,1280]{2,1,0:T(8,128)(2,1)S(1)} %slice.383), channel_id=1, source_target_pairs={{0,1},{1,0},{2,3},{3,2},{4,5},{5,4},{6,7},{7,6},{8,9},{9,8},{10,11... | collective-permute-start | bytes 2211848 | tf_op jit(solution)/shard_map/ppermute | solution.py:557
  264.0 25.4 %collective-permute-start.31 = (bf16[4,72,3328]{2,1,0:T(8,128)(2,1)}, bf16[4,72,3328]{2,1,0:T(8,128)(2,1)S(1)}, u32[]{:S(2)}, u32[]{:S(2)}) collective-permute-start(bf16[4,72,3328]{2,1,0:T(8,128)(2,1)} %bitcast.41.refs_11_.refs_3_.refs_6_), channel_id=1, source_target_pairs={{0,2},{2,0},{1,3},{3,1},{4,6},{6,4},{5,7},{7,5},{8,10},{10,8},{9,1... | collective-permute-start | bytes 5750792 | tf_op jit(solution)/shard_map/ppermute | solution.py:557
  264.2 25.1 %collective-permute-start.33 = (bf16[4,72,3328]{2,1,0:T(8,128)(2,1)}, bf16[4,72,3328]{2,1,0:T(8,128)(2,1)S(1)}, u32[]{:S(2)}, u32[]{:S(2)}) collective-permute-start(bf16[4,72,3328]{2,1,0:T(8,128)(2,1)} %collective-permute-done.29.refs_5_.refs_8_), channel_id=1, source_target_pairs={{0,2},{2,0},{1,3},{3,1},{4,6},{6,4},{5,7},{7,5},{8,10},{10,8},{9,1... | collective-permute-start | bytes 5750792 | tf_op jit(solution)/shard_map/ppermute | solution.py:557
  284.5 48.7 %collective-permute-start.40 = (bf16[4,72,2048]{2,1,0:T(8,128)(2,1)}, bf16[4,72,2048]{2,1,0:T(8,128)(2,1)}, u32[]{:S(2)}, u32[]{:S(2)}) collective-permute-start(bf16[4,72,2048]{2,1,0:T(8,128)(2,1)} %fusion.29.refs_11_), channel_id=1, source_target_pairs={{0,4},{4,0},{1,5},{5,1},{2,6},{6,2},{3,7},{7,3},{8,12},{12,8},{9,1... | collective-permute-start | bytes 3538952 | tf_op jit(solution)/shard_map/ppermute | solution.py:557
  288.6 48.4 %collective-permute-start.39 = (bf16[2,4,72,1280]{3,2,1,0:T(8,128)(2,1)}, bf16[2,4,72,1280]{3,2,1,0:T(8,128)(2,1)}, u32[]{:S(2)}, u32[]{:S(2)}) collective-permute-start(bf16[2,4,72,1280]{3,2,1,0:T(8,128)(2,1)} %get-tuple-element.131.refs_12_), channel_id=1, source_target_pairs={{0,1},{1,0},{2,3},{3,2},{4,5},{5,4},{6,7},{7,6},{8,9},{9,8},{10,11... | collective-permute-start | bytes 4423688 | tf_op jit(solution)/shard_map/ppermute | solution.py:557
  333.2 50.5 %collective-permute-start.36 = (bf16[2,4,288,1152]{3,2,1,0:T(8,128)(2,1)}, bf16[2,4,288,1152]{3,2,1,0:T(8,128)(2,1)}, u32[]{:S(2)}, u32[]{:S(2)}) collective-permute-start(bf16[2,4,288,1152]{3,2,1,0:T(8,128)(2,1)} %bitcast.579), channel_id=1, source_target_pairs={{0,2},{2,0},{1,3},{3,1},{4,6},{6,4},{5,7},{7,5},{8,10},{10,8},{9,1... | collective-permute-start | bytes 15925256 | tf_op jit(solution)/shard_map/ppermute | solution.py:557
  339.2 38.5 %collective-permute-start.41 = (bf16[4,72,1280]{2,1,0:T(8,128)(2,1)}, bf16[4,72,1280]{2,1,0:T(8,128)(2,1)}, u32[]{:S(2)}, u32[]{:S(2)}) collective-permute-start(bf16[4,72,1280]{2,1,0:T(8,128)(2,1)} %fusion.39.refs_22_), channel_id=1, source_target_pairs={{0,4},{4,0},{1,5},{5,1},{2,6},{6,2},{3,7},{7,3},{8,12},{12,8},{9,1... | collective-permute-start | bytes 2211848 | tf_op jit(solution)/shard_map/ppermute | solution.py:557
  380.9 125.8 %reduce-scatter.8.cloned.1.call-start = ((), (), s32[]{:S(2)}) async-start(), calls=%async_computation.5 | async-start | bytes 2396160 | tf_op jit(solution)/shard_map/reduce_scatter | solution.py:642
  382.2 138.4 %collective-permute-start.57 = (bf16[4,72,1152]{2,1,0:T(8,128)(2,1)}, bf16[4,72,1152]{2,1,0:T(8,128)(2,1)}, u32[]{:S(2)}, u32[]{:S(2)}) collective-permute-start(bf16[4,72,1152]{2,1,0:T(8,128)(2,1)} %fusion.20), channel_id=1, source_target_pairs={{0,4},{4,0},{1,5},{5,1},{2,6},{6,2},{3,7},{7,3},{8,12},{12,8},{9,1... | collective-permute-start | bytes 1990664 | tf_op jit(solution)/shard_map/ppermute | solution.py:557
  386.7 38.4 %collective-permute-start.37 = (bf16[4,128,1152]{2,1,0:T(8,128)(2,1)}, bf16[4,128,1152]{2,1,0:T(8,128)(2,1)}, u32[]{:S(2)}, u32[]{:S(2)}) collective-permute-start(bf16[4,128,1152]{2,1,0:T(8,128)(2,1)} %fusion.31.refs_3_), channel_id=1, source_target_pairs={{0,4},{4,0},{1,5},{5,1},{2,6},{6,2},{3,7},{7,3},{8,12},{12,8},{9,1... | collective-permute-start | bytes 3538952 | tf_op jit(solution)/shard_map/ppermute | solution.py:557
  392.6 36.0 %collective-permute-start.38 = (bf16[2,4,80,1152]{3,2,1,0:T(8,128)(2,1)}, bf16[2,4,80,1152]{3,2,1,0:T(8,128)(2,1)}, u32[]{:S(2)}, u32[]{:S(2)}) collective-permute-start(bf16[2,4,80,1152]{3,2,1,0:T(8,128)(2,1)} %get-tuple-element.132.refs_4_), channel_id=1, source_target_pairs={{0,1},{1,0},{2,3},{3,2},{4,5},{5,4},{6,7},{7,6},{8,9},{9,8},{10,11... | collective-permute-start | bytes 4423688 | tf_op jit(solution)/shard_map/ppermute | solution.py:557
  431.0 33.2 %collective-permute-start.42 = (bf16[4,80,1152]{2,1,0:T(8,128)(2,1)}, bf16[4,80,1152]{2,1,0:T(8,128)(2,1)}, u32[]{:S(2)}, u32[]{:S(2)}) collective-permute-start(bf16[4,80,1152]{2,1,0:T(8,128)(2,1)} %fusion.42.rest_0_), channel_id=1, source_target_pairs={{0,4},{4,0},{1,5},{5,1},{2,6},{6,2},{3,7},{7,3},{8,12},{12,8},{9,1... | collective-permute-start | bytes 2211848 | tf_op jit(solution)/shard_map/ppermute | solution.py:557
  441.2 26.1 %collective-permute-start.43 = (bf16[2,4,3,72,1152]{4,3,1,2,0:T(8,128)(2,1)}, bf16[2,4,3,72,1152]{4,3,1,2,0:T(8,128)(2,1)}, u32[]{:S(2)}, u32[]{:S(2)}) collective-permute-start(bf16[2,4,3,72,1152]{4,3,1,2,0:T(8,128)(2,1)} %copy.103), channel_id=1, source_target_pairs={{0,2},{2,0},{1,3},{3,1},{4,6},{6,4},{5,7},{7,5},{8,10},{10,8},{9,1... | collective-permute-start | bytes 11943944 | tf_op jit(solution)/shard_map/ppermute | solution.py:557
  467.3 135.1 %reduce-scatter.10.cloned.1.call-start = ((), (), s32[]{:S(2)}) async-start(), calls=%async_computation.8 | async-start | bytes 2488320
  509.5 32.3 %collective-permute-start.58 = (bf16[2,4,72,1152]{3,2,1,0:T(8,128)(2,1)}, bf16[2,4,72,1152]{3,2,1,0:T(8,128)(2,1)}, u32[]{:S(2)}, u32[]{:S(2)}) collective-permute-start(bf16[2,4,72,1152]{3,2,1,0:T(8,128)(2,1)} %get-tuple-element.135.refs_16_), channel_id=1, source_target_pairs={{0,1},{1,0},{2,3},{3,2},{4,5},{5,4},{6,7},{7,6},{8,9},{9,8},{10,11... | collective-permute-start | bytes 3981320 | tf_op jit(solution)/shard_map/ppermute | solution.py:557
  516.0 9.0 %collective-permute-start.47 = (f32[1,432]{1,0:T(1,128)S(1)}, f32[1,432]{1,0:T(1,128)S(1)}, u32[]{:S(2)}, u32[]{:S(2)}) collective-permute-start(f32[1,432]{1,0:T(1,128)S(1)} %get-tuple-element.170), channel_id=1, source_target_pairs={{0,8},{8,16},{16,24},{24,0},{1,9},{9,17},{17,25},{25,1},{2,10},{10... | collective-permute-start | bytes 5192 | tf_op jit(solution)/shard_map/ppermute | solution.py:579
  516.7 9.9 %collective-permute-start.48 = (f32[1,432]{1,0:T(1,128)S(1)}, f32[1,432]{1,0:T(1,128)S(1)}, u32[]{:S(2)}, u32[]{:S(2)}) collective-permute-start(f32[1,432]{1,0:T(1,128)S(1)} %get-tuple-element.169), channel_id=1, source_target_pairs={{0,16},{8,24},{16,0},{24,8},{1,17},{9,25},{17,1},{25,9},{2,18},{10... | collective-permute-start | bytes 5192 | tf_op jit(solution)/shard_map/ppermute | solution.py:579
  523.2 27.8 %collective-permute-start.62 = (bf16[72,3328]{1,0:T(8,128)(2,1)}, bf16[72,3328]{1,0:T(8,128)(2,1)}, u32[]{:S(2)}, u32[]{:S(2)}) collective-permute-start(bf16[72,3328]{1,0:T(8,128)(2,1)} %reduce-scatter.6.cloned.1.call-done.refs_17_), channel_id=1, source_target_pairs={{0,1},{1,0},{2,3},{3,2},{4,5},{5,4},{6,7},{7,6},{8,9},{9,8},{10,11... | collective-permute-start | bytes 1437704 | tf_op jit(solution)/shard_map/ppermute | solution.py:557
  525.1 28.9 %collective-permute-start.55 = (bf16[4,72,1152]{2,1,0:T(8,128)(2,1)}, bf16[4,72,1152]{2,1,0:T(8,128)(2,1)}, u32[]{:S(2)}, u32[]{:S(2)}) collective-permute-start(bf16[4,72,1152]{2,1,0:T(8,128)(2,1)} %fusion.43.refs_15_), channel_id=1, source_target_pairs={{0,4},{4,0},{1,5},{5,1},{2,6},{6,2},{3,7},{7,3},{8,12},{12,8},{9,1... | collective-permute-start | bytes 1990664 | tf_op jit(solution)/shard_map/ppermute | solution.py:557
  528.1 24.9 %collective-permute-start.50 = (f32[4,1152]{1,0:T(4,128)S(1)}, f32[4,1152]{1,0:T(4,128)S(1)}, u32[]{:S(2)}, u32[]{:S(2)}) collective-permute-start(f32[4,1152]{1,0:T(4,128)S(1)} %convolution_select_fusion), channel_id=1, source_target_pairs={{0,2},{2,0},{1,3},{3,1},{4,6},{6,4},{5,7},{7,5},{8,10},{10,8},{9,1... | collective-permute-start | bytes 55304 | tf_op jit(solution)/shard_map/ppermute | solution.py:557
  543.2 15.1 %collective-permute-start.59 = (bf16[4,72,1152]{2,1,0:T(8,128)(2,1)S(1)}, bf16[4,72,1152]{2,1,0:T(8,128)(2,1)S(1)}, u32[]{:S(2)}, u32[]{:S(2)}) collective-permute-start(bf16[4,72,1152]{2,1,0:T(8,128)(2,1)S(1)} %fusion.48), channel_id=1, source_target_pairs={{0,4},{4,0},{1,5},{5,1},{2,6},{6,2},{3,7},{7,3},{8,12},{12,8},{9,1... | collective-permute-start | bytes 1990664 | tf_op jit(solution)/shard_map/ppermute | solution.py:557
  568.6 10.8 %collective-permute-start.61 = (bf16[208,1152]{1,0:T(8,128)(2,1)S(1)}, bf16[208,1152]{1,0:T(8,128)(2,1)S(1)}, u32[]{:S(2)}, u32[]{:S(2)}) collective-permute-start(bf16[208,1152]{1,0:T(8,128)(2,1)S(1)} %copy-done.35), channel_id=1, source_target_pairs={{0,1},{1,0},{2,3},{3,2},{4,5},{5,4},{6,7},{7,6},{8,9},{9,8},{10,11... | collective-permute-start | bytes 1437704 | tf_op jit(solution)/shard_map/ppermute | solution.py:557
  604.3 13.0 %collective-permute-start.60 = (bf16[3,72,1152]{2,1,0:T(8,128)(2,1)S(1)}, bf16[3,72,1152]{2,1,0:T(8,128)(2,1)S(1)}, u32[]{:S(2)}, u32[]{:S(2)}) collective-permute-start(bf16[3,72,1152]{2,1,0:T(8,128)(2,1)S(1)} %copy.107), channel_id=1, source_target_pairs={{0,1},{1,0},{2,3},{3,2},{4,5},{5,4},{6,7},{7,6},{8,9},{9,8},{10,11... | collective-permute-start | bytes 1493000 | tf_op jit(solution)/shard_map/ppermute | solution.py:557
  (87 other events, 701.2 us)
Sparse Core Ops, SparseCore 0:
  24.2 46.8 all-gather.5
  73.2 41.8 all-gather.9
  125.2 40.9 all-gather.7
  381.0 40.0 reduce-scatter.5
  467.4 39.1 reduce-scatter.7
  561.2 41.0 reduce-scatter.9

commit v3 on v2

--- a/solution.py
+++ b/solution.py
@@ -73,7 +73,7 @@
 
 
 BF16, F32 = jnp.bfloat16, jnp.float32
-SLAB = 16
+SLAB = 128
 COST_FLOPS, COST_BYTES = 6e9, 18e6
 GROUP = 128
 WIDE = 256
@@ -107,7 +107,7 @@
     return pl.CostEstimate(flops=int(us * COST_FLOPS), bytes_accessed=int(us * COST_BYTES), transcendentals=0)
 
 
-def run_kernel(body, operands, outs, scratch, us, ordered_after=(), mib=56, **kw):
+def run_kernel(body, operands, outs, scratch, us, ordered_after=(), mib=56, steps=None):
     arrays = [array for array, _ in operands] + list(ordered_after)
     specs = [spec for _, spec in operands] + [any_spec() for _ in ordered_after]
     n_in, n_dep = len(operands), len(ordered_after)
@@ -117,27 +117,27 @@
 
     return pl.pallas_call(
         kernel,
-        out_shape=[jax.ShapeDtypeStruct(shape, dtype) for shape, dtype in outs],
+        grid=() if steps is None else (steps,),
+        out_shape=[jax.ShapeDtypeStruct(*out[:2]) for out in outs],
         in_specs=specs,
-        out_specs=[vmem_spec() for _ in outs],
+        out_specs=[out[2] if len(out) > 2 else vmem_spec() for out in outs],
         scratch_shapes=scratch,
         compiler_params=pltpu.CompilerParams(vmem_limit_bytes=mib * 2**20),
         cost_estimate=cost(us),
-        **kw,
     )(*arrays)
 
 
 PIECES = 8
 
 
-def block_order(place):
+def block_order(place, zz=None):
     y, c = place[1], place[2]
-    for dc in range(2):
-        for dy in range(2):
-            yy = y if dy == 0 else 1 - y
-            cc = c if dc == 0 else 1 - c
-            for zz in range(4):
-                yield dc * 4 + dy * 2, zz, (zz * 2 + yy) * 2 + cc
+    for z in range(4) if zz is None else (zz,):
+        for dc in range(2):
+            for dy in range(2):
+                yy = y if dy == 0 else 1 - y
+                cc = c if dc == 0 else 1 - c
+                yield dc * 4 + dy * 2, z, (z * 2 + yy) * 2 + cc
 
 
 def start_all(copies, sems):
@@ -151,23 +151,23 @@
     x = place[3]
     for at, zz, b in block_order(place):
         main, other = pieces[at : at + 2]
-        yield main.at[zz, 0], wide.at[b * 3]
-        yield main.at[zz, 2], wide.at[b * 3 + 1 + x]
+        yield main.at[zz, :, pl.ds(0, D)], wide.at[b * 3]
+        yield main.at[zz, :, pl.ds(2 * D, D)], wide.at[b * 3 + 1 + x]
         yield other.at[zz], wide.at[b * 3 + 2 - x]
 
 
 def merge_copies(pieces, place, wide):
     for at, zz, b in block_order(place):
-        yield pieces[at].at[zz, 1], wide.at[b]
+        yield pieces[at].at[zz, :, pl.ds(D, D)], wide.at[b]
 
 
 UP_E, UP_L = 128, 80
 
 
-def up_copies(pieces, place, wide):
+def up_copies(pieces, place, wide, z=None):
     x = place[3]
     size = UP_E + 2 * UP_L
-    for at, zz, b in block_order(place):
+    for at, zz, b in block_order(place, z):
         main, other = pieces[at : at + 2]
         row = pl.multiple_of(b * size, 16)
         near_row = pl.multiple_of(b * size + UP_E + UP_L * x, 16)
@@ -185,8 +185,9 @@
     near_col = pl.multiple_of(DOWN_E + DOWN_L * x, 128)
     other_col = pl.multiple_of(DOWN_E + DOWN_L - DOWN_L * x, 128)
     for at, zz, b in block_order(place):
+        yield pieces[at].at[zz, :, pl.ds(0, DOWN_E)], wide.at[b, :, pl.ds(0, DOWN_E)]
+    for at, zz, b in block_order(place):
         main, other = pieces[at : at + 2]
-        yield main.at[zz, :, pl.ds(0, DOWN_E)], wide.at[b, :, pl.ds(0, DOWN_E)]
         yield main.at[zz, :, pl.ds(DOWN_E, DOWN_L)], wide.at[b, :, pl.ds(near_col, DOWN_L)]
         yield other.at[zz], wide.at[b, :, pl.ds(other_col, DOWN_L)]
 
@@ -244,8 +245,8 @@
     scores = dot_nn(key.astype(F32).T.astype(BF16), query) * (1.0 / math.sqrt(HEAD))
     scores = jnp.where(mask, scores, -1e30)
     top = jnp.max(scores, axis=0, keepdims=True)
-    expo = jnp.where(mask, jnp.exp(scores - top), 0.0)
-    return expo / jnp.sum(expo, axis=0, keepdims=True)
+    expo = jnp.exp(scores - top)
+    return expo * (1.0 / jnp.sum(expo, axis=0, keepdims=True))
 
 
 def qkv_kernel(place, tokens, mods, *rest):
@@ -297,29 +298,43 @@
     slabs(rows, SLAB, norm_two)
 
 
+def gelu_parts(u):
+    root = math.sqrt(2.0 / math.pi)
+    square = u * u
+    bent = jnp.tanh(u * (root + (root * 0.044715) * square))
+    half = 0.5 + 0.5 * bent
+    rise = root + (root * 3.0 * 0.044715) * square
+    return u * half, half + (0.5 * u) * (1.0 - bent * bent) * rise
+
+
 def up_kernel(place, h2, *rest):
     pieces, rest = rest[:PIECES], rest[PIECES:]
-    act, slope, wide, upper, sems = rest
-    for copy in start_all(list(up_copies(pieces, place, wide)), sems):
-        copy.wait()
+    act, slope, wide, even, odd, sems = rest
+    step = pl.program_id(0)
+
+    @pl.when(step == 0)
+    def _():
+        start_all(list(up_copies(pieces, place, wide)), sems)
+
+    for i, (src, dst) in enumerate(up_copies(pieces, place, wide, step)):
+        pltpu.make_async_copy(src, dst, sems.at[step * 12 + i]).wait()
     rows = h2.shape[0]
-    root = math.sqrt(2.0 / math.pi)
-
-    @pl.loop(0, FF // WIDE)
-    def _(i):
-        cols = pl.ds(pl.multiple_of(i * WIDE, WIDE), WIDE)
-        upper[...] = dot_nt(h2[...], wide[cols])
-
-        def gelu(at):
-            u = upper[at]
-            square = u * u
-            bent = jnp.tanh(root * u * (1.0 + 0.044715 * square))
-            half = 0.5 * (1.0 + bent)
-            act[at, cols] = (u * half).astype(BF16)
-            rise = root * (1.0 + 3.0 * 0.044715 * square)
-            slope[at, cols] = (half + 0.5 * u * (1.0 - bent * bent) * rise).astype(BF16)
-
-        slabs(rows, 32, gelu)
+    ends = [(at, min(WIDE, D - at)) for at in range(0, D, WIDE)]
+
+    def finish(upper, first, width):
+        for row in range(0, rows, 32):
+            at = pl.ds(row, 32)
+            value, rise = gelu_parts(upper[at, :width])
+            act[at, pl.ds(first, width)] = value.astype(BF16)
+            slope[at, pl.ds(first, width)] = rise.astype(BF16)
+
+    for number, (first, width) in enumerate(ends):
+        upper, before = (even, odd) if number % 2 == 0 else (odd, even)
+        at = pl.ds(pl.multiple_of(step * D + first, 128), width)
+        upper[:, :width] = dot_nt(h2[...], wide[at])
+        if number:
+            finish(before, *ends[number - 1])
+    finish(even if len(ends) % 2 else odd, *ends[-1])
 
 
 def start_back_kernel(place, out_grad, mods, d_mlp, relative, turned):
@@ -337,22 +352,35 @@
 
 def d_upper_kernel(place, d_mlp, slope, *rest):
     pieces, rest = rest[:PIECES], rest[PIECES:]
-    d_upper, d_upper_t, wide, value, sems = rest
-    for copy in start_all(list(down_copies(pieces, place, wide)), sems):
-        copy.wait()
+    d_upper, d_upper_t, wide, even, odd, sems = rest
+    step = pl.program_id(0)
+
+    @pl.when(step == 0)
+    def _():
+        for copy in start_all(list(down_copies(pieces, place, wide)), sems)[:16]:
+            copy.wait()
+
+    @pl.when(step == DOWN_E // (2 * WIDE))
+    def _():
+        for i, (src, dst) in enumerate(down_copies(pieces, place, wide)):
+            if i >= 16:
+                pltpu.make_async_copy(src, dst, sems.at[i]).wait()
+
     rows = d_mlp.shape[0]
 
-    @pl.loop(0, FF // WIDE)
-    def _(i):
-        cols = pl.ds(pl.multiple_of(i * WIDE, WIDE), WIDE)
-        value[...] = dot_nn(d_mlp[...], rows_of(wide, 0, 16, cols))
-
-        @pl.loop(0, rows // GROUP)
-        def _(j):
-            at = pl.ds(pl.multiple_of(j * GROUP, GROUP), GROUP)
+    def finish(value, first):
+        cols = pl.ds(first, WIDE)
+        for row in range(0, rows, GROUP):
+            at = pl.ds(row, GROUP)
             part = value[at] * slope[at, cols].astype(F32)
             d_upper[at, cols] = part.astype(BF16)
             d_upper_t[cols, at] = part.T.astype(BF16)
+
+    base = pl.multiple_of(step * 2 * WIDE, 2 * WIDE)
+    even[...] = dot_nn(d_mlp[...], rows_of(wide, 0, 16, pl.ds(base, WIDE)))
+    odd[...] = dot_nn(d_mlp[...], rows_of(wide, 0, 16, pl.ds(base + WIDE, WIDE)))
+    finish(even, 0)
+    finish(odd, WIDE)
 
 
 def middle_back_kernel(place, d_upper, tokens, out_grad, branch, mods, *rest):
@@ -360,10 +388,17 @@
     d_middle, d_branch, relative, d_att, sums, wide, merge, value, turned, fold_a, fold_b, fold_c, sems = rest
     copies = list(up_copies(ups, place, wide)) + list(merge_copies(firsts, place, merge))
     copies = start_all(copies, sems)
-    for copy in copies:
+    rows = tokens.shape[0]
+    for z in range(4):
+        for copy in copies[z * 12 : (z + 1) * 12]:
+            copy.wait()
+        add = dot_nn(d_upper[:, z * D : (z + 1) * D], wide[z * D : (z + 1) * D])
+        if z == 0:
+            value[...] = add
+        else:
+            value[...] += add
+    for copy in copies[48:]:
         copy.wait()
-    rows = tokens.shape[0]
-    value[...] = dot_nn(d_upper[...], wide[...])
     for ref in (fold_a, fold_b, fold_c):
         ref[...] = jnp.zeros_like(ref)
 
@@ -399,10 +434,11 @@
     mask = frame_mask(place[4])
     scale = 1.0 / math.sqrt(HEAD)
 
-    @pl.loop(0, HEADS)
-    def _(head):
-        for group in range(rows // GROUP):
-            at = pl.ds(group * GROUP, GROUP)
+    @pl.loop(0, HEADS // 2)
+    def _(pair):
+        for number in range(2 * rows // GROUP):
+            head = pair * 2 + number % 2
+            at = pl.ds(number // 2 * GROUP, GROUP)
             query, key = qkv[head, :, at], qkv[HEADS + head, :, at]
             val, grad = qkv[2 * HEADS + head, :, at], d_att[head, :, at]
             probs = probs_of(key, query, mask)
@@ -423,7 +459,7 @@
             zz, yy, cc = b // 4, (b // 2) % 2, b % 2
             dy = y if yy == 0 else 1 - y
             dc = c if cc == 0 else 1 - c
-            relative[dc, dy * 4 + zz, tile] = ref[head].astype(BF16)
+            relative[dc, tile, dy * 4 + zz] = ref[head].astype(BF16)
 
 
 def input_back_kernel(place, d_qkv, tokens, d_middle, mods, *rest):
@@ -458,15 +494,15 @@
 def output_kernel(place, act, tokens, branch, out_grad, mods, *rest):
     pieces, rest = rest[:PIECES], rest[PIECES:]
     block_out, sums, wide, value, fold_a, sems = rest
-    for copy in start_all(list(down_copies(pieces, place, wide)), sems):
+    copies = start_all(list(down_copies(pieces, place, wide)), sems)
+    rows = tokens.shape[0]
+    for copy in copies[:16]:
         copy.wait()
-    rows = tokens.shape[0]
-    value[...] = jnp.zeros_like(value)
-
-    @pl.loop(0, FF // WIDE)
-    def _(i):
-        cols = pl.ds(pl.multiple_of(i * WIDE, WIDE), WIDE)
-        value[...] += dot_nt(act[:, cols], rows_of(wide, 0, 16, cols))
+    value[...] = dot_nt(act[:, :DOWN_E], rows_of(wide, 0, 16, pl.ds(0, DOWN_E)))
+    for copy in copies[16:]:
+        copy.wait()
+    rest_cols = pl.ds(DOWN_E, FF - DOWN_E)
+    value[...] += dot_nt(act[:, DOWN_E:], rows_of(wide, 0, 16, rest_cols))
 
     fold_a[...] = jnp.zeros_like(fold_a)
 
@@ -606,16 +642,12 @@
     return jnp.where(flag, jnp.concatenate([early, near_late], axis=axis), got)
 
 
-def gather_near(mine):
-    near = lax.all_gather(mine.reshape(-1, mine.shape[-1]), "z", axis=0, tiled=False)
-    return near.reshape(near.shape[:1] + mine.shape)
-
-
-def gather_pieces(near, cut, before_far, before_late):
+def gather_pieces(near, cut, before_far, before_near_late, before_late, before_core=()):
     far = swap(after(near, *before_far), "y")
-    late = swap(cut(after(far, *before_late)), "x")
-    pieces = [near, swap(cut(near), "x"), far, late]
-    return pieces + [swap(piece, "c") for piece in pieces]
+    near_late = swap(cut(after(near, *before_near_late)), "x")
+    far_late = swap(cut(after(far, near_late, *before_late)), "x")
+    pieces = [near, near_late, far, far_late]
+    return pieces + [swap(after(piece, *before_core), "c") for piece in pieces]
 
 
 def core_sum(keep, send, cut, x):
@@ -633,8 +665,8 @@
     return [add_low(late_keep[i], got[i]) for i in range(2)]
 
 
-def over_y(halves):
-    return add_low(halves[0], swap(halves[1], "y"))
+def over_y(halves, before=()):
+    return add_low(halves[0], after(swap(halves[1], "y"), *before))
 
 
 def over_z(value):
@@ -661,12 +693,13 @@
     attend_t, merge_t, up_t, down_t = own_low[3:]
     tiles = attend_t.reshape(3, span, width)
     flags = jnp.stack([own[3], own[4]])[:, None, None]
+    flag = jnp.where(jnp.arange(2 * width) < width, own[3], own[4])
     first_mine = own_block(
-        jnp.stack([tiles[0], merge_t]),
-        (tiles[1:2], tiles[2:3]),
-        jnp.stack([own[3], own[4]])[:, None, None],
+        jnp.concatenate([tiles[0], merge_t], axis=1),
+        (tiles[1], tiles[2]),
+        flag,
         (own[3], own[3]),
-        0,
+        1,
         x,
         (),
     )
@@ -709,12 +742,9 @@
     mod_row = sum_plane(mod_row)
     mods = jnp.concatenate([mod_row.reshape(6, width), jnp.zeros((2, width), F32)])
 
-    first_near, up_near, down_near = (
-        gather_near(mine) for mine in (first_mine, up_mine, down_mine)
-    )
-    firsts = gather_pieces(first_near, lambda main: main[:, 2], (mods,), ())
-    ups = gather_pieces(up_near, lambda main: main[:, UP_E:], firsts[:1], ())
-
+    first_near = lax.all_gather(first_mine, "z", axis=0, tiled=False)
+    up_near = lax.all_gather(up_mine, "z", axis=0, tiled=False)
+    down_near = lax.all_gather(down_mine, "z", axis=0, tiled=False)
     tokens = inputs.reshape(rows, width)
     grad_out = out_grad.reshape(rows, width)
     spot = (place, smem_spec())
@@ -727,7 +757,10 @@
         [spot] + in_vmem(grad_out, mods),
         [((rows, width), BF16), ((2, 8, span, rows), BF16)],
         [vmem(width, rows, dtype=F32)],
-        us=4,
+        us=1,
+    )
+    firsts = gather_pieces(
+        first_near, lambda main: main[:, :, 2 * width :], (mods,), (), ()
     )
     h1, qkv = run_kernel(
         qkv_kernel,
@@ -735,7 +768,7 @@
         [((rows, width), BF16), ((48, span, rows), BF16)],
         [vmem(48, span, width), sems(48)],
         us=18,
-        ordered_after=[down_near],
+        ordered_after=[d_mlp_rel],
     )
     attended, branch, h2 = run_kernel(
         attend_kernel,
@@ -744,15 +777,17 @@
         [vmem(16, span, width), vmem(16, span, rows, dtype=F32), sems(16)],
         us=20,
     )
-    downs = gather_pieces(down_near, lambda main: main[:, :, DOWN_E:], ups[:1], (h2,))
+    ups = gather_pieces(up_near, lambda main: main[:, UP_E:], firsts[:1], (), (h1,), (h2,))
     act, slope = run_kernel(
         up_kernel,
         [spot] + in_vmem(h2) + in_place(ups),
-        [((rows, FF), BF16)] * 2,
-        [vmem(FF, width), vmem(rows, WIDE, dtype=F32), sems(48)],
-        us=27,
-    )
-    down_keep, down_send = pair_grads(d_mlp_rel.reshape(2, 8 * span, rows), act, downs[3:4])
+        [((rows, FF), BF16, pl.BlockSpec((rows, width), lambda i: (0, i)))] * 2,
+        [vmem(FF, width)] + [vmem(rows, WIDE, dtype=F32)] * 2 + [sems(48)],
+        steps=4,
+        us=15,
+    )
+    down_keep, down_send = pair_grads(d_mlp_rel.reshape(2, 8 * span, rows), act)
+    downs = gather_pieces(down_near, lambda main: main[:, :, DOWN_E:], (h1,), (h2,), (act,), (down_keep,))
     cut_down = lambda v: (
         v[..., :DOWN_E],
         v[..., DOWN_E : DOWN_E + DOWN_L],
@@ -763,18 +798,23 @@
 
     d_upper, d_upper_t = run_kernel(
         d_upper_kernel,
-        [spot] + in_vmem(d_mlp, slope) + in_place(downs),
-        [((rows, FF), BF16), ((FF, rows), BF16)],
-        [vmem(16, span, FF), vmem(rows, WIDE, dtype=F32), sems(48)],
-        us=28,
-        ordered_after=[down_early[1], down_late[1]],
-    )
-    up_keep, up_send = up_grads(place, d_upper_t, h2)
+        [spot]
+        + in_vmem(d_mlp)
+        + [(slope, pl.BlockSpec((rows, 2 * WIDE), lambda i: (0, i)))]
+        + in_place(downs),
+        [
+            ((rows, FF), BF16, pl.BlockSpec((rows, 2 * WIDE), lambda i: (0, i))),
+            ((FF, rows), BF16, pl.BlockSpec((2 * WIDE, rows), lambda i: (i, 0))),
+        ],
+        [vmem(16, span, FF)] + [vmem(rows, WIDE, dtype=F32)] * 2 + [sems(48)],
+        steps=FF // (2 * WIDE),
+        us=16,
+    )
+    up_keep, up_send = up_grads(place, d_upper_t, h2, [down_early[1], down_late[1]])
     cut_up = lambda v: (v[:, :, :UP_E], v[:, :, UP_E : UP_E + UP_L], v[:, :, UP_E + UP_L :])
     shape = (2, 4, 4 * span, width)
     up_early, *up_late = core_sum(up_keep.reshape(shape), up_send.reshape(shape), cut_up, x)
 
-    down_late = late_sum(*down_late, (up_keep,))
     d_middle, d_branch, d_branch_rel, d_att, sums_two = run_kernel(
         middle_back_kernel,
         [spot] + in_vmem(d_upper, tokens, grad_out, branch, mods) + in_place(ups + firsts),
@@ -793,32 +833,34 @@
         ]
         + [vmem(8, width, dtype=F32)] * 3
         + [sems(64)],
-        ordered_after=[down_late[1]],
-        us=33,
+        ordered_after=[up_keep],
+        us=24,
     )
     merge_keep, merge_send = pair_grads(d_branch_rel.reshape(2, 8 * span, rows), attended)
     shape = (2, 4, span, width)
     merge_keep = merge_keep.reshape(shape)
     merge_got = swap(merge_send.reshape(shape), "c")
-    merge_total = over_y([add_low(merge_keep[i], merge_got[i]) for i in range(2)])
-
-    down_total = jnp.concatenate(
-        [over_y(down_early), after(over_y(down_late), d_middle)], axis=-1
-    )
+    merge_halves = [add_low(merge_keep[i], merge_got[i]) for i in range(2)]
+
+    down_late = late_sum(*down_late, (d_middle,))
     d_qkv, d_qkv_rel = run_kernel(
         attend_back_kernel,
         [spot] + in_vmem(qkv, d_att),
-        [((rows, 3 * width), BF16), ((2, 8, 3, span, rows), BF16)],
+        [((rows, 3 * width), BF16), ((2, 3, 8, span, rows), BF16)],
         [vmem(16, span, rows, dtype=F32)] * 3,
-        ordered_after=[up_early[1], up_late[1], down_total],
-        us=26,
+        ordered_after=[up_early[1], up_late[1], down_late[1]],
+        us=25,
     )
     up_late = late_sum(*up_late, (d_qkv,))
+    down_total = jnp.concatenate(
+        [over_y(down_early, (d_qkv,)), over_y(down_late, (d_qkv,))], axis=-1
+    )
+    up_over = over_y(up_early)
     attend_keep, attend_send = pair_grads(
-        d_qkv_rel.reshape(2, 24 * span, rows), h1, [up_late[1]]
-    )
-    cut_attend = lambda v: (v[:, :, 0], v[:, :, 1], v[:, :, 2])
-    shape = (2, 4, 3, span, width)
+        d_qkv_rel.reshape(2, 24 * span, rows), h1, [down_total, up_late[1], up_over]
+    )
+    cut_attend = lambda v: (v[0], v[1], v[2])
+    shape = (3, 2, 4, span, width)
     first_early, *first_late = core_sum(
         attend_keep.reshape(shape), attend_send.reshape(shape), cut_attend, x
     )
@@ -831,10 +873,13 @@
         [vmem(48, span, width), vmem(rows, width, dtype=F32)]
         + [vmem(8, width, dtype=F32)] * 2
         + [sems(48)],
-        ordered_after=[attend_keep],
-        us=22,
-    )
-    up_total = jnp.concatenate([over_y(up_early), after(over_y(up_late), input_grad)], axis=1)
+        ordered_after=[first_early[1], first_late[1]],
+        us=16,
+    )
+    up_total = jnp.concatenate([up_over, over_y(up_late)], axis=1)
+    early_total = jnp.concatenate(
+        [over_y(halves, (input_grad,)) for halves in (first_early, merge_halves)], axis=2
+    )
     block_out, sums_out = run_kernel(
         output_kernel,
         [spot] + in_vmem(act, tokens, branch, grad_out, mods) + in_place(downs),
@@ -845,25 +890,25 @@
             vmem(8, width, dtype=F32),
             sems(48),
         ],
-        ordered_after=[up_total, first_early[1], first_late[1], down_part],
-        us=21,
-    )
+        ordered_after=[up_total, early_total],
+        us=17,
+    )
+    up_part = over_z(after(up_total, down_part))
     first_late = late_sum(*first_late, (block_out,))
-    up_part = over_z(after(up_total, down_part))
-    first_total = jnp.concatenate([over_y(first_early), merge_total, over_y(first_late)], axis=2)
-    first_part = over_z(after(first_total, up_part))
-    first_part = first_part.reshape(span, 3, width).transpose(1, 0, 2)
-    down_got, up_got, first_got = swap(down_part, "x"), swap(up_part, "x"), swap(first_part, "x")
+    early_part = over_z(after(early_total, up_part))
+    late_part = over_z(after(over_y(first_late), up_part))
+    down_got, up_got = swap(down_part, "x"), swap(up_part, "x")
+    early_got, late_got = swap(early_part, "x"), swap(late_part, "x")
 
     d_vector = jnp.concatenate([sums_one[:2], sums_two[:3], sums_out[:1]]).reshape(6 * width)
-    d_mod = sum_plane(after(d_vector, up_part).reshape(4, 4, mod_span))
+    d_mod = sum_plane(after(d_vector, up_part, first_late[1]).reshape(4, 4, mod_span))
     d_mod = lax.dynamic_index_in_dim(d_mod, y * 2 + c, 1, keepdims=False)
     d_mod = turn_z(d_mod, z)
     grad_mod = contract_rows(d_mod, cond_act.astype(F32), HIGHEST)
     d_cond_part = jnp.dot(
         d_mod, own_low[2].astype(F32), precision=HIGHEST, preferred_element_type=F32
     )
-    d_cond_act = sum_all(jnp.where(own[2], d_cond_part, 0.0))
+    d_cond_act = sum_all(after(jnp.where(own[2], d_cond_part, 0.0), early_part))
     d_cond = silu_back(d_cond_act)[0]
     d_time_pre = jax.vjp(jax.nn.silu, time_pre)[1](d_cond)[0]
     d_cond_block = lax.dynamic_slice_in_dim(d_cond, block * span, span, 1)
@@ -885,12 +930,12 @@
         grad_mod,
         jnp.concatenate(
             [
-                both(first_part[0], first_got[0]),
-                jnp.where(x == 0, first_part[2], first_got[2]).astype(F32),
-                jnp.where(x == 0, first_got[2], first_part[2]).astype(F32),
+                both(early_part[:, :width], early_got[:, :width]),
+                jnp.where(x == 0, late_part, late_got).astype(F32),
+                jnp.where(x == 0, late_got, late_part).astype(F32),
             ]
         ),
-        both(first_part[1], first_got[1]),
+        both(early_part[:, width:], early_got[:, width:]),
         jnp.concatenate(
             [
                 both(up_part[:UP_E], up_got[:UP_E]),

time: 635 us -> 588 us (0.926)
  Pallas kernels: 224 us -> 171 us
  waiting for transfers between devices: 194 us -> 219 us
  local copies, waits for them, and re-layouts: 41.9 us -> 27.4 us
    ppermute x53 -> x54, waiting for transfers between devices: 116 us -> 196 us  [swap(): return lax.ppermute(value, axis, [(0, 1), (1, 0)])]
    pallas_call x9, Pallas kernels: 199 us -> 144 us  [run_kernel(): pl.pallas_call(kernel, grid=() if steps is None else (steps,), out_shape=...]
    all_gather x3, waiting for transfers between devices: 36.3 us -> 0.02 us  [the longest x1 0.02 us: on_grid(): up_near = lax.all_gather(up_mine, 'z', axis=0, tiled=False)]
    unnamed x7 -> x8, waiting for transfers between devices: 22.9 us -> 10.5 us
    reduce_scatter x2 -> x3, waiting for transfers between devices: 10.6 us -> 1.16 us  [over_z(): part = lax.psum_scatter(flat, 'z', scatter_dimension=0, tiled=True)]
    ppermute x53 -> x54, starting transfers between devices: 49.3 us -> 47.7 us  [swap(): return lax.ppermute(value, axis, [(0, 1), (1, 0)])]
  transfers between devices with their start and end apart: 69 -> 71, of which waited for: 25 -> 30; matrix products, arithmetic and copies ran while one was open for 16% -> 15% of each run, Pallas kernels for 34% -> 28%
where the time goes in v3:
time: 588 us; the launch traced here: 582 us
  waiting for transfers between devices  219 us (37%)
  Pallas kernels  171 us (29%)
  other arithmetic  69.2 us (12%)
  starting transfers between devices  63.5 us (11%)
  local copies, waits for them, and re-layouts  27.4 us (5%)
  between operations  20.3 us (3%)
  matrix products  12.3 us (2%)
    ppermute x54, waiting for transfers between devices, swap(): return lax.ppermute(value, axis, [(0, 1), (1, 0)])  196 us
    pallas_call x9, Pallas kernels, run_kernel(): pl.pallas_call(kernel, grid=() if steps is None else (steps,), out_shape=...  144 us
    ppermute x54, starting transfers between devices, swap(): return lax.ppermute(value, axis, [(0, 1), (1, 0)])  47.7 us
    convert_element_type x17, other arithmetic, add_low(): return total.astype(BF16)  40 us
    pallas_call x3, Pallas kernels, pair_grads(): pl.pallas_call(kernel, grid=grid, out_shape=[jax.ShapeDtypeStruct((rows,...  18.1 us
    convert_element_type x4, other arithmetic, on_grid(): copy_list.append(fresh.astype(BF16))  14.9 us
  transfers between devices with their start and end apart: 71, of which 30 were waited for; matrix products, arithmetic and copies ran while one was open for 15% of the time, Pallas kernels for 28%

profile of v3, /device:TPU:0, one launch (start us, length us, event | category | flops | bytes accessed | tf_op | source)
XLA Modules:
  0.0 582.4 jit_solution(9912455640907300319)
XLA Ops:
  8.8 3.0 collective-permute-start.11
  15.5 7.6 %collective-permute-done.11 = bf16[72,3456]{1,0:T(8,128)(2,1)S(1)} collective-permute-done((bf16[72,3456]{1,0:T(8,128)(2,1)S(1)}, bf16[72,3456]{1,0:T(8,128)(2,1)S(1)}, u32[]{:S(2)}, u32[]{:S(2)}) %collective-permute-start.11) | collective-permute-done | bytes 497696 | tf_op jit(solution)/shard_map/ppermute | solution.py:593
  29.9 2.3 collective-permute-start.2
  36.4 2.8 collective-permute-done.3
  39.3 2.9 collective-permute-start.4
  43.9 2.8 collective-permute-done.4
  48.2 3.4 collective-permute-start.6
  58.5 11.3 %collective-permute-done.9 = f32[4,4,432]{2,1,0:T(4,128)S(1)} collective-permute-done((f32[4,4,432]{2,1,0:T(4,128)S(1)}, f32[4,4,432]{2,1,0:T(4,128)S(1)}, u32[]{:S(2)}, u32[]{:S(2)}) %collective-permute-start.9) | collective-permute-done | bytes 27680 | tf_op jit(solution)/shard_map/ppermute | solution.py:593
  81.7 37.0 %collective-permute-done.13.refs_5_.refs_6_.refs_16_.refs_7_ = bf16[4,72,3456]{2,1,0:T(8,128)(2,1)} collective-permute-done((bf16[4,72,3456]{2,1,0:T(8,128)(2,1)}, bf16[4,72,3456]{2,1,0:T(8,128)(2,1)}, u32[]{:S(2)}, u32[]{:S(2)}) %collective-permute-start.13) | collective-permute-done | bytes 1990688 | tf_op jit(solution)/shard_map/ppermute | solution.py:593
  124.8 3.5 shard_map.490
  128.4 9.6 %collective-permute-done.14.refs_6_.refs_7_.refs_17_.refs_8_ = bf16[4,72,1152]{2,1,0:T(8,128)(2,1)S(1)} collective-permute-done((bf16[4,72,1152]{2,1,0:T(8,128)(2,1)S(1)}, bf16[4,72,1152]{2,1,0:T(8,128)(2,1)S(1)}, u32[]{:S(2)}, u32[]{:S(2)}) %collective-permute-start.14) | collective-permute-done | bytes 663584 | tf_op jit(solution)/shard_map/ppermute | solution.py:593
  137.9 9.9 %collective-permute-done.27 = bf16[72,3328]{1,0:T(8,128)(2,1)S(1)} collective-permute-done((bf16[72,3328]{1,0:T(8,128)(2,1)S(1)}, bf16[72,3328]{1,0:T(8,128)(2,1)S(1)}, u32[]{:S(2)}, u32[]{:S(2)}) %collective-permute-start.27) | collective-permute-done | bytes 479264 | tf_op jit(solution)/shard_map/ppermute | solution.py:593
  155.4 14.0 %shard_map.491 = (bf16[512,1152]{1,0:T(8,128)(2,1)}, bf16[48,72,512]{2,1,0:T(8,128)(2,1)}) custom-call(s32[8]{0:T(128)} %stack.32.refs_0_.place_ref, bf16[512,1152]{1,0:T(8,128)(2,1)} %bitcast.524, f32[8,1152]{1,0:T(8,128)} %concatenate.65.refs_2_.refs_3_.refs_5_.refs_4_, bf16[4,72,3456]{2,1,0:T(8,128)(2,1)} %bitcast.25.refs_3_.refs_4_.refs_14_.refs_5_, ...), custom_call_target="tpu_custom_call" | custom-call | flops 108000002048 | bytes 324000000 | tf_op jit(solution)/shard_map/pallas_call | solution.py:118
  169.4 15.4 %shard_map.492 = (bf16[512,1152]{1,0:T(8,128)(2,1)}, f32[512,1152]{1,0:T(8,128)}, bf16[512,1152]{1,0:T(8,128)(2,1)}) custom-call(s32[8]{0:T(128)} %stack.32.refs_0_.place_ref, bf16[48,72,512]{2,1,0:T(8,128)(2,1)} %get-tuple-element.91.refs_1_, bf16[512,1152]{1,0:T(8,128)(2,1)} %bitcast.525, f32[8,1152]{1,0:T(8,128)} %concatenate.65.refs_2_.refs_3_.refs_5_.refs_4_, ...), custom_call_target="tpu_custom_call" | custom-call | flops 120000004096 | bytes 360000000 | tf_op jit(solution)/shard_map/pallas_call | solution.py:118
  184.8 8.3 %collective-permute-done.21.refs_4_.refs_8_ = bf16[4,208,1152]{2,1,0:T(8,128)(2,1)} collective-permute-done((bf16[4,208,1152]{2,1,0:T(8,128)(2,1)}, bf16[4,208,1152]{2,1,0:T(8,128)(2,1)}, u32[]{:S(2)}, u32[]{:S(2)}) %collective-permute-start.21) | collective-permute-done | bytes 1916960 | tf_op jit(solution)/shard_map/ppermute | solution.py:593
  196.4 16.9 %collective-permute-done.22.refs_5_.refs_9_ = bf16[4,80,1152]{2,1,0:T(8,128)(2,1)} collective-permute-done((bf16[4,80,1152]{2,1,0:T(8,128)(2,1)S(1)}, bf16[4,80,1152]{2,1,0:T(8,128)(2,1)}, u32[]{:S(2)}, u32[]{:S(2)}) %collective-permute-start.22) | collective-permute-done | bytes 737312 | tf_op jit(solution)/shard_map/ppermute | solution.py:593
  217.7 14.9 %shard_map.493 = (bf16[512,4608]{1,0:T(8,128)(2,1)}, bf16[512,4608]{1,0:T(8,128)(2,1)}) custom-call(s32[8]{0:T(128)} %stack.32.refs_0_.place_ref, bf16[512,1152]{1,0:T(8,128)(2,1)} %get-tuple-element.92.refs_1_.right_ref, bf16[4,208,1152]{2,1,0:T(8,128)(2,1)} %bitcast.30.refs_2_.refs_6_, bf16[4,80,1152]{2,1,0:T(8,128)(2,1)} %collective-permute-done.20.refs_3_.refs_7_, ...), custom_call_target="tpu_custom_call" | custom-call | flops 89999998976 | bytes 270000000 | tf_op jit(solution)/shard_map/pallas_call | solution.py:118
  232.7 2.3 copy-done.10
  235.0 9.2 %shard_map.494 = (bf16[576,4608]{1,0:T(8,128)(2,1)S(1)}, bf16[576,4608]{1,0:T(8,128)(2,1)}) custom-call(bf16[2,576,512]{2,1,0:T(8,128)(2,1)S(1)} %bitcast.499, bf16[2,576,512]{2,1,0:T(8,128)(2,1)S(1)} %bitcast.500, bf16[512,4608]{1,0:T(8,128)(2,1)S(1)} %copy-done.10), custom_call_target="tpu_custom_call" | custom-call | flops 27179089920 | bytes 81537272 | tf_op jit(solution)/shard_map/pallas_call | solution.py:535
  244.1 16.3 %collective-permute-done.29.refs_5_.refs_8_ = bf16[4,72,3328]{2,1,0:T(8,128)(2,1)} collective-permute-done((bf16[4,72,3328]{2,1,0:T(8,128)(2,1)}, bf16[4,72,3328]{2,1,0:T(8,128)(2,1)}, u32[]{:S(2)}, u32[]{:S(2)}) %collective-permute-start.29) | collective-permute-done | bytes 1916960 | tf_op jit(solution)/shard_map/ppermute | solution.py:593
  262.9 18.0 %collective-permute-done.30.refs_6_.refs_9_ = bf16[4,72,1280]{2,1,0:T(8,128)(2,1)S(1)} collective-permute-done((bf16[4,72,1280]{2,1,0:T(8,128)(2,1)S(1)}, bf16[4,72,1280]{2,1,0:T(8,128)(2,1)S(1)}, u32[]{:S(2)}, u32[]{:S(2)}) %collective-permute-start.30) | collective-permute-done | bytes 737312 | tf_op jit(solution)/shard_map/ppermute | solution.py:593
  281.4 2.7 collective-permute-done.34.refs_10_.refs_13_
  286.8 15.7 %shard_map.495 = (bf16[512,4608]{1,0:T(8,128)(2,1)}, bf16[4608,512]{1,0:T(8,128)(2,1)}) custom-call(s32[8]{0:T(128)} %stack.32.refs_0_.place_ref, bf16[512,1152]{1,0:T(8,128)(2,1)} %get-tuple-element.112.refs_1_, bf16[512,4608]{1,0:T(8,128)(2,1)} %get-tuple-element.113.refs_2_, bf16[4,72,3328]{2,1,0:T(8,128)(2,1)} %bitcast.518, ...), custom_call_target="tpu_custom_call" | custom-call | flops 96000000000 | bytes 288000000 | tf_op jit(solution)/shard_map/pallas_call | solution.py:118
  302.6 4.7 add_convert_fusion
  307.7 2.7 fusion.29.rest_0_
  312.0 8.9 %shard_map.496 = (bf16[8,288,1152]{2,1,0:T(8,128)(2,1)S(1)}, bf16[8,288,1152]{2,1,0:T(8,128)(2,1)}) custom-call(s32[8]{0:T(128)S(1)} %copy-done.5, bf16[4608,512]{1,0:T(8,128)(2,1)S(1)} %copy-done.12, bf16[4608,512]{1,0:T(8,128)(2,1)S(1)} %copy-done.12, bf16[512,1152]{1,0:T(8,128)(2,1)S(1)} %copy-done.13, bf16[4,72,2048]{2,1,0:T(8,128)(2,1)} %fusion.29.rest_0_, ...), custom_call_target="tpu_custom_call" | custom-call | flops 54000001024 | bytes 162000000 | tf_op jit(solution)/shard_map/pallas_call | solution.py:568
  323.2 23.6 %shard_map.497 = (f32[512,1152]{1,0:T(8,128)}, bf16[512,1152]{1,0:T(8,128)(2,1)}, bf16[2,8,72,512]{3,2,1,0:T(8,128)(2,1)}, bf16[16,72,512]{2,1,0:T(8,128)(2,1)}, f32[8,1152]{1,0:T(8,128)}) custom-call(s32[8]{0:T(128)} %stack.32.refs_0_.place_ref, bf16[512,4608]{1,0:T(8,128)(2,1)} %get-tuple-element.118.refs_1_, bf16[512,1152]{1,0:T(8,128)(2,1)} %bitcast.526, ...), custom_call_target="tpu_custom_call" | custom-call | flops 143999991808 | bytes 432000000 | tf_op jit(solution)/shard_map/pallas_call | solution.py:118
  349.5 2.6 fusion.31.refs_3_
  353.7 4.5 add_convert_fusion.1
  359.6 24.5 %shard_map.498 = (bf16[512,3456]{1,0:T(8,128)(2,1)}, bf16[2,3,8,72,512]{4,3,2,1,0:T(8,128)(2,1)}) custom-call(s32[8]{0:T(128)} %stack.32.refs_0_.place_ref, bf16[48,72,512]{2,1,0:T(8,128)(2,1)} %get-tuple-element.91.refs_1_, bf16[16,72,512]{2,1,0:T(8,128)(2,1)} %get-tuple-element.119.refs_2_, bf16[4,128,1152]{2,1,0:T(8,128)(2,1)} %fusion.31.refs_3_, ...), custom_call_target="tpu_custom_call" | custom-call | flops 149999992832 | bytes 450000000 | tf_op jit(solution)/shard_map/pallas_call | solution.py:118
  385.7 2.6 fusion.2
  388.5 5.0 collective-permute-done.37
  393.5 2.6 fusion.3.rest_2_
  397.7 6.3 %shard_map.499 = (bf16[1728,1152]{1,0:T(8,128)(2,1)S(1)}, bf16[1728,1152]{1,0:T(8,128)(2,1)}) custom-call(bf16[2,1728,512]{2,1,0:T(8,128)(2,1)S(1)} %bitcast.497, bf16[2,1728,512]{2,1,0:T(8,128)(2,1)S(1)} %bitcast.498, bf16[512,1152]{1,0:T(8,128)(2,1)S(1)} %copy-done.11, bf16[4,72,3328]{2,1,0:T(8,128)(2,1)S(1)} %pad_maximum_fusion.1.rest_0_, ...), custom_call_target="tpu_custom_call" | custom-call | flops 20384317440 | bytes 61152952 | tf_op jit(solution)/shard_map/pallas_call | solution.py:535
  404.1 2.6 shard_map.501
  409.6 3.6 collective-permute-done.45
  419.7 28.5 %collective-permute-done.40 = bf16[4,80,1152]{2,1,0:T(8,128)(2,1)S(1)} collective-permute-done((bf16[4,80,1152]{2,1,0:T(8,128)(2,1)S(1)}, bf16[4,80,1152]{2,1,0:T(8,128)(2,1)S(1)}, u32[]{:S(2)}, u32[]{:S(2)}) %collective-permute-start.40) | collective-permute-done | bytes 737312 | tf_op jit(solution)/shard_map/ppermute | solution.py:593
  454.5 4.3 fusion
  459.5 15.5 %shard_map.500 = (bf16[512,1152]{1,0:T(8,128)(2,1)}, f32[8,1152]{1,0:T(8,128)}) custom-call(s32[8]{0:T(128)} %stack.32.refs_0_.place_ref, bf16[512,3456]{1,0:T(8,128)(2,1)} %get-tuple-element.122.refs_1_, bf16[512,1152]{1,0:T(8,128)(2,1)} %bitcast.527, f32[512,1152]{1,0:T(8,128)} %get-tuple-element.120.refs_3_, ...), custom_call_target="tpu_custom_call" | custom-call | flops 96000000000 | bytes 288000000 | tf_op jit(solution)/shard_map/pallas_call | solution.py:118
  479.9 16.3 %shard_map.502 = (bf16[512,1152]{1,0:T(8,128)(2,1)}, f32[8,1152]{1,0:T(8,128)}) custom-call(s32[8]{0:T(128)} %stack.32.refs_0_.place_ref, bf16[512,4608]{1,0:T(8,128)(2,1)} %get-tuple-element.101.right_ref.refs_1_, bf16[512,1152]{1,0:T(8,128)(2,1)} %bitcast.528, f32[512,1152]{1,0:T(8,128)} %get-tuple-element.102.refs_4_.refs_3_, ...), custom_call_target="tpu_custom_call" | custom-call | flops 102000001024 | bytes 306000000 | tf_op jit(solution)/shard_map/pallas_call | solution.py:118
  505.4 5.3 fusion.46
  510.7 9.1 %collective-permute-done.60 = bf16[4,72,1152]{2,1,0:T(8,128)(2,1)S(1)} collective-permute-done((bf16[4,72,1152]{2,1,0:T(8,128)(2,1)S(1)}, bf16[4,72,1152]{2,1,0:T(8,128)(2,1)S(1)}, u32[]{:S(2)}, u32[]{:S(2)}) %collective-permute-start.60) | collective-permute-done | bytes 663584 | tf_op jit(solution)/shard_map/ppermute | solution.py:593
  529.6 7.8 %convert_bitcast_fusion = (bf16[1,1152,432]{1,2,0:T(8,128)(2,1)}, f32[1152,432]{0,1:T(8,128)}, f32[1,1152,432]{1,2,0:T(8,128)}, f32[1,1152,432]{1,2,0:T(8,128)}) fusion(f32[1,1152,432]{1,2,0:T(8,128)} %param.49, f32[1,1152,432]{1,2,0:T(8,128)} %param.42, f32[1,1152,432]{1,2,0:T(8,128)S(1)} %copy-done.15, pred[]{:T(512)S(6)} %eq.61, ...), kind=kOutput, calls=%fused_computation.107 | convolution fusion | flops 33887232 | bytes 12983041 | tf_op jit(solution)/shard_map/dot_general | solution.py:27
  543.7 10.4 %reduce-scatter.13.cloned.1.call-done = bf16[72,1152]{1,0:T(8,128)(2,1)} async-done(((bf16[288,1152]{1,0:T(8,128)(2,1)}), bf16[72,1152]{1,0:T(8,128)(2,1)}) %reduce-scatter.13.cloned.1.call-update) | async-done | bytes 165904
  555.6 5.4 fusion.45
  563.3 2.5 collective-permute-done.58
  568.7 2.4 collective-permute-done.59
  572.5 2.9 fusion.47
  (383 shorter events, 127.9 us)
Async XLA Ops:
  7.2 67.2 %all-gather.7.cloned.1.call-start = ((), (), s32[]{:S(2)}) async-start(), calls=%async_computation.7 | async-start | bytes 2488320 | tf_op jit(solution)/shard_map/all_gather | solution.py:745
  8.8 14.4 %collective-permute-start.11 = (bf16[72,3456]{1,0:T(8,128)(2,1)S(1)}, bf16[72,3456]{1,0:T(8,128)(2,1)S(1)}, u32[]{:S(2)}, u32[]{:S(2)}) collective-permute-start(bf16[72,3456]{1,0:T(8,128)(2,1)S(1)} %pad_maximum_fusion.11), channel_id=1, source_target_pairs={{0,1},{1,0},{2,3},{3,2},{4,5},{5,4},{6,7},{7,6},{8,9},{9,8},{10,11... | collective-permute-start | bytes 1493000 | tf_op jit(solution)/shard_map/ppermute | solution.py:593
  24.1 125.2 %all-gather.9.cloned.1.call-start = ((), (), s32[]{:S(2)}) async-start(), calls=%async_computation.8 | async-start | bytes 2396160 | tf_op jit(solution)/shard_map/all_gather | solution.py:746
  55.6 21.1 %collective-permute-start.19 = (bf16[208,1152]{1,0:T(8,128)(2,1)S(1)}, bf16[208,1152]{1,0:T(8,128)(2,1)S(1)}, u32[]{:S(2)}, u32[]{:S(2)}) collective-permute-start(bf16[208,1152]{1,0:T(8,128)(2,1)S(1)} %pad_maximum_fusion.6), channel_id=1, source_target_pairs={{0,1},{1,0},{2,3},{3,2},{4,5},{5,4},{6,7},{7,6},{8,9},{9,8},{10,11... | collective-permute-start | bytes 1437704 | tf_op jit(solution)/shard_map/ppermute | solution.py:593
  57.3 12.4 %collective-permute-start.9 = (f32[4,4,432]{2,1,0:T(4,128)S(1)}, f32[4,4,432]{2,1,0:T(4,128)S(1)}, u32[]{:S(2)}, u32[]{:S(2)}) collective-permute-start(f32[4,4,432]{2,1,0:T(4,128)S(1)} %add.440), channel_id=1, source_target_pairs={{0,1},{1,0},{2,3},{3,2},{4,5},{5,4},{6,7},{7,6},{8,9},{9,8},{10,11... | collective-permute-start | bytes 82952 | tf_op jit(solution)/shard_map/ppermute | solution.py:593
  74.4 44.2 %collective-permute-start.13 = (bf16[4,72,3456]{2,1,0:T(8,128)(2,1)}, bf16[4,72,3456]{2,1,0:T(8,128)(2,1)}, u32[]{:S(2)}, u32[]{:S(2)}) collective-permute-start(bf16[4,72,3456]{2,1,0:T(8,128)(2,1)} %bitcast.25.refs_3_.refs_4_.refs_14_.refs_5_), channel_id=1, source_target_pairs={{0,4},{4,0},{1,5},{5,1},{2,6},{6,2},{3,7},{7,3},{8,12},{12,8},{9,1... | collective-permute-start | bytes 5971976 | tf_op jit(solution)/shard_map/ppermute | solution.py:593
  78.8 134.6 %all-gather.11.cloned.1.call-start = ((), (), s32[]{:S(2)}) async-start(), calls=%async_computation.9 | async-start | bytes 2396160 | tf_op jit(solution)/shard_map/all_gather | solution.py:747
  80.0 38.8 %collective-permute-start.12 = (bf16[4,72,1152]{2,1,0:T(8,128)(2,1)S(1)}, bf16[4,72,1152]{2,1,0:T(8,128)(2,1)S(1)}, u32[]{:S(2)}, u32[]{:S(2)}) collective-permute-start(bf16[4,72,1152]{2,1,0:T(8,128)(2,1)S(1)} %slice.355), channel_id=1, source_target_pairs={{0,1},{1,0},{2,3},{3,2},{4,5},{5,4},{6,7},{7,6},{8,9},{9,8},{10,11... | collective-permute-start | bytes 1990664 | tf_op jit(solution)/shard_map/ppermute | solution.py:593
  81.6 72.9 %collective-permute-start.15 = (bf16[4,72,3456]{2,1,0:T(8,128)(2,1)}, bf16[4,72,3456]{2,1,0:T(8,128)(2,1)}, u32[]{:S(2)}, u32[]{:S(2)}) collective-permute-start(bf16[4,72,3456]{2,1,0:T(8,128)(2,1)} %bitcast.25.refs_3_.refs_4_.refs_14_.refs_5_), channel_id=1, source_target_pairs={{0,2},{2,0},{1,3},{3,1},{4,6},{6,4},{5,7},{7,5},{8,10},{10,8},{9,1... | collective-permute-start | bytes 5971976 | tf_op jit(solution)/shard_map/ppermute | solution.py:593
  118.7 35.9 %collective-permute-start.17 = (bf16[4,72,3456]{2,1,0:T(8,128)(2,1)}, bf16[4,72,3456]{2,1,0:T(8,128)(2,1)}, u32[]{:S(2)}, u32[]{:S(2)}) collective-permute-start(bf16[4,72,3456]{2,1,0:T(8,128)(2,1)} %collective-permute-done.13.refs_5_.refs_6_.refs_16_.refs_7_), channel_id=1, source_target_pairs={{0,2},{2,0},{1,3},{3,1},{4,6},{6,4},{5,7},{7,5},{8,10},{10,8},{9,1... | collective-permute-start | bytes 5971976 | tf_op jit(solution)/shard_map/ppermute | solution.py:593
  120.2 17.8 %collective-permute-start.14 = (bf16[4,72,1152]{2,1,0:T(8,128)(2,1)S(1)}, bf16[4,72,1152]{2,1,0:T(8,128)(2,1)S(1)}, u32[]{:S(2)}, u32[]{:S(2)}) collective-permute-start(bf16[4,72,1152]{2,1,0:T(8,128)(2,1)S(1)} %slice.282), channel_id=1, source_target_pairs={{0,1},{1,0},{2,3},{3,2},{4,5},{5,4},{6,7},{7,6},{8,9},{9,8},{10,11... | collective-permute-start | bytes 1990664 | tf_op jit(solution)/shard_map/ppermute | solution.py:593
  124.4 23.4 %collective-permute-start.27 = (bf16[72,3328]{1,0:T(8,128)(2,1)S(1)}, bf16[72,3328]{1,0:T(8,128)(2,1)S(1)}, u32[]{:S(2)}, u32[]{:S(2)}) collective-permute-start(bf16[72,3328]{1,0:T(8,128)(2,1)S(1)} %pad_maximum_fusion.8), channel_id=1, source_target_pairs={{0,1},{1,0},{2,3},{3,2},{4,5},{5,4},{6,7},{7,6},{8,9},{9,8},{10,11... | collective-permute-start | bytes 1437704 | tf_op jit(solution)/shard_map/ppermute | solution.py:593
  128.4 24.7 %collective-permute-start.16 = (bf16[4,72,1152]{2,1,0:T(8,128)(2,1)S(1)}, bf16[4,72,1152]{2,1,0:T(8,128)(2,1)}, u32[]{:S(2)}, u32[]{:S(2)}) collective-permute-start(bf16[4,72,1152]{2,1,0:T(8,128)(2,1)S(1)} %collective-permute-done.12.refs_4_.refs_5_.refs_15_.refs_6_), channel_id=1, source_target_pairs={{0,2},{2,0},{1,3},{3,1},{4,6},{6,4},{5,7},{7,5},{8,10},{10,8},{9,1... | collective-permute-start | bytes 1990664 | tf_op jit(solution)/shard_map/ppermute | solution.py:593
  137.9 16.6 %collective-permute-start.18 = (bf16[4,72,1152]{2,1,0:T(8,128)(2,1)S(1)}, bf16[4,72,1152]{2,1,0:T(8,128)(2,1)S(1)}, u32[]{:S(2)}, u32[]{:S(2)}) collective-permute-start(bf16[4,72,1152]{2,1,0:T(8,128)(2,1)S(1)} %collective-permute-done.14.refs_6_.refs_7_.refs_17_.refs_8_), channel_id=1, source_target_pairs={{0,2},{2,0},{1,3},{3,1},{4,6},{6,4},{5,7},{7,5},{8,10},{10,8},{9,1... | collective-permute-start | bytes 1990664 | tf_op jit(solution)/shard_map/ppermute | solution.py:593
  148.7 302.3 %reduce-scatter.7.cloned.1.call-start = ((), (), s32[]{:S(2)}) async-start(), calls=%async_computation.4 | async-start | bytes 2396160 | tf_op jit(solution)/shard_map/reduce_scatter | solution.py:674
  149.3 43.8 %collective-permute-start.21 = (bf16[4,208,1152]{2,1,0:T(8,128)(2,1)}, bf16[4,208,1152]{2,1,0:T(8,128)(2,1)}, u32[]{:S(2)}, u32[]{:S(2)}) collective-permute-start(bf16[4,208,1152]{2,1,0:T(8,128)(2,1)} %bitcast.30.refs_2_.refs_6_), channel_id=1, source_target_pairs={{0,4},{4,0},{1,5},{5,1},{2,6},{6,2},{3,7},{7,3},{8,12},{12,8},{9,1... | collective-permute-start | bytes 5750792 | tf_op jit(solution)/shard_map/ppermute | solution.py:593
  153.1 40.5 %collective-permute-start.20 = (bf16[4,80,1152]{2,1,0:T(8,128)(2,1)}, bf16[4,80,1152]{2,1,0:T(8,128)(2,1)}, u32[]{:S(2)}, u32[]{:S(2)}) collective-permute-start(bf16[4,80,1152]{2,1,0:T(8,128)(2,1)} %slice.359), channel_id=1, source_target_pairs={{0,1},{1,0},{2,3},{3,2},{4,5},{5,4},{6,7},{7,6},{8,9},{9,8},{10,11... | collective-permute-start | bytes 2211848 | tf_op jit(solution)/shard_map/ppermute | solution.py:593
  193.1 24.6 %collective-permute-start.25 = (bf16[4,208,1152]{2,1,0:T(8,128)(2,1)}, bf16[4,208,1152]{2,1,0:T(8,128)(2,1)}, u32[]{:S(2)}, u32[]{:S(2)}) collective-permute-start(bf16[4,208,1152]{2,1,0:T(8,128)(2,1)} %collective-permute-done.21.refs_4_.refs_8_), channel_id=1, source_target_pairs={{0,2},{2,0},{1,3},{3,1},{4,6},{6,4},{5,7},{7,5},{8,10},{10,8},{9,1... | collective-permute-start | bytes 5750792 | tf_op jit(solution)/shard_map/ppermute | solution.py:593
  193.1 24.6 %collective-permute-start.23 = (bf16[4,208,1152]{2,1,0:T(8,128)(2,1)}, bf16[4,208,1152]{2,1,0:T(8,128)(2,1)}, u32[]{:S(2)}, u32[]{:S(2)}) collective-permute-start(bf16[4,208,1152]{2,1,0:T(8,128)(2,1)} %bitcast.30.refs_2_.refs_6_), channel_id=1, source_target_pairs={{0,2},{2,0},{1,3},{3,1},{4,6},{6,4},{5,7},{7,5},{8,10},{10,8},{9,1... | collective-permute-start | bytes 5750792 | tf_op jit(solution)/shard_map/ppermute | solution.py:593
  194.8 18.6 %collective-permute-start.22 = (bf16[4,80,1152]{2,1,0:T(8,128)(2,1)S(1)}, bf16[4,80,1152]{2,1,0:T(8,128)(2,1)}, u32[]{:S(2)}, u32[]{:S(2)}) collective-permute-start(bf16[4,80,1152]{2,1,0:T(8,128)(2,1)S(1)} %slice.288), channel_id=1, source_target_pairs={{0,1},{1,0},{2,3},{3,2},{4,5},{5,4},{6,7},{7,6},{8,9},{9,8},{10,11... | collective-permute-start | bytes 2211848 | tf_op jit(solution)/shard_map/ppermute | solution.py:593
  196.4 19.8 %collective-permute-start.24 = (bf16[4,80,1152]{2,1,0:T(8,128)(2,1)}, bf16[4,80,1152]{2,1,0:T(8,128)(2,1)}, u32[]{:S(2)}, u32[]{:S(2)}) collective-permute-start(bf16[4,80,1152]{2,1,0:T(8,128)(2,1)} %collective-permute-done.20.refs_3_.refs_7_), channel_id=1, source_target_pairs={{0,2},{2,0},{1,3},{3,1},{4,6},{6,4},{5,7},{7,5},{8,10},{10,8},{9,1... | collective-permute-start | bytes 2211848 | tf_op jit(solution)/shard_map/ppermute | solution.py:593
  214.6 46.4 %collective-permute-start.28 = (bf16[4,72,1280]{2,1,0:T(8,128)(2,1)S(1)}, bf16[4,72,1280]{2,1,0:T(8,128)(2,1)S(1)}, u32[]{:S(2)}, u32[]{:S(2)}) collective-permute-start(bf16[4,72,1280]{2,1,0:T(8,128)(2,1)S(1)} %slice.293), channel_id=1, source_target_pairs={{0,1},{1,0},{2,3},{3,2},{4,5},{5,4},{6,7},{7,6},{8,9},{9,8},{10,11... | collective-permute-start | bytes 2211848 | tf_op jit(solution)/shard_map/ppermute | solution.py:593
  216.2 44.2 %collective-permute-start.29 = (bf16[4,72,3328]{2,1,0:T(8,128)(2,1)}, bf16[4,72,3328]{2,1,0:T(8,128)(2,1)}, u32[]{:S(2)}, u32[]{:S(2)}) collective-permute-start(bf16[4,72,3328]{2,1,0:T(8,128)(2,1)} %bitcast.517), channel_id=1, source_target_pairs={{0,4},{4,0},{1,5},{5,1},{2,6},{6,2},{3,7},{7,3},{8,12},{12,8},{9,1... | collective-permute-start | bytes 5750792 | tf_op jit(solution)/shard_map/ppermute | solution.py:593
  260.4 23.7 %collective-permute-start.33 = (bf16[4,72,3328]{2,1,0:T(8,128)(2,1)}, bf16[4,72,3328]{2,1,0:T(8,128)(2,1)S(1)}, u32[]{:S(2)}, u32[]{:S(2)}) collective-permute-start(bf16[4,72,3328]{2,1,0:T(8,128)(2,1)} %collective-permute-done.29.refs_5_.refs_8_), channel_id=1, source_target_pairs={{0,2},{2,0},{1,3},{3,1},{4,6},{6,4},{5,7},{7,5},{8,10},{10,8},{9,1... | collective-permute-start | bytes 5750792 | tf_op jit(solution)/shard_map/ppermute | solution.py:593
  260.4 23.7 %collective-permute-start.31 = (bf16[4,72,3328]{2,1,0:T(8,128)(2,1)S(1)}, bf16[4,72,3328]{2,1,0:T(8,128)(2,1)S(1)}, u32[]{:S(2)}, u32[]{:S(2)}) collective-permute-start(bf16[4,72,3328]{2,1,0:T(8,128)(2,1)S(1)} %bitcast.520), channel_id=1, source_target_pairs={{0,2},{2,0},{1,3},{3,1},{4,6},{6,4},{5,7},{7,5},{8,10},{10,8},{9,1... | collective-permute-start | bytes 5750792 | tf_op jit(solution)/shard_map/ppermute | solution.py:593
  262.4 18.5 %collective-permute-start.30 = (bf16[4,72,1280]{2,1,0:T(8,128)(2,1)S(1)}, bf16[4,72,1280]{2,1,0:T(8,128)(2,1)S(1)}, u32[]{:S(2)}, u32[]{:S(2)}) collective-permute-start(bf16[4,72,1280]{2,1,0:T(8,128)(2,1)S(1)} %slice.294), channel_id=1, source_target_pairs={{0,1},{1,0},{2,3},{3,2},{4,5},{5,4},{6,7},{7,6},{8,9},{9,8},{10,11... | collective-permute-start | bytes 2211848 | tf_op jit(solution)/shard_map/ppermute | solution.py:593
  262.9 18.5 %collective-permute-start.32 = (bf16[4,72,1280]{2,1,0:T(8,128)(2,1)S(1)}, bf16[4,72,1280]{2,1,0:T(8,128)(2,1)S(1)}, u32[]{:S(2)}, u32[]{:S(2)}) collective-permute-start(bf16[4,72,1280]{2,1,0:T(8,128)(2,1)S(1)} %collective-permute-done.28.refs_4_.refs_7_), channel_id=1, source_target_pairs={{0,2},{2,0},{1,3},{3,1},{4,6},{6,4},{5,7},{7,5},{8,10},{10,8},{9,1... | collective-permute-start | bytes 2211848 | tf_op jit(solution)/shard_map/ppermute | solution.py:593
  280.9 21.7 %collective-permute-start.35 = (bf16[2,4,72,4608]{3,2,1,0:T(8,128)(2,1)}, bf16[2,4,72,4608]{3,2,1,0:T(8,128)(2,1)}, u32[]{:S(2)}, u32[]{:S(2)}) collective-permute-start(bf16[2,4,72,4608]{3,2,1,0:T(8,128)(2,1)} %bitcast.521), channel_id=1, source_target_pairs={{0,2},{2,0},{1,3},{3,1},{4,6},{6,4},{5,7},{7,5},{8,10},{10,8},{9,1... | collective-permute-start | bytes 15925256 | tf_op jit(solution)/shard_map/ppermute | solution.py:593
  307.3 39.6 %collective-permute-start.39 = (bf16[2,4,72,1280]{3,2,1,0:T(8,128)(2,1)}, bf16[2,4,72,1280]{3,2,1,0:T(8,128)(2,1)}, u32[]{:S(2)}, u32[]{:S(2)}) collective-permute-start(bf16[2,4,72,1280]{3,2,1,0:T(8,128)(2,1)} %get-tuple-element.161.rest_1_), channel_id=1, source_target_pairs={{0,1},{1,0},{2,3},{3,2},{4,5},{5,4},{6,7},{7,6},{8,9},{9,8},{10,11... | collective-permute-start | bytes 4423688 | tf_op jit(solution)/shard_map/ppermute | solution.py:593
  310.4 75.3 %collective-permute-start.41 = (bf16[4,72,2048]{2,1,0:T(8,128)(2,1)}, bf16[4,72,2048]{2,1,0:T(8,128)(2,1)}, u32[]{:S(2)}, u32[]{:S(2)}) collective-permute-start(bf16[4,72,2048]{2,1,0:T(8,128)(2,1)} %fusion.29.rest_0_), channel_id=1, source_target_pairs={{0,4},{4,0},{1,5},{5,1},{2,6},{6,2},{3,7},{7,3},{8,12},{12,8},{9,1... | collective-permute-start | bytes 3538952 | tf_op jit(solution)/shard_map/ppermute | solution.py:593
  323.2 26.3 %collective-permute-start.36 = (bf16[2,4,288,1152]{3,2,1,0:T(8,128)(2,1)}, bf16[2,4,288,1152]{3,2,1,0:T(8,128)(2,1)}, u32[]{:S(2)}, u32[]{:S(2)}) collective-permute-start(bf16[2,4,288,1152]{3,2,1,0:T(8,128)(2,1)} %bitcast.522), channel_id=1, source_target_pairs={{0,2},{2,0},{1,3},{3,1},{4,6},{6,4},{5,7},{7,5},{8,10},{10,8},{9,1... | collective-permute-start | bytes 15925256 | tf_op jit(solution)/shard_map/ppermute | solution.py:593
  349.1 35.1 %collective-permute-start.42 = (bf16[4,72,1280]{2,1,0:T(8,128)(2,1)}, bf16[4,72,1280]{2,1,0:T(8,128)(2,1)}, u32[]{:S(2)}, u32[]{:S(2)}) collective-permute-start(bf16[4,72,1280]{2,1,0:T(8,128)(2,1)} %fusion.39.refs_5_), channel_id=1, source_target_pairs={{0,4},{4,0},{1,5},{5,1},{2,6},{6,2},{3,7},{7,3},{8,12},{12,8},{9,1... | collective-permute-start | bytes 2211848 | tf_op jit(solution)/shard_map/ppermute | solution.py:593
  352.1 41.4 %collective-permute-start.37 = (bf16[4,128,1152]{2,1,0:T(8,128)(2,1)}, bf16[4,128,1152]{2,1,0:T(8,128)(2,1)}, u32[]{:S(2)}, u32[]{:S(2)}) collective-permute-start(bf16[4,128,1152]{2,1,0:T(8,128)(2,1)} %fusion.31.refs_3_), channel_id=1, source_target_pairs={{0,4},{4,0},{1,5},{5,1},{2,6},{6,2},{3,7},{7,3},{8,12},{12,8},{9,1... | collective-permute-start | bytes 3538952 | tf_op jit(solution)/shard_map/ppermute | solution.py:593
  358.1 38.0 %collective-permute-start.38 = (bf16[2,4,80,1152]{3,2,1,0:T(8,128)(2,1)}, bf16[2,4,80,1152]{3,2,1,0:T(8,128)(2,1)}, u32[]{:S(2)}, u32[]{:S(2)}) collective-permute-start(bf16[2,4,80,1152]{3,2,1,0:T(8,128)(2,1)} %get-tuple-element.162.refs_4_), channel_id=1, source_target_pairs={{0,1},{1,0},{2,3},{3,2},{4,5},{5,4},{6,7},{7,6},{8,9},{9,8},{10,11... | collective-permute-start | bytes 4423688 | tf_op jit(solution)/shard_map/ppermute | solution.py:593
  404.0 48.6 %collective-permute-start.43 = (bf16[3,2,4,72,1152]{4,3,2,1,0:T(8,128)(2,1)}, bf16[3,2,4,72,1152]{4,3,2,1,0:T(8,128)(2,1)}, u32[]{:S(2)}, u32[]{:S(2)}) collective-permute-start(bf16[3,2,4,72,1152]{4,3,2,1,0:T(8,128)(2,1)} %bitcast.523), channel_id=1, source_target_pairs={{0,2},{2,0},{1,3},{3,1},{4,6},{6,4},{5,7},{7,5},{8,10},{10,8},{9,1... | collective-permute-start | bytes 11943944 | tf_op jit(solution)/shard_map/ppermute | solution.py:593
  407.1 91.2 %reduce-scatter.9.cloned.1.call-start = ((), (), s32[]{:S(2)}) async-start(), calls=%async_computation.5 | async-start | bytes 2396160 | tf_op jit(solution)/shard_map/reduce_scatter | solution.py:674
  415.3 59.8 %collective-permute-start.46 = (bf16[4,72,1152]{2,1,0:T(8,128)(2,1)}, bf16[4,72,1152]{2,1,0:T(8,128)(2,1)}, u32[]{:S(2)}, u32[]{:S(2)}) collective-permute-start(bf16[4,72,1152]{2,1,0:T(8,128)(2,1)} %fusion.19), channel_id=1, source_target_pairs={{0,4},{4,0},{1,5},{5,1},{2,6},{6,2},{3,7},{7,3},{8,12},{12,8},{9,1... | collective-permute-start | bytes 1990664 | tf_op jit(solution)/shard_map/ppermute | solution.py:593
  415.7 32.5 %collective-permute-start.40 = (bf16[4,80,1152]{2,1,0:T(8,128)(2,1)S(1)}, bf16[4,80,1152]{2,1,0:T(8,128)(2,1)S(1)}, u32[]{:S(2)}, u32[]{:S(2)}) collective-permute-start(bf16[4,80,1152]{2,1,0:T(8,128)(2,1)S(1)} %fusion.41.rest_1_), channel_id=1, source_target_pairs={{0,4},{4,0},{1,5},{5,1},{2,6},{6,2},{3,7},{7,3},{8,12},{12,8},{9,1... | collective-permute-start | bytes 2211848 | tf_op jit(solution)/shard_map/ppermute | solution.py:593
  451.0 78.5 %reduce-scatter.11.cloned.1.call-start = ((), (), s32[]{:S(2)}) async-start(), calls=%async_computation.6 | async-start | bytes 1658880 | tf_op jit(solution)/shard_map/reduce_scatter | solution.py:674
  451.1 47.5 %collective-permute-start.63 = (bf16[72,3328]{1,0:T(8,128)(2,1)}, bf16[72,3328]{1,0:T(8,128)(2,1)}, u32[]{:S(2)}, u32[]{:S(2)}) collective-permute-start(bf16[72,3328]{1,0:T(8,128)(2,1)} %reduce-scatter.7.cloned.1.call-done), channel_id=1, source_target_pairs={{0,1},{1,0},{2,3},{3,2},{4,5},{5,4},{6,7},{7,6},{8,9},{9,8},{10,11... | collective-permute-start | bytes 1437704 | tf_op jit(solution)/shard_map/ppermute | solution.py:593
  453.9 23.5 %collective-permute-start.44 = (bf16[4,72,1152]{2,1,0:T(8,128)(2,1)S(1)}, bf16[4,72,1152]{2,1,0:T(8,128)(2,1)S(1)}, u32[]{:S(2)}, u32[]{:S(2)}) collective-permute-start(bf16[4,72,1152]{2,1,0:T(8,128)(2,1)S(1)} %fusion.21.refs_13_), channel_id=1, source_target_pairs={{0,4},{4,0},{1,5},{5,1},{2,6},{6,2},{3,7},{7,3},{8,12},{12,8},{9,1... | collective-permute-start | bytes 1990664 | tf_op jit(solution)/shard_map/ppermute | solution.py:593
  458.8 38.3 %collective-permute-start.47 = (bf16[2,4,72,1152]{3,2,1,0:T(8,128)(2,1)}, bf16[2,4,72,1152]{3,2,1,0:T(8,128)(2,1)}, u32[]{:S(2)}, u32[]{:S(2)}) collective-permute-start(bf16[2,4,72,1152]{3,2,1,0:T(8,128)(2,1)} %get-tuple-element.167.refs_14_), channel_id=1, source_target_pairs={{0,1},{1,0},{2,3},{3,2},{4,5},{5,4},{6,7},{7,6},{8,9},{9,8},{10,11... | collective-permute-start | bytes 3981320 | tf_op jit(solution)/shard_map/ppermute | solution.py:593
  498.4 55.7 %reduce-scatter.13.cloned.1.call-start = ((), (), s32[]{:S(2)}) async-start(), calls=%async_computation.10 | async-start | bytes 829440
  502.4 17.3 %collective-permute-start.60 = (bf16[4,72,1152]{2,1,0:T(8,128)(2,1)S(1)}, bf16[4,72,1152]{2,1,0:T(8,128)(2,1)S(1)}, u32[]{:S(2)}, u32[]{:S(2)}) collective-permute-start(bf16[4,72,1152]{2,1,0:T(8,128)(2,1)S(1)} %fusion.43), channel_id=1, source_target_pairs={{0,4},{4,0},{1,5},{5,1},{2,6},{6,2},{3,7},{7,3},{8,12},{12,8},{9,1... | collective-permute-start | bytes 1990664 | tf_op jit(solution)/shard_map/ppermute | solution.py:593
  503.9 16.2 %collective-permute-start.50 = (f32[4,4,432]{2,1,0:T(4,128)S(1)}, f32[4,4,432]{2,1,0:T(4,128)S(1)}, u32[]{:S(2)}, u32[]{:S(2)}) collective-permute-start(f32[4,4,432]{2,1,0:T(4,128)S(1)} %add.469), channel_id=1, source_target_pairs={{0,4},{4,0},{1,5},{5,1},{2,6},{6,2},{3,7},{7,3},{8,12},{12,8},{9,1... | collective-permute-start | bytes 82952 | tf_op jit(solution)/shard_map/ppermute | solution.py:593
  526.2 12.7 %collective-permute-start.62 = (bf16[208,1152]{1,0:T(8,128)(2,1)}, bf16[208,1152]{1,0:T(8,128)(2,1)}, u32[]{:S(2)}, u32[]{:S(2)}) collective-permute-start(bf16[208,1152]{1,0:T(8,128)(2,1)} %reduce-scatter.9.cloned.1.call-done), channel_id=1, source_target_pairs={{0,1},{1,0},{2,3},{3,2},{4,5},{5,4},{6,7},{7,6},{8,9},{9,8},{10,11... | collective-permute-start | bytes 1437704 | tf_op jit(solution)/shard_map/ppermute | solution.py:593
  541.2 14.3 %collective-permute-start.56 = (f32[4,1152]{1,0:T(4,128)S(1)}, f32[4,1152]{1,0:T(4,128)S(1)}, u32[]{:S(2)}, u32[]{:S(2)}) collective-permute-start(f32[4,1152]{1,0:T(4,128)S(1)} %add.472), channel_id=1, source_target_pairs={{0,4},{4,0},{1,5},{5,1},{2,6},{6,2},{3,7},{7,3},{8,12},{12,8},{9,1... | collective-permute-start | bytes 55304 | tf_op jit(solution)/shard_map/ppermute | solution.py:593
  554.1 8.6 %collective-permute-start.61 = (bf16[72,1152]{1,0:T(8,128)(2,1)}, bf16[72,1152]{1,0:T(8,128)(2,1)S(1)}, u32[]{:S(2)}, u32[]{:S(2)}) collective-permute-start(bf16[72,1152]{1,0:T(8,128)(2,1)} %reduce-scatter.13.cloned.1.call-done), channel_id=1, source_target_pairs={{0,1},{1,0},{2,3},{3,2},{4,5},{5,4},{6,7},{7,6},{8,9},{9,8},{10,11... | collective-permute-start | bytes 497672 | tf_op jit(solution)/shard_map/ppermute | solution.py:593
  (99 other events, 842.1 us)
Sparse Core Ops, SparseCore 0:
  24.2 47.2 all-gather.6
  78.9 41.3 all-gather.8
  148.9 42.3 all-gather.10
  407.3 39.4 reduce-scatter.6
  451.2 39.5 reduce-scatter.8
  498.5 30.9 reduce-scatter.10
  532.4 21.6 reduce-scatter.12

commit v4 on v3

--- a/solution.py
+++ b/solution.py
@@ -544,7 +544,7 @@
         + [any_spec()] * n_dep,
         out_specs=[pl.BlockSpec((row_block, col_block), lambda j, i: (i, j))] * 2,
         compiler_params=pltpu.CompilerParams(vmem_limit_bytes=40 * 2**20),
-        cost_estimate=cost(rows * cols * depth / 3e8),
+        cost_estimate=cost(0.5),
     )(left, left, right, *ordered_after)
 
 
@@ -647,7 +647,8 @@
     near_late = swap(cut(after(near, *before_near_late)), "x")
     far_late = swap(cut(after(far, near_late, *before_late)), "x")
     pieces = [near, near_late, far, far_late]
-    return pieces + [swap(after(piece, *before_core), "c") for piece in pieces]
+    held = [(), before_late, before_late, before_core]
+    return pieces + [swap(after(piece, *hold), "c") for piece, hold in zip(pieces, held)]
 
 
 def core_sum(keep, send, cut, x):
@@ -760,34 +761,34 @@
         us=1,
     )
     firsts = gather_pieces(
-        first_near, lambda main: main[:, :, 2 * width :], (mods,), (), ()
+        first_near, lambda main: main[:, :, 2 * width :], (d_mlp_rel,), (), (up_near,)
     )
     h1, qkv = run_kernel(
         qkv_kernel,
         [spot] + in_vmem(tokens, mods) + in_place(firsts),
         [((rows, width), BF16), ((48, span, rows), BF16)],
         [vmem(48, span, width), sems(48)],
-        us=18,
-        ordered_after=[d_mlp_rel],
+        us=2,
+        ordered_after=[d_mlp_rel, down_near],
     )
     attended, branch, h2 = run_kernel(
         attend_kernel,
         [spot] + in_vmem(qkv, tokens, mods) + in_place(firsts),
         [((rows, width), BF16), ((rows, width), F32), ((rows, width), BF16)],
         [vmem(16, span, width), vmem(16, span, rows, dtype=F32), sems(16)],
-        us=20,
-    )
-    ups = gather_pieces(up_near, lambda main: main[:, UP_E:], firsts[:1], (), (h1,), (h2,))
+        us=2,
+    )
+    ups = gather_pieces(up_near, lambda main: main[:, UP_E:], firsts[:1], firsts[3:4], (h1,), (h2,))
     act, slope = run_kernel(
         up_kernel,
         [spot] + in_vmem(h2) + in_place(ups),
         [((rows, FF), BF16, pl.BlockSpec((rows, width), lambda i: (0, i)))] * 2,
         [vmem(FF, width)] + [vmem(rows, WIDE, dtype=F32)] * 2 + [sems(48)],
         steps=4,
-        us=15,
+        us=2,
     )
     down_keep, down_send = pair_grads(d_mlp_rel.reshape(2, 8 * span, rows), act)
-    downs = gather_pieces(down_near, lambda main: main[:, :, DOWN_E:], (h1,), (h2,), (act,), (down_keep,))
+    downs = gather_pieces(down_near, lambda main: main[:, :, DOWN_E:], (), (h2,), (act,), (down_keep,))
     cut_down = lambda v: (
         v[..., :DOWN_E],
         v[..., DOWN_E : DOWN_E + DOWN_L],
@@ -843,28 +844,29 @@
     merge_halves = [add_low(merge_keep[i], merge_got[i]) for i in range(2)]
 
     down_late = late_sum(*down_late, (d_middle,))
+    down_over_early = over_y(down_early)
+    down_part = over_z(down_over_early)
     d_qkv, d_qkv_rel = run_kernel(
         attend_back_kernel,
         [spot] + in_vmem(qkv, d_att),
         [((rows, 3 * width), BF16), ((2, 3, 8, span, rows), BF16)],
         [vmem(16, span, rows, dtype=F32)] * 3,
-        ordered_after=[up_early[1], up_late[1], down_late[1]],
+        ordered_after=[up_early[1], up_late[1], down_late[1], down_over_early],
         us=25,
     )
     up_late = late_sum(*up_late, (d_qkv,))
-    down_total = jnp.concatenate(
-        [over_y(down_early, (d_qkv,)), over_y(down_late, (d_qkv,))], axis=-1
-    )
+    down_over = over_y(down_late, (d_qkv,))
     up_over = over_y(up_early)
     attend_keep, attend_send = pair_grads(
-        d_qkv_rel.reshape(2, 24 * span, rows), h1, [down_total, up_late[1], up_over]
+        d_qkv_rel.reshape(2, 24 * span, rows), h1, [down_over, up_late[1], up_over]
     )
     cut_attend = lambda v: (v[0], v[1], v[2])
     shape = (3, 2, 4, span, width)
     first_early, *first_late = core_sum(
         attend_keep.reshape(shape), attend_send.reshape(shape), cut_attend, x
     )
-    down_part = over_z(down_total)
+    down_late_part = over_z(after(down_over, down_part))
+    up_part = over_z(after(up_over, down_late_part))
 
     input_grad, sums_one = run_kernel(
         input_back_kernel,
@@ -874,9 +876,9 @@
         + [vmem(8, width, dtype=F32)] * 2
         + [sems(48)],
         ordered_after=[first_early[1], first_late[1]],
-        us=16,
-    )
-    up_total = jnp.concatenate([up_over, over_y(up_late)], axis=1)
+        us=3,
+    )
+    up_late_over = over_y(up_late, (input_grad,))
     early_total = jnp.concatenate(
         [over_y(halves, (input_grad,)) for halves in (first_early, merge_halves)], axis=2
     )
@@ -890,25 +892,34 @@
             vmem(8, width, dtype=F32),
             sems(48),
         ],
-        ordered_after=[up_total, early_total],
-        us=17,
-    )
-    up_part = over_z(after(up_total, down_part))
+        ordered_after=[up_late_over, early_total],
+        us=3,
+    )
+    up_late_part = over_z(after(up_late_over, up_part))
     first_late = late_sum(*first_late, (block_out,))
-    early_part = over_z(after(early_total, up_part))
-    late_part = over_z(after(over_y(first_late), up_part))
-    down_got, up_got = swap(down_part, "x"), swap(up_part, "x")
-    early_got, late_got = swap(early_part, "x"), swap(late_part, "x")
+    early_part = over_z(after(early_total, up_late_part))
+    first_late_over = over_y(first_late)
+    late_part = over_z(after(first_late_over, early_part))
+
+    def ends(part, late):
+        early = part.astype(F32) + swap(part, "x").astype(F32)
+        other = swap(late, "x")
+        first = x == 0
+        return early, jnp.where(first, late, other), jnp.where(first, other, late)
+
+    down_ends = ends(down_part, down_late_part)
+    up_ends = ends(up_part, up_late_part)
+    first_ends = ends(early_part, late_part)
 
     d_vector = jnp.concatenate([sums_one[:2], sums_two[:3], sums_out[:1]]).reshape(6 * width)
-    d_mod = sum_plane(after(d_vector, up_part, first_late[1]).reshape(4, 4, mod_span))
+    d_mod = sum_plane(after(d_vector, first_late_over).reshape(4, 4, mod_span))
     d_mod = lax.dynamic_index_in_dim(d_mod, y * 2 + c, 1, keepdims=False)
     d_mod = turn_z(d_mod, z)
     grad_mod = contract_rows(d_mod, cond_act.astype(F32), HIGHEST)
     d_cond_part = jnp.dot(
         d_mod, own_low[2].astype(F32), precision=HIGHEST, preferred_element_type=F32
     )
-    d_cond_act = sum_all(after(jnp.where(own[2], d_cond_part, 0.0), early_part))
+    d_cond_act = sum_all(after(jnp.where(own[2], d_cond_part, 0.0), late_part))
     d_cond = silu_back(d_cond_act)[0]
     d_time_pre = jax.vjp(jax.nn.silu, time_pre)[1](d_cond)[0]
     d_cond_block = lax.dynamic_slice_in_dim(d_cond, block * span, span, 1)
@@ -916,41 +927,14 @@
     grad_table = contract_rows(d_cond_block, one_hot.astype(F32), HIGHEST)
     grad_time = contract_rows(d_time_block, features.astype(F32), HIGHEST)
 
-    def joined(early, part, got, axis):
-        first = x == 0
-        halves = [jnp.where(first, part, got), jnp.where(first, got, part)]
-        return jnp.concatenate([early.astype(BF16)] + halves, axis=axis).astype(F32)
-
-    def both(part, got):
-        return part.astype(F32) + got.astype(F32)
-
     grads = (
         grad_time,
         grad_table,
         grad_mod,
-        jnp.concatenate(
-            [
-                both(early_part[:, :width], early_got[:, :width]),
-                jnp.where(x == 0, late_part, late_got).astype(F32),
-                jnp.where(x == 0, late_got, late_part).astype(F32),
-            ]
-        ),
-        both(early_part[:, width:], early_got[:, width:]),
-        jnp.concatenate(
-            [
-                both(up_part[:UP_E], up_got[:UP_E]),
-                jnp.where(x == 0, up_part[UP_E:], up_got[UP_E:]).astype(F32),
-                jnp.where(x == 0, up_got[UP_E:], up_part[UP_E:]).astype(F32),
-            ]
-        ),
-        jnp.concatenate(
-            [
-                both(down_part[:, :DOWN_E], down_got[:, :DOWN_E]),
-                jnp.where(x == 0, down_part[:, DOWN_E:], down_got[:, DOWN_E:]).astype(F32),
-                jnp.where(x == 0, down_got[:, DOWN_E:], down_part[:, DOWN_E:]).astype(F32),
-            ],
-            axis=1,
-        ),
+        jnp.concatenate([first_ends[0][:, :width], *first_ends[1:]]),
+        first_ends[0][:, width:],
+        jnp.concatenate(up_ends),
+        jnp.concatenate(down_ends, axis=1),
     )
     rates = [
         0.5 * FREQ ** (-0.5),

time: 588 us -> 545 us (0.927)
  waiting for transfers between devices: 219 us -> 165 us
  starting transfers between devices: 63.5 us -> 74.1 us
  other arithmetic: 69.2 us -> 76.3 us
    ppermute x54 -> x56, waiting for transfers between devices: 196 us -> 75.9 us  [swap(): return lax.ppermute(value, axis, [(0, 1), (1, 0)])]
    all_gather x1, waiting for transfers between devices: 0.02 us -> 31.8 us  [on_grid(): up_near = lax.all_gather(up_mine, 'z', axis=0, tiled=False)]
    all_gather x1, waiting for transfers between devices: 0.01 us -> 20 us  [on_grid(): down_near = lax.all_gather(down_mine, 'z', axis=0, tiled=False)]
    reduce_scatter x3 -> x5, waiting for transfers between devices: 1.16 us -> 18.6 us  [over_z(): part = lax.psum_scatter(flat, 'z', scatter_dimension=0, tiled=True)]
    ppermute x54 -> x56, starting transfers between devices: 47.7 us -> 56.5 us  [swap(): return lax.ppermute(value, axis, [(0, 1), (1, 0)])]
  transfers between devices with their start and end apart: 71 -> 75, of which waited for: 30 -> 32; matrix products, arithmetic and copies ran while one was open for 15% -> 17% of each run, Pallas kernels for 28% -> 31%
where the time goes in v4:
time: 545 us; the launch traced here: 540 us
  Pallas kernels  168 us (31%)
  waiting for transfers between devices  165 us (30%)
  other arithmetic  76.3 us (14%)
  starting transfers between devices  74.1 us (14%)
  local copies, waits for them, and re-layouts  26 us (5%)
  between operations  20 us (4%)
  matrix products  10.7 us (2%)
    pallas_call x9, Pallas kernels, run_kernel(): pl.pallas_call(kernel, grid=() if steps is None else (steps,), out_shape=...  142 us
    ppermute x56, waiting for transfers between devices, swap(): return lax.ppermute(value, axis, [(0, 1), (1, 0)])  75.9 us
    ppermute x56, starting transfers between devices, swap(): return lax.ppermute(value, axis, [(0, 1), (1, 0)])  56.5 us
    convert_element_type x17, other arithmetic, add_low(): return total.astype(BF16)  43.6 us
    all_gather x1, waiting for transfers between devices, on_grid(): up_near = lax.all_gather(up_mine, 'z', axis=0, tiled=False)  31.8 us
    all_gather x1, waiting for transfers between devices, on_grid(): down_near = lax.all_gather(down_mine, 'z', axis=0, tiled=False)  20 us
    reduce_scatter x5, waiting for transfers between devices, over_z(): part = lax.psum_scatter(flat, 'z', scatter_dimension=0, tiled=True)  18.6 us
    pallas_call x3, Pallas kernels, pair_grads(): pl.pallas_call(kernel, grid=grid, out_shape=[jax.ShapeDtypeStruct((rows,...  17.3 us
  transfers between devices with their start and end apart: 75, of which 32 were waited for; matrix products, arithmetic and copies ran while one was open for 17% of the time, Pallas kernels for 31%

profile of v4, /device:TPU:0, one launch (start us, length us, event | category | flops | bytes accessed | tf_op | source)
XLA Modules:
  0.0 540.1 jit_solution(1481012900270335476)
XLA Ops:
  8.8 3.0 collective-permute-start.11
  15.8 7.3 %collective-permute-done.11 = bf16[72,3456]{1,0:T(8,128)(2,1)S(1)} collective-permute-done((bf16[72,3456]{1,0:T(8,128)(2,1)S(1)}, bf16[72,3456]{1,0:T(8,128)(2,1)S(1)}, u32[]{:S(2)}, u32[]{:S(2)}) %collective-permute-start.11) | collective-permute-done | bytes 497696 | tf_op jit(solution)/shard_map/ppermute | solution.py:593
  34.6 3.1 collective-permute-done.3
  37.8 2.6 collective-permute-start.4
  44.3 2.7 collective-permute-start.5
  47.0 3.7 collective-permute-start.6
  55.0 4.5 collective-permute-done.14
  71.5 3.5 shard_map.490
  80.9 2.4 collective-permute-start.12
  83.3 31.8 %all-gather.9.cloned.1.call-done = bf16[832,1152]{1,0:T(8,128)(2,1)} async-done(((bf16[208,1152]{1,0:T(8,128)(2,1)}), bf16[832,1152]{1,0:T(8,128)(2,1)}) %all-gather.9.cloned.1.call-update) | async-done | bytes 1916944 | tf_op jit(solution)/shard_map/all_gather | solution.py:747
  120.8 14.5 %collective-permute-done.15.refs_6_.refs_7_.refs_17_.refs_8_ = bf16[4,72,1152]{2,1,0:T(8,128)(2,1)} collective-permute-done((bf16[4,72,1152]{2,1,0:T(8,128)(2,1)S(1)}, bf16[4,72,1152]{2,1,0:T(8,128)(2,1)}, u32[]{:S(2)}, u32[]{:S(2)}) %collective-permute-start.15) | collective-permute-done | bytes 663584 | tf_op jit(solution)/shard_map/ppermute | solution.py:593
  138.9 20.0 %all-gather.11.cloned.1.call-done = bf16[288,3328]{1,0:T(8,128)(2,1)} async-done(((bf16[72,3328]{1,0:T(8,128)(2,1)}), bf16[288,3328]{1,0:T(8,128)(2,1)}) %all-gather.11.cloned.1.call-update) | async-done | bytes 1916944 | tf_op jit(solution)/shard_map/all_gather | solution.py:748
  158.9 14.0 %shard_map.491 = (bf16[512,1152]{1,0:T(8,128)(2,1)}, bf16[48,72,512]{2,1,0:T(8,128)(2,1)}) custom-call(s32[8]{0:T(128)} %stack.32.refs_0_.place_ref, bf16[512,1152]{1,0:T(8,128)(2,1)} %bitcast.537, f32[8,1152]{1,0:T(8,128)} %concatenate.59.refs_2_.refs_3_.refs_5_.refs_4_, bf16[4,72,3456]{2,1,0:T(8,128)(2,1)} %bitcast.529, ...), custom_call_target="tpu_custom_call" | custom-call | flops 12000000000 | bytes 36000000 | tf_op jit(solution)/shard_map/pallas_call | solution.py:118
  177.5 15.4 %shard_map.492 = (bf16[512,1152]{1,0:T(8,128)(2,1)}, f32[512,1152]{1,0:T(8,128)}, bf16[512,1152]{1,0:T(8,128)(2,1)}) custom-call(s32[8]{0:T(128)} %stack.32.refs_0_.place_ref, bf16[48,72,512]{2,1,0:T(8,128)(2,1)} %get-tuple-element.97.refs_1_, bf16[512,1152]{1,0:T(8,128)(2,1)} %bitcast.538, f32[8,1152]{1,0:T(8,128)} %concatenate.59.refs_2_.refs_3_.refs_5_.refs_4_, ...), custom_call_target="tpu_custom_call" | custom-call | flops 12000000000 | bytes 36000000 | tf_op jit(solution)/shard_map/pallas_call | solution.py:118
  199.0 15.0 %shard_map.493 = (bf16[512,4608]{1,0:T(8,128)(2,1)}, bf16[512,4608]{1,0:T(8,128)(2,1)}) custom-call(s32[8]{0:T(128)} %stack.32.refs_0_.place_ref, bf16[512,1152]{1,0:T(8,128)(2,1)} %get-tuple-element.98.refs_1_.right_ref, bf16[4,208,1152]{2,1,0:T(8,128)(2,1)} %bitcast.30.refs_2_.refs_6_, bf16[4,80,1152]{2,1,0:T(8,128)(2,1)} %copy-done.56, ...), custom_call_target="tpu_custom_call" | custom-call | flops 12000000000 | bytes 36000000 | tf_op jit(solution)/shard_map/pallas_call | solution.py:118
  214.0 3.3 collective-permute-done.29.refs_5_.refs_8_
  220.5 2.3 copy-done.11
  222.8 9.1 %shard_map.494 = (bf16[576,4608]{1,0:T(8,128)(2,1)S(1)}, bf16[576,4608]{1,0:T(8,128)(2,1)}) custom-call(bf16[2,576,512]{2,1,0:T(8,128)(2,1)S(1)} %bitcast.501, bf16[2,576,512]{2,1,0:T(8,128)(2,1)S(1)} %bitcast.502, bf16[512,4608]{1,0:T(8,128)(2,1)S(1)} %copy-done.11), custom_call_target="tpu_custom_call" | custom-call | flops 3000000000 | bytes 9000000 | tf_op jit(solution)/shard_map/pallas_call | solution.py:535
  232.0 5.7 %collective-permute-done.30.refs_6_.refs_9_ = bf16[4,72,1280]{2,1,0:T(8,128)(2,1)S(1)} collective-permute-done((bf16[4,72,1280]{2,1,0:T(8,128)(2,1)S(1)}, bf16[4,72,1280]{2,1,0:T(8,128)(2,1)S(1)}, u32[]{:S(2)}, u32[]{:S(2)}) %collective-permute-start.30) | collective-permute-done | bytes 737312 | tf_op jit(solution)/shard_map/ppermute | solution.py:593
  238.6 2.4 collective-permute-done.34.refs_10_.refs_13_
  241.8 15.6 %shard_map.495 = (bf16[512,4608]{1,0:T(8,128)(2,1)}, bf16[4608,512]{1,0:T(8,128)(2,1)}) custom-call(s32[8]{0:T(128)} %stack.32.refs_0_.place_ref, bf16[512,1152]{1,0:T(8,128)(2,1)} %get-tuple-element.114.refs_1_, bf16[512,4608]{1,0:T(8,128)(2,1)} %get-tuple-element.115.refs_2_, bf16[4,72,3328]{2,1,0:T(8,128)(2,1)} %bitcast.522, ...), custom_call_target="tpu_custom_call" | custom-call | flops 96000000000 | bytes 288000000 | tf_op jit(solution)/shard_map/pallas_call | solution.py:118
  257.5 2.8 fusion.29.rest_0_
  261.8 4.5 add_convert_fusion
  267.8 8.9 %shard_map.496 = (bf16[8,288,1152]{2,1,0:T(8,128)(2,1)S(1)}, bf16[8,288,1152]{2,1,0:T(8,128)(2,1)}) custom-call(s32[8]{0:T(128)S(1)} %copy-done.6, bf16[4608,512]{1,0:T(8,128)(2,1)S(1)} %bitcast.506, bf16[4608,512]{1,0:T(8,128)(2,1)S(1)} %bitcast.506, bf16[512,1152]{1,0:T(8,128)(2,1)S(1)} %copy-done.13, bf16[4,72,2048]{2,1,0:T(8,128)(2,1)} %fusion.29.rest_0_, ...), custom_call_target="tpu_custom_call" | custom-call | flops 54000001024 | bytes 162000000 | tf_op jit(solution)/shard_map/pallas_call | solution.py:568
  276.7 2.4 copy-done
  279.1 22.6 %shard_map.497 = (f32[512,1152]{1,0:T(8,128)}, bf16[512,1152]{1,0:T(8,128)(2,1)}, bf16[2,8,72,512]{3,2,1,0:T(8,128)(2,1)}, bf16[16,72,512]{2,1,0:T(8,128)(2,1)}, f32[8,1152]{1,0:T(8,128)}) custom-call(s32[8]{0:T(128)} %stack.32.refs_0_.place_ref, bf16[512,4608]{1,0:T(8,128)(2,1)} %get-tuple-element.120.refs_1_, bf16[512,1152]{1,0:T(8,128)(2,1)} %bitcast.539, ...), custom_call_target="tpu_custom_call" | custom-call | flops 143999991808 | bytes 432000000 | tf_op jit(solution)/shard_map/pallas_call | solution.py:118
  301.7 3.8 fusion.3.refs_6_
  308.5 3.0 fusion.30.refs_3_
  313.0 4.6 add_convert_fusion.1
  318.0 24.6 %shard_map.498 = (bf16[512,3456]{1,0:T(8,128)(2,1)}, bf16[2,3,8,72,512]{4,3,2,1,0:T(8,128)(2,1)}) custom-call(s32[8]{0:T(128)} %stack.32.refs_0_.place_ref, bf16[48,72,512]{2,1,0:T(8,128)(2,1)} %get-tuple-element.97.refs_1_, bf16[16,72,512]{2,1,0:T(8,128)(2,1)} %get-tuple-element.121.refs_2_, bf16[4,128,1152]{2,1,0:T(8,128)(2,1)} %fusion.30.refs_3_, ...), custom_call_target="tpu_custom_call" | custom-call | flops 149999992832 | bytes 450000000 | tf_op jit(solution)/shard_map/pallas_call | solution.py:118
  344.2 8.2 %collective-permute-done.42 = bf16[4,128,1152]{2,1,0:T(8,128)(2,1)} collective-permute-done((bf16[4,128,1152]{2,1,0:T(8,128)(2,1)}, bf16[4,128,1152]{2,1,0:T(8,128)(2,1)}, u32[]{:S(2)}, u32[]{:S(2)}) %collective-permute-start.42) | collective-permute-done | bytes 1179680 | tf_op jit(solution)/shard_map/ppermute | solution.py:593
  352.4 2.6 fusion.2.rest_2_
  357.0 6.3 %shard_map.499 = (bf16[1728,1152]{1,0:T(8,128)(2,1)S(1)}, bf16[1728,1152]{1,0:T(8,128)(2,1)}) custom-call(bf16[2,1728,512]{2,1,0:T(8,128)(2,1)S(1)} %bitcast.499, bf16[2,1728,512]{2,1,0:T(8,128)(2,1)S(1)} %bitcast.500, bf16[512,1152]{1,0:T(8,128)(2,1)S(1)} %copy-done.10, bf16[4,72,1280]{2,1,0:T(8,128)(2,1)S(1)} %fusion.14.rest_0_, ...), custom_call_target="tpu_custom_call" | custom-call | flops 3000000000 | bytes 9000000 | tf_op jit(solution)/shard_map/pallas_call | solution.py:535
  368.9 5.4 collective-permute-done.45
  378.4 9.6 %reduce-scatter.11.cloned.1.call-done = bf16[72,1280]{1,0:T(8,128)(2,1)} async-done(((bf16[288,1280]{1,0:T(8,128)(2,1)}), bf16[72,1280]{1,0:T(8,128)(2,1)}) %reduce-scatter.11.cloned.1.call-update) | async-done | bytes 184336 | tf_op jit(solution)/shard_map/reduce_scatter | solution.py:675
  395.1 3.7 fusion
  400.4 15.1 %shard_map.500 = (bf16[512,1152]{1,0:T(8,128)(2,1)}, f32[8,1152]{1,0:T(8,128)}) custom-call(s32[8]{0:T(128)} %stack.32.refs_0_.place_ref, bf16[512,3456]{1,0:T(8,128)(2,1)} %get-tuple-element.124.refs_1_, bf16[512,1152]{1,0:T(8,128)(2,1)} %bitcast.540, f32[512,1152]{1,0:T(8,128)} %get-tuple-element.122.refs_3_, ...), custom_call_target="tpu_custom_call" | custom-call | flops 17999998976 | bytes 54000000 | tf_op jit(solution)/shard_map/pallas_call | solution.py:118
  415.6 2.3 fusion.15.refs_14_
  421.2 2.5 collective-permute-done.44
  426.4 16.2 %shard_map.502 = (bf16[512,1152]{1,0:T(8,128)(2,1)}, f32[8,1152]{1,0:T(8,128)}) custom-call(s32[8]{0:T(128)} %stack.32.refs_0_.place_ref, bf16[512,4608]{1,0:T(8,128)(2,1)} %get-tuple-element.106.right_ref.refs_1_, bf16[512,1152]{1,0:T(8,128)(2,1)} %bitcast.541, f32[512,1152]{1,0:T(8,128)} %get-tuple-element.107.refs_4_.refs_3_, ...), custom_call_target="tpu_custom_call" | custom-call | flops 17999998976 | bytes 54000000 | tf_op jit(solution)/shard_map/pallas_call | solution.py:118
  450.8 9.5 %collective-permute-done.48 = bf16[4,72,1152]{2,1,0:T(8,128)(2,1)S(1)} collective-permute-done((bf16[4,72,1152]{2,1,0:T(8,128)(2,1)S(1)}, bf16[4,72,1152]{2,1,0:T(8,128)(2,1)S(1)}, u32[]{:S(2)}, u32[]{:S(2)}) %collective-permute-start.48) | collective-permute-done | bytes 663584 | tf_op jit(solution)/shard_map/ppermute | solution.py:593
  470.8 6.5 %reduce-scatter.17.cloned.1.call-done = bf16[72,2304]{1,0:T(8,128)(2,1)} async-done(((bf16[288,2304]{1,0:T(8,128)(2,1)}), bf16[72,2304]{1,0:T(8,128)(2,1)}) %reduce-scatter.17.cloned.1.call-update) | async-done | bytes 331792 | tf_op jit(solution)/shard_map/reduce_scatter | solution.py:675
  477.4 5.9 %fusion.46 = (bf16[1,4608,72]{1,2,0:T(8,128)(2,1)}, f32[72,4608]{1,0:T(8,128)}, f32[1,4608,72]{1,2,0:T(8,128)}, f32[1,4608,72]{1,2,0:T(8,128)}) fusion(f32[1,4608,72]{1,2,0:T(8,128)} %param.53, f32[72,1280]{1,0:T(8,128)} %get-tuple-element.195, f32[72,1280]{1,0:T(8,128)} %get-tuple-element.194, f32[72,2048]{1,0:T(8,128)} %convert_add_fusion.12, ...), kind=kLoop, calls=%fused_computation.115 | loop fusion | flops 6635520 | bytes 9953281 | tf_op jit(solution)/shard_map/convert_element_type | solution.py:961
  486.0 2.4 collective-permute-start.54
  493.8 8.1 %reduce-scatter.19.cloned.1.call-done = bf16[72,1152]{1,0:T(8,128)(2,1)} async-done(((bf16[288,1152]{1,0:T(8,128)(2,1)}), bf16[72,1152]{1,0:T(8,128)(2,1)}) %reduce-scatter.19.cloned.1.call-update) | async-done | bytes 165904
  505.6 5.5 %fusion.45 = (bf16[1,1152,288]{1,2,0:T(8,128)(2,1)}, f32[288,1152]{1,0:T(8,128)}, f32[1,1152,288]{1,2,0:T(8,128)}, f32[1,1152,288]{1,2,0:T(8,128)}) fusion(f32[1,1152,288]{1,2,0:T(8,128)} %param.52, f32[80,1152]{1,0:T(8,128)S(1)} %get-tuple-element.197, f32[80,1152]{1,0:T(8,128)S(1)} %get-tuple-element.196, f32[128,1152]{1,0:T(8,128)S(1)} %copy-done.26, ...), kind=kLoop, calls=%fused_computation.114 | loop fusion | flops 6635520 | bytes 9953281 | tf_op jit(solution)/shard_map/convert_element_type | solution.py:961
  513.1 5.6 %convert_bitcast_fusion = (bf16[1,1152,432]{1,2,0:T(8,128)(2,1)}, f32[1152,432]{0,1:T(8,128)}, f32[1,1152,432]{1,2,0:T(8,128)}, f32[1,1152,432]{1,2,0:T(8,128)}) fusion(f32[1,1152,432]{1,2,0:T(8,128)S(1)} %copy-done.49, f32[1,1152,432]{1,2,0:T(8,128)S(1)} %copy-done.50, f32[1,1152,432]{1,2,0:T(8,128)S(1)} %copy-done.15, pred[]{:T(512)S(6)} %eq.58, ...), kind=kOutput, calls=%fused_computation.105 | convolution fusion | flops 33887232 | bytes 12983041 | tf_op jit(solution)/shard_map/dot_general | solution.py:27
  530.5 2.9 fusion.47
  (386 shorter events, 142.6 us)
Async XLA Ops:
  7.2 67.8 %all-gather.7.cloned.1.call-start = ((), (), s32[]{:S(2)}) async-start(), calls=%async_computation.11 | async-start | bytes 2488320 | tf_op jit(solution)/shard_map/all_gather | solution.py:746
  8.8 14.4 %collective-permute-start.11 = (bf16[72,3456]{1,0:T(8,128)(2,1)S(1)}, bf16[72,3456]{1,0:T(8,128)(2,1)S(1)}, u32[]{:S(2)}, u32[]{:S(2)}) collective-permute-start(bf16[72,3456]{1,0:T(8,128)(2,1)S(1)} %pad_maximum_fusion.9), channel_id=1, source_target_pairs={{0,1},{1,0},{2,3},{3,2},{4,5},{5,4},{6,7},{7,6},{8,9},{9,8},{10,11... | collective-permute-start | bytes 1493000 | tf_op jit(solution)/shard_map/ppermute | solution.py:593
  14.4 9.7 %collective-permute-start = (f32[2,4,1152]{2,1,0:T(4,128)S(1)}, f32[2,4,1152]{2,1,0:T(4,128)S(1)}, u32[]{:S(2)}, u32[]{:S(2)}) collective-permute-start(f32[2,4,1152]{2,1,0:T(4,128)S(1)} %dynamic_update_slice.38), channel_id=1, source_target_pairs={{0,2},{2,0},{1,3},{3,1},{4,6},{6,4},{5,7},{7,5},{8,10},{10,8},{9,1... | collective-permute-start | bytes 110600 | tf_op jit(solution)/shard_map/ppermute | solution.py:593
  24.1 91.0 %all-gather.9.cloned.1.call-start = ((), (), s32[]{:S(2)}) async-start(), calls=%async_computation.12 | async-start | bytes 2396160 | tf_op jit(solution)/shard_map/all_gather | solution.py:747
  60.5 98.4 %all-gather.11.cloned.1.call-start = ((), (), s32[]{:S(2)}) async-start(), calls=%async_computation.13 | async-start | bytes 2396160 | tf_op jit(solution)/shard_map/all_gather | solution.py:748
  75.0 41.7 %collective-permute-start.13 = (bf16[4,72,3456]{2,1,0:T(8,128)(2,1)}, bf16[4,72,3456]{2,1,0:T(8,128)(2,1)}, u32[]{:S(2)}, u32[]{:S(2)}) collective-permute-start(bf16[4,72,3456]{2,1,0:T(8,128)(2,1)} %bitcast.527), channel_id=1, source_target_pairs={{0,4},{4,0},{1,5},{5,1},{2,6},{6,2},{3,7},{7,3},{8,12},{12,8},{9,1... | collective-permute-start | bytes 5971976 | tf_op jit(solution)/shard_map/ppermute | solution.py:593
  79.2 288.7 %reduce-scatter.9.cloned.1.call-start = ((), (), s32[]{:S(2)}) async-start(), calls=%async_computation.6 | async-start | bytes 1474560 | tf_op jit(solution)/shard_map/reduce_scatter | solution.py:675
  80.9 35.8 %collective-permute-start.12 = (bf16[4,72,1152]{2,1,0:T(8,128)(2,1)S(1)}, bf16[4,72,1152]{2,1,0:T(8,128)(2,1)}, u32[]{:S(2)}, u32[]{:S(2)}) collective-permute-start(bf16[4,72,1152]{2,1,0:T(8,128)(2,1)S(1)} %slice.311), channel_id=1, source_target_pairs={{0,1},{1,0},{2,3},{3,2},{4,5},{5,4},{6,7},{7,6},{8,9},{9,8},{10,11... | collective-permute-start | bytes 1990664 | tf_op jit(solution)/shard_map/ppermute | solution.py:593
  83.3 53.8 %collective-permute-start.16 = (bf16[4,72,3456]{2,1,0:T(8,128)(2,1)S(1)}, bf16[4,72,3456]{2,1,0:T(8,128)(2,1)}, u32[]{:S(2)}, u32[]{:S(2)}) collective-permute-start(bf16[4,72,3456]{2,1,0:T(8,128)(2,1)S(1)} %bitcast.533), channel_id=1, source_target_pairs={{0,2},{2,0},{1,3},{3,1},{4,6},{6,4},{5,7},{7,5},{8,10},{10,8},{9,1... | collective-permute-start | bytes 5971976 | tf_op jit(solution)/shard_map/ppermute | solution.py:593
  116.7 42.2 %collective-permute-start.18 = (bf16[4,72,3456]{2,1,0:T(8,128)(2,1)}, bf16[4,72,3456]{2,1,0:T(8,128)(2,1)}, u32[]{:S(2)}, u32[]{:S(2)}) collective-permute-start(bf16[4,72,3456]{2,1,0:T(8,128)(2,1)} %collective-permute-done.13.refs_5_.refs_6_.refs_16_.refs_7_), channel_id=1, source_target_pairs={{0,2},{2,0},{1,3},{3,1},{4,6},{6,4},{5,7},{7,5},{8,10},{10,8},{9,1... | collective-permute-start | bytes 5971976 | tf_op jit(solution)/shard_map/ppermute | solution.py:593
  117.8 17.5 %collective-permute-start.15 = (bf16[4,72,1152]{2,1,0:T(8,128)(2,1)S(1)}, bf16[4,72,1152]{2,1,0:T(8,128)(2,1)}, u32[]{:S(2)}, u32[]{:S(2)}) collective-permute-start(bf16[4,72,1152]{2,1,0:T(8,128)(2,1)S(1)} %slice.252), channel_id=1, source_target_pairs={{0,1},{1,0},{2,3},{3,2},{4,5},{5,4},{6,7},{7,6},{8,9},{9,8},{10,11... | collective-permute-start | bytes 1990664 | tf_op jit(solution)/shard_map/ppermute | solution.py:593
  119.4 53.5 %collective-permute-start.22 = (bf16[4,208,1152]{2,1,0:T(8,128)(2,1)}, bf16[4,208,1152]{2,1,0:T(8,128)(2,1)}, u32[]{:S(2)}, u32[]{:S(2)}) collective-permute-start(bf16[4,208,1152]{2,1,0:T(8,128)(2,1)} %bitcast.30.refs_2_.refs_6_), channel_id=1, source_target_pairs={{0,4},{4,0},{1,5},{5,1},{2,6},{6,2},{3,7},{7,3},{8,12},{12,8},{9,1... | collective-permute-start | bytes 5750792 | tf_op jit(solution)/shard_map/ppermute | solution.py:593
  120.8 15.7 %collective-permute-start.17 = (bf16[4,72,1152]{2,1,0:T(8,128)(2,1)}, bf16[4,72,1152]{2,1,0:T(8,128)(2,1)S(1)}, u32[]{:S(2)}, u32[]{:S(2)}) collective-permute-start(bf16[4,72,1152]{2,1,0:T(8,128)(2,1)} %collective-permute-done.12.refs_4_.refs_5_.refs_15_.refs_6_), channel_id=1, source_target_pairs={{0,2},{2,0},{1,3},{3,1},{4,6},{6,4},{5,7},{7,5},{8,10},{10,8},{9,1... | collective-permute-start | bytes 1990664 | tf_op jit(solution)/shard_map/ppermute | solution.py:593
  135.3 23.6 %collective-permute-start.19 = (bf16[4,72,1152]{2,1,0:T(8,128)(2,1)}, bf16[4,72,1152]{2,1,0:T(8,128)(2,1)}, u32[]{:S(2)}, u32[]{:S(2)}) collective-permute-start(bf16[4,72,1152]{2,1,0:T(8,128)(2,1)} %collective-permute-done.15.refs_6_.refs_7_.refs_17_.refs_8_), channel_id=1, source_target_pairs={{0,2},{2,0},{1,3},{3,1},{4,6},{6,4},{5,7},{7,5},{8,10},{10,8},{9,1... | collective-permute-start | bytes 1990664 | tf_op jit(solution)/shard_map/ppermute | solution.py:593
  136.5 58.2 %collective-permute-start.24 = (bf16[4,208,1152]{2,1,0:T(8,128)(2,1)}, bf16[4,208,1152]{2,1,0:T(8,128)(2,1)}, u32[]{:S(2)}, u32[]{:S(2)}) collective-permute-start(bf16[4,208,1152]{2,1,0:T(8,128)(2,1)} %bitcast.30.refs_2_.refs_6_), channel_id=1, source_target_pairs={{0,2},{2,0},{1,3},{3,1},{4,6},{6,4},{5,7},{7,5},{8,10},{10,8},{9,1... | collective-permute-start | bytes 5750792 | tf_op jit(solution)/shard_map/ppermute | solution.py:593
  137.4 37.2 %collective-permute-start.21 = (bf16[4,80,1152]{2,1,0:T(8,128)(2,1)S(1)}, bf16[4,80,1152]{2,1,0:T(8,128)(2,1)S(1)}, u32[]{:S(2)}, u32[]{:S(2)}) collective-permute-start(bf16[4,80,1152]{2,1,0:T(8,128)(2,1)S(1)} %slice.257), channel_id=1, source_target_pairs={{0,1},{1,0},{2,3},{3,2},{4,5},{5,4},{6,7},{7,6},{8,9},{9,8},{10,11... | collective-permute-start | bytes 2211848 | tf_op jit(solution)/shard_map/ppermute | solution.py:593
  172.9 23.9 %collective-permute-start.26 = (bf16[4,208,1152]{2,1,0:T(8,128)(2,1)}, bf16[4,208,1152]{2,1,0:T(8,128)(2,1)S(1)}, u32[]{:S(2)}, u32[]{:S(2)}) collective-permute-start(bf16[4,208,1152]{2,1,0:T(8,128)(2,1)} %collective-permute-done.22.refs_4_.refs_8_), channel_id=1, source_target_pairs={{0,2},{2,0},{1,3},{3,1},{4,6},{6,4},{5,7},{7,5},{8,10},{10,8},{9,1... | collective-permute-start | bytes 5750792 | tf_op jit(solution)/shard_map/ppermute | solution.py:593
  173.0 44.3 %collective-permute-start.29 = (bf16[4,72,3328]{2,1,0:T(8,128)(2,1)S(1)}, bf16[4,72,3328]{2,1,0:T(8,128)(2,1)}, u32[]{:S(2)}, u32[]{:S(2)}) collective-permute-start(bf16[4,72,3328]{2,1,0:T(8,128)(2,1)S(1)} %bitcast.524), channel_id=1, source_target_pairs={{0,4},{4,0},{1,5},{5,1},{2,6},{6,2},{3,7},{7,3},{8,12},{12,8},{9,1... | collective-permute-start | bytes 5750792 | tf_op jit(solution)/shard_map/ppermute | solution.py:593
  176.0 18.6 %collective-permute-start.23 = (bf16[4,80,1152]{2,1,0:T(8,128)(2,1)S(1)}, bf16[4,80,1152]{2,1,0:T(8,128)(2,1)S(1)}, u32[]{:S(2)}, u32[]{:S(2)}) collective-permute-start(bf16[4,80,1152]{2,1,0:T(8,128)(2,1)S(1)} %slice.258), channel_id=1, source_target_pairs={{0,1},{1,0},{2,3},{3,2},{4,5},{5,4},{6,7},{7,6},{8,9},{9,8},{10,11... | collective-permute-start | bytes 2211848 | tf_op jit(solution)/shard_map/ppermute | solution.py:593
  177.5 17.7 %collective-permute-start.25 = (bf16[4,80,1152]{2,1,0:T(8,128)(2,1)S(1)}, bf16[4,80,1152]{2,1,0:T(8,128)(2,1)S(1)}, u32[]{:S(2)}, u32[]{:S(2)}) collective-permute-start(bf16[4,80,1152]{2,1,0:T(8,128)(2,1)S(1)} %collective-permute-done.21.refs_3_.refs_7_), channel_id=1, source_target_pairs={{0,2},{2,0},{1,3},{3,1},{4,6},{6,4},{5,7},{7,5},{8,10},{10,8},{9,1... | collective-permute-start | bytes 2211848 | tf_op jit(solution)/shard_map/ppermute | solution.py:593
  194.7 43.5 %collective-permute-start.31 = (bf16[4,72,3328]{2,1,0:T(8,128)(2,1)S(1)}, bf16[4,72,3328]{2,1,0:T(8,128)(2,1)}, u32[]{:S(2)}, u32[]{:S(2)}) collective-permute-start(bf16[4,72,3328]{2,1,0:T(8,128)(2,1)S(1)} %bitcast.526), channel_id=1, source_target_pairs={{0,2},{2,0},{1,3},{3,1},{4,6},{6,4},{5,7},{7,5},{8,10},{10,8},{9,1... | collective-permute-start | bytes 5750792 | tf_op jit(solution)/shard_map/ppermute | solution.py:593
  195.3 22.0 %collective-permute-start.28 = (bf16[4,72,1280]{2,1,0:T(8,128)(2,1)S(1)}, bf16[4,72,1280]{2,1,0:T(8,128)(2,1)S(1)}, u32[]{:S(2)}, u32[]{:S(2)}) collective-permute-start(bf16[4,72,1280]{2,1,0:T(8,128)(2,1)S(1)} %slice.259), channel_id=1, source_target_pairs={{0,1},{1,0},{2,3},{3,2},{4,5},{5,4},{6,7},{7,6},{8,9},{9,8},{10,11... | collective-permute-start | bytes 2211848 | tf_op jit(solution)/shard_map/ppermute | solution.py:593
  217.3 23.6 %collective-permute-start.33 = (bf16[4,72,3328]{2,1,0:T(8,128)(2,1)}, bf16[4,72,3328]{2,1,0:T(8,128)(2,1)}, u32[]{:S(2)}, u32[]{:S(2)}) collective-permute-start(bf16[4,72,3328]{2,1,0:T(8,128)(2,1)} %collective-permute-done.29.refs_5_.refs_8_), channel_id=1, source_target_pairs={{0,2},{2,0},{1,3},{3,1},{4,6},{6,4},{5,7},{7,5},{8,10},{10,8},{9,1... | collective-permute-start | bytes 5750792 | tf_op jit(solution)/shard_map/ppermute | solution.py:593
  218.8 19.0 %collective-permute-start.30 = (bf16[4,72,1280]{2,1,0:T(8,128)(2,1)S(1)}, bf16[4,72,1280]{2,1,0:T(8,128)(2,1)S(1)}, u32[]{:S(2)}, u32[]{:S(2)}) collective-permute-start(bf16[4,72,1280]{2,1,0:T(8,128)(2,1)S(1)} %slice.260), channel_id=1, source_target_pairs={{0,1},{1,0},{2,3},{3,2},{4,5},{5,4},{6,7},{7,6},{8,9},{9,8},{10,11... | collective-permute-start | bytes 2211848 | tf_op jit(solution)/shard_map/ppermute | solution.py:593
  220.3 18.0 %collective-permute-start.32 = (bf16[4,72,1280]{2,1,0:T(8,128)(2,1)S(1)}, bf16[4,72,1280]{2,1,0:T(8,128)(2,1)S(1)}, u32[]{:S(2)}, u32[]{:S(2)}) collective-permute-start(bf16[4,72,1280]{2,1,0:T(8,128)(2,1)S(1)} %collective-permute-done.28.refs_4_.refs_7_), channel_id=1, source_target_pairs={{0,2},{2,0},{1,3},{3,1},{4,6},{6,4},{5,7},{7,5},{8,10},{10,8},{9,1... | collective-permute-start | bytes 2211848 | tf_op jit(solution)/shard_map/ppermute | solution.py:593
  237.7 19.8 %collective-permute-start.35 = (bf16[2,4,72,4608]{3,2,1,0:T(8,128)(2,1)}, bf16[2,4,72,4608]{3,2,1,0:T(8,128)(2,1)}, u32[]{:S(2)}, u32[]{:S(2)}) collective-permute-start(bf16[2,4,72,4608]{3,2,1,0:T(8,128)(2,1)} %bitcast.535), channel_id=1, source_target_pairs={{0,2},{2,0},{1,3},{3,1},{4,6},{6,4},{5,7},{7,5},{8,10},{10,8},{9,1... | collective-permute-start | bytes 15925256 | tf_op jit(solution)/shard_map/ppermute | solution.py:593
  260.3 41.4 %collective-permute-start.39 = (bf16[4,72,2048]{2,1,0:T(8,128)(2,1)}, bf16[4,72,2048]{2,1,0:T(8,128)(2,1)}, u32[]{:S(2)}, u32[]{:S(2)}) collective-permute-start(bf16[4,72,2048]{2,1,0:T(8,128)(2,1)} %fusion.29.rest_0_), channel_id=1, source_target_pairs={{0,4},{4,0},{1,5},{5,1},{2,6},{6,2},{3,7},{7,3},{8,12},{12,8},{9,1... | collective-permute-start | bytes 3538952 | tf_op jit(solution)/shard_map/ppermute | solution.py:593
  266.3 39.3 %collective-permute-start.38 = (bf16[2,4,72,1280]{3,2,1,0:T(8,128)(2,1)}, bf16[2,4,72,1280]{3,2,1,0:T(8,128)(2,1)}, u32[]{:S(2)}, u32[]{:S(2)}) collective-permute-start(bf16[2,4,72,1280]{3,2,1,0:T(8,128)(2,1)} %get-tuple-element.165.rest_1_), channel_id=1, source_target_pairs={{0,1},{1,0},{2,3},{3,2},{4,5},{5,4},{6,7},{7,6},{8,9},{9,8},{10,11... | collective-permute-start | bytes 4423688 | tf_op jit(solution)/shard_map/ppermute | solution.py:593
  279.1 29.4 %collective-permute-start.36 = (bf16[2,4,288,1152]{3,2,1,0:T(8,128)(2,1)}, bf16[2,4,288,1152]{3,2,1,0:T(8,128)(2,1)}, u32[]{:S(2)}, u32[]{:S(2)}) collective-permute-start(bf16[2,4,288,1152]{3,2,1,0:T(8,128)(2,1)} %bitcast.534), channel_id=1, source_target_pairs={{0,2},{2,0},{1,3},{3,1},{4,6},{6,4},{5,7},{7,5},{8,10},{10,8},{9,1... | collective-permute-start | bytes 15925256 | tf_op jit(solution)/shard_map/ppermute | solution.py:593
  305.5 82.5 %reduce-scatter.11.cloned.1.call-start = ((), (), s32[]{:S(2)}) async-start(), calls=%async_computation.7 | async-start | bytes 921600 | tf_op jit(solution)/shard_map/reduce_scatter | solution.py:675
  307.9 34.6 %collective-permute-start.41 = (bf16[4,72,1280]{2,1,0:T(8,128)(2,1)}, bf16[4,72,1280]{2,1,0:T(8,128)(2,1)}, u32[]{:S(2)}, u32[]{:S(2)}) collective-permute-start(bf16[4,72,1280]{2,1,0:T(8,128)(2,1)} %fusion.39.refs_5_), channel_id=1, source_target_pairs={{0,4},{4,0},{1,5},{5,1},{2,6},{6,2},{3,7},{7,3},{8,12},{12,8},{9,1... | collective-permute-start | bytes 2211848 | tf_op jit(solution)/shard_map/ppermute | solution.py:593
  311.4 41.0 %collective-permute-start.42 = (bf16[4,128,1152]{2,1,0:T(8,128)(2,1)}, bf16[4,128,1152]{2,1,0:T(8,128)(2,1)}, u32[]{:S(2)}, u32[]{:S(2)}) collective-permute-start(bf16[4,128,1152]{2,1,0:T(8,128)(2,1)} %fusion.30.refs_3_), channel_id=1, source_target_pairs={{0,4},{4,0},{1,5},{5,1},{2,6},{6,2},{3,7},{7,3},{8,12},{12,8},{9,1... | collective-permute-start | bytes 3538952 | tf_op jit(solution)/shard_map/ppermute | solution.py:593
  317.6 37.4 %collective-permute-start.37 = (bf16[2,4,80,1152]{3,2,1,0:T(8,128)(2,1)}, bf16[2,4,80,1152]{3,2,1,0:T(8,128)(2,1)}, u32[]{:S(2)}, u32[]{:S(2)}) collective-permute-start(bf16[2,4,80,1152]{3,2,1,0:T(8,128)(2,1)} %get-tuple-element.166.refs_4_), channel_id=1, source_target_pairs={{0,1},{1,0},{2,3},{3,2},{4,5},{5,4},{6,7},{7,6},{8,9},{9,8},{10,11... | collective-permute-start | bytes 4423688 | tf_op jit(solution)/shard_map/ppermute | solution.py:593
  365.4 26.1 %collective-permute-start.43 = (bf16[3,2,4,72,1152]{4,3,2,1,0:T(8,128)(2,1)}, bf16[3,2,4,72,1152]{4,3,2,1,0:T(8,128)(2,1)}, u32[]{:S(2)}, u32[]{:S(2)}) collective-permute-start(bf16[3,2,4,72,1152]{4,3,2,1,0:T(8,128)(2,1)} %bitcast.536), channel_id=1, source_target_pairs={{0,2},{2,0},{1,3},{3,1},{4,6},{6,4},{5,7},{7,5},{8,10},{10,8},{9,1... | collective-permute-start | bytes 11943944 | tf_op jit(solution)/shard_map/ppermute | solution.py:593
  367.9 51.3 %reduce-scatter.13.cloned.1.call-start = ((), (), s32[]{:S(2)}) async-start(), calls=%async_computation.8 | async-start | bytes 1474560 | tf_op jit(solution)/shard_map/reduce_scatter | solution.py:675
  376.4 43.2 %collective-permute-start.46 = (bf16[4,72,1152]{2,1,0:T(8,128)(2,1)}, bf16[4,72,1152]{2,1,0:T(8,128)(2,1)}, u32[]{:S(2)}, u32[]{:S(2)}) collective-permute-start(bf16[4,72,1152]{2,1,0:T(8,128)(2,1)} %fusion.19), channel_id=1, source_target_pairs={{0,4},{4,0},{1,5},{5,1},{2,6},{6,2},{3,7},{7,3},{8,12},{12,8},{9,1... | collective-permute-start | bytes 1990664 | tf_op jit(solution)/shard_map/ppermute | solution.py:593
  376.9 38.6 %collective-permute-start.40 = (bf16[4,80,1152]{2,1,0:T(8,128)(2,1)S(1)}, bf16[4,80,1152]{2,1,0:T(8,128)(2,1)S(1)}, u32[]{:S(2)}, u32[]{:S(2)}) collective-permute-start(bf16[4,80,1152]{2,1,0:T(8,128)(2,1)S(1)} %fusion.41.rest_1_), channel_id=1, source_target_pairs={{0,4},{4,0},{1,5},{5,1},{2,6},{6,2},{3,7},{7,3},{8,12},{12,8},{9,1... | collective-permute-start | bytes 2211848 | tf_op jit(solution)/shard_map/ppermute | solution.py:593
  388.1 55.7 %reduce-scatter.15.cloned.1.call-start = ((), (), s32[]{:S(2)}) async-start(), calls=%async_computation.9 | async-start | bytes 921600 | tf_op jit(solution)/shard_map/reduce_scatter | solution.py:675
  393.6 30.1 %collective-permute-start.44 = (bf16[4,72,1152]{2,1,0:T(8,128)(2,1)}, bf16[4,72,1152]{2,1,0:T(8,128)(2,1)}, u32[]{:S(2)}, u32[]{:S(2)}) collective-permute-start(bf16[4,72,1152]{2,1,0:T(8,128)(2,1)} %fusion.22.refs_13_), channel_id=1, source_target_pairs={{0,4},{4,0},{1,5},{5,1},{2,6},{6,2},{3,7},{7,3},{8,12},{12,8},{9,1... | collective-permute-start | bytes 1990664 | tf_op jit(solution)/shard_map/ppermute | solution.py:593
  398.8 43.7 %collective-permute-start.47 = (bf16[2,4,72,1152]{3,2,1,0:T(8,128)(2,1)}, bf16[2,4,72,1152]{3,2,1,0:T(8,128)(2,1)}, u32[]{:S(2)}, u32[]{:S(2)}) collective-permute-start(bf16[2,4,72,1152]{3,2,1,0:T(8,128)(2,1)} %get-tuple-element.171.refs_14_), channel_id=1, source_target_pairs={{0,1},{1,0},{2,3},{3,2},{4,5},{5,4},{6,7},{7,6},{8,9},{9,8},{10,11... | collective-permute-start | bytes 3981320 | tf_op jit(solution)/shard_map/ppermute | solution.py:593
  419.2 58.2 %reduce-scatter.17.cloned.1.call-start = ((), (), s32[]{:S(2)}) async-start(), calls=%async_computation.10 | async-start | bytes 1658880 | tf_op jit(solution)/shard_map/reduce_scatter | solution.py:675
  443.8 58.1 %reduce-scatter.19.cloned.1.call-start = ((), (), s32[]{:S(2)}) async-start(), calls=%async_computation.14 | async-start | bytes 829440
  445.1 15.2 %collective-permute-start.48 = (bf16[4,72,1152]{2,1,0:T(8,128)(2,1)S(1)}, bf16[4,72,1152]{2,1,0:T(8,128)(2,1)S(1)}, u32[]{:S(2)}, u32[]{:S(2)}) collective-permute-start(bf16[4,72,1152]{2,1,0:T(8,128)(2,1)S(1)} %fusion.44), channel_id=1, source_target_pairs={{0,4},{4,0},{1,5},{5,1},{2,6},{6,2},{3,7},{7,3},{8,12},{12,8},{9,1... | collective-permute-start | bytes 1990664 | tf_op jit(solution)/shard_map/ppermute | solution.py:593
  447.2 15.5 %collective-permute-start.64 = (bf16[72,2048]{1,0:T(8,128)(2,1)}, bf16[72,2048]{1,0:T(8,128)(2,1)}, u32[]{:S(2)}, u32[]{:S(2)}) collective-permute-start(bf16[72,2048]{1,0:T(8,128)(2,1)} %reduce-scatter.9.cloned.1.call-done), channel_id=1, source_target_pairs={{0,1},{1,0},{2,3},{3,2},{4,5},{5,4},{6,7},{7,6},{8,9},{9,8},{10,11... | collective-permute-start | bytes 884744 | tf_op jit(solution)/shard_map/ppermute | solution.py:593
  448.7 17.6 %collective-permute-start.65 = (bf16[72,1280]{1,0:T(8,128)(2,1)S(1)}, bf16[72,1280]{1,0:T(8,128)(2,1)}, u32[]{:S(2)}, u32[]{:S(2)}) collective-permute-start(bf16[72,1280]{1,0:T(8,128)(2,1)S(1)} %copy-done.39), channel_id=1, source_target_pairs={{0,1},{1,0},{2,3},{3,2},{4,5},{5,4},{6,7},{7,6},{8,9},{9,8},{10,11... | collective-permute-start | bytes 552968 | tf_op jit(solution)/shard_map/ppermute | solution.py:593
  468.1 20.2 %collective-permute-start.62 = (bf16[128,1152]{1,0:T(8,128)(2,1)}, bf16[128,1152]{1,0:T(8,128)(2,1)}, u32[]{:S(2)}, u32[]{:S(2)}) collective-permute-start(bf16[128,1152]{1,0:T(8,128)(2,1)} %reduce-scatter.13.cloned.1.call-done), channel_id=1, source_target_pairs={{0,1},{1,0},{2,3},{3,2},{4,5},{5,4},{6,7},{7,6},{8,9},{9,8},{10,11... | collective-permute-start | bytes 884744 | tf_op jit(solution)/shard_map/ppermute | solution.py:593
  469.4 13.9 %collective-permute-start.51 = (f32[4,4,432]{2,1,0:T(4,128)}, f32[4,4,432]{2,1,0:T(4,128)}, u32[]{:S(2)}, u32[]{:S(2)}) collective-permute-start(f32[4,4,432]{2,1,0:T(4,128)} %add.472), channel_id=1, source_target_pairs={{0,4},{4,0},{1,5},{5,1},{2,6},{6,2},{3,7},{7,3},{8,12},{12,8},{9,1... | collective-permute-start | bytes 82952 | tf_op jit(solution)/shard_map/ppermute | solution.py:593
  490.3 11.7 %collective-permute-start.63 = (bf16[80,1152]{1,0:T(8,128)(2,1)S(1)}, bf16[80,1152]{1,0:T(8,128)(2,1)}, u32[]{:S(2)}, u32[]{:S(2)}) collective-permute-start(bf16[80,1152]{1,0:T(8,128)(2,1)S(1)} %copy-done.38), channel_id=1, source_target_pairs={{0,1},{1,0},{2,3},{3,2},{4,5},{5,4},{6,7},{7,6},{8,9},{9,8},{10,11... | collective-permute-start | bytes 552968 | tf_op jit(solution)/shard_map/ppermute | solution.py:593
  (100 other events, 703.3 us)
Sparse Core Ops, SparseCore 0:
  24.2 46.8 all-gather.6
  73.2 41.8 all-gather.8
  117.3 41.5 all-gather.10
  305.6 26.4 reduce-scatter.8
  368.0 19.9 reduce-scatter.10
  390.8 28.3 reduce-scatter.12
  422.0 21.6 reduce-scatter.14
  446.6 30.6 reduce-scatter.16
  480.3 21.6 reduce-scatter.18

commit v5 on v4

--- a/solution.py
+++ b/solution.py
@@ -519,7 +519,7 @@
     sums[0:1] = jnp.sum(fold_a[...], axis=0, keepdims=True)
 
 
-def pair_grads(left, right, ordered_after=(), row_block=288):
+def pair_grads(left, right, us, ordered_after=(), row_block=288):
     _, rows, depth = left.shape
     cols = right.shape[1]
     n_dep = len(ordered_after)
@@ -529,7 +529,6 @@
         send[...] = dot_nn(send_l[0], right_ref[...]).astype(BF16)
         keep[...] = dot_nn(keep_l[0], right_ref[...]).astype(BF16)
 
-    col_block = WIDE * 5 if cols > D else cols
     col_block = cols // 4 if cols > D else cols
     grid = (cols // col_block, rows // row_block)
     return pl.pallas_call(
@@ -544,7 +543,7 @@
         + [any_spec()] * n_dep,
         out_specs=[pl.BlockSpec((row_block, col_block), lambda j, i: (i, j))] * 2,
         compiler_params=pltpu.CompilerParams(vmem_limit_bytes=40 * 2**20),
-        cost_estimate=cost(0.5),
+        cost_estimate=cost(us),
     )(left, left, right, *ordered_after)
 
 
@@ -733,8 +732,7 @@
     parts = sum_all(parts)
     time_pre = parts[0]
     cond_vec = parts[1] + jax.nn.silu(time_pre)
-    cond_act, silu_back = jax.vjp(jax.nn.silu, cond_vec)
-    cond_act = cond_act.astype(BF16)
+    cond_act = jax.nn.silu(cond_vec).astype(BF16)
     mod_part = jnp.where(own[2], contract_cols(cond_act, own_low[2]), 0.0)
     mod_span = mod_part.shape[1]
     mod_row = lax.dynamic_update_slice(
@@ -787,7 +785,7 @@
         steps=4,
         us=2,
     )
-    down_keep, down_send = pair_grads(d_mlp_rel.reshape(2, 8 * span, rows), act)
+    down_keep, down_send = pair_grads(d_mlp_rel.reshape(2, 8 * span, rows), act, 0.5)
     downs = gather_pieces(down_near, lambda main: main[:, :, DOWN_E:], (), (h2,), (act,), (down_keep,))
     cut_down = lambda v: (
         v[..., :DOWN_E],
@@ -837,7 +835,7 @@
         ordered_after=[up_keep],
         us=24,
     )
-    merge_keep, merge_send = pair_grads(d_branch_rel.reshape(2, 8 * span, rows), attended)
+    merge_keep, merge_send = pair_grads(d_branch_rel.reshape(2, 8 * span, rows), attended, 0.02)
     shape = (2, 4, span, width)
     merge_keep = merge_keep.reshape(shape)
     merge_got = swap(merge_send.reshape(shape), "c")
@@ -858,7 +856,7 @@
     down_over = over_y(down_late, (d_qkv,))
     up_over = over_y(up_early)
     attend_keep, attend_send = pair_grads(
-        d_qkv_rel.reshape(2, 24 * span, rows), h1, [down_over, up_late[1], up_over]
+        d_qkv_rel.reshape(2, 24 * span, rows), h1, 0.02, [down_over, up_late[1], up_over]
     )
     cut_attend = lambda v: (v[0], v[1], v[2])
     shape = (3, 2, 4, span, width)
@@ -915,27 +913,6 @@
     d_mod = sum_plane(after(d_vector, first_late_over).reshape(4, 4, mod_span))
     d_mod = lax.dynamic_index_in_dim(d_mod, y * 2 + c, 1, keepdims=False)
     d_mod = turn_z(d_mod, z)
-    grad_mod = contract_rows(d_mod, cond_act.astype(F32), HIGHEST)
-    d_cond_part = jnp.dot(
-        d_mod, own_low[2].astype(F32), precision=HIGHEST, preferred_element_type=F32
-    )
-    d_cond_act = sum_all(after(jnp.where(own[2], d_cond_part, 0.0), late_part))
-    d_cond = silu_back(d_cond_act)[0]
-    d_time_pre = jax.vjp(jax.nn.silu, time_pre)[1](d_cond)[0]
-    d_cond_block = lax.dynamic_slice_in_dim(d_cond, block * span, span, 1)
-    d_time_block = lax.dynamic_slice_in_dim(d_time_pre, block * span, span, 1)
-    grad_table = contract_rows(d_cond_block, one_hot.astype(F32), HIGHEST)
-    grad_time = contract_rows(d_time_block, features.astype(F32), HIGHEST)
-
-    grads = (
-        grad_time,
-        grad_table,
-        grad_mod,
-        jnp.concatenate([first_ends[0][:, :width], *first_ends[1:]]),
-        first_ends[0][:, width:],
-        jnp.concatenate(up_ends),
-        jnp.concatenate(down_ends, axis=1),
-    )
     rates = [
         0.5 * FREQ ** (-0.5),
         0.5,
@@ -945,19 +922,44 @@
         0.5 * D ** (-0.5),
         0.5 * FF ** (-0.5),
     ]
+
+    def updated(number, grad):
+        results = adamw_step(
+            masters[number][0].T, means[number][0].T, squares[number][0].T, grad, rates[number]
+        )
+        return [jnp.where(own[number], result, 0.0).T[None] for result in results]
+
+    updated_mod = updated(2, contract_rows(d_mod, cond_act.astype(F32), HIGHEST))
+    d_cond_part = jnp.dot(
+        d_mod, own_low[2].astype(F32), precision=HIGHEST, preferred_element_type=F32
+    )
+    d_cond_part = after(jnp.where(own[2], d_cond_part, 0.0), early_part)
+    d_cond_part = d_cond_part.reshape(clips, 4, 4 * span)
+    d_cond_act = jnp.sum(turn_z(d_cond_part.transpose(1, 0, 2), z), axis=0)
+    d_cond_act = sum_plane(after(d_cond_act, late_part, updated_mod[0]))
+    d_cond_act = lax.dynamic_slice_in_dim(d_cond_act, (y * 2 + c) * span, span, 1)
+    time_block = lax.dynamic_slice_in_dim(time_pre, block * span, span, 1)
+    cond_block = lax.dynamic_slice_in_dim(cond_vec, block * span, span, 1)
+    d_cond_block = jax.vjp(jax.nn.silu, cond_block)[1](d_cond_act)[0]
+    d_time_block = jax.vjp(jax.nn.silu, time_block)[1](d_cond_block)[0]
+    grad_table = contract_rows(d_cond_block, one_hot.astype(F32), HIGHEST)
+    grad_time = contract_rows(d_time_block, features.astype(F32), HIGHEST)
+
+    grads = (
+        grad_time,
+        grad_table,
+        None,
+        jnp.concatenate([first_ends[0][:, :width], *first_ends[1:]]),
+        first_ends[0][:, width:],
+        jnp.concatenate(up_ends),
+        jnp.concatenate(down_ends, axis=1),
+    )
     new_list, first_list, second_list, copy_list = ([], [], [], [])
     for number in range(7):
-        fresh, mean, square = adamw_step(
-            masters[number][0].T,
-            means[number][0].T,
-            squares[number][0].T,
-            grads[number],
-            rates[number],
-        )
-        fresh = jnp.where(own[number], fresh, 0.0).T[None]
+        fresh, mean, square = updated_mod if number == 2 else updated(number, grads[number])
         new_list.append(fresh)
-        first_list.append(jnp.where(own[number], mean, 0.0).T[None])
-        second_list.append(jnp.where(own[number], square, 0.0).T[None])
+        first_list.append(mean)
+        second_list.append(square)
         copy_list.append(fresh.astype(BF16))
     return (
         block_out.reshape(inputs.shape),

time: 545 us -> 538 us (0.987)
    reduce_scatter x5, waiting for transfers between devices: 18.6 us -> 10.4 us  [over_z(): part = lax.psum_scatter(flat, 'z', scatter_dimension=0, tiled=True)]
    ppermute x56, starting transfers between devices: 56.5 us -> 49.4 us  [swap(): return lax.ppermute(value, axis, [(0, 1), (1, 0)])]
    ppermute x56, waiting for transfers between devices: 75.9 us -> 82.2 us  [swap(): return lax.ppermute(value, axis, [(0, 1), (1, 0)])]
    all_gather x1, waiting for transfers between devices: 31.8 us -> 38.1 us  [on_grid(): up_near = lax.all_gather(up_mine, 'z', axis=0, tiled=False)]
    ppermute x6 -> x9, starting transfers between devices: 10.6 us -> 15.5 us  [turn_z(): got = lax.ppermute(entry, 'z', [(i, (i + step) % 4) for i in range(4)])]
    unnamed x146 -> x140, local copies, waits for them, and re-layouts: 10.9 us -> 11.5 us
  transfers between devices with their start and end apart: 75 -> 76, of which waited for: 32 -> 29; matrix products, arithmetic and copies ran while one was open for 17% -> 17% of each run, Pallas kernels for 31% -> 32%
where the time goes in v5:
time: 538 us; the launch traced here: 532 us
  Pallas kernels  168 us (31%)
  waiting for transfers between devices  162 us (30%)
  other arithmetic  73 us (14%)
  starting transfers between devices  71 us (13%)
  local copies, waits for them, and re-layouts  26.2 us (5%)
  between operations  20.1 us (4%)
  matrix products  11.6 us (2%)
    pallas_call x9, Pallas kernels, run_kernel(): pl.pallas_call(kernel, grid=() if steps is None else (steps,), out_shape=...  142 us
    ppermute x56, waiting for transfers between devices, swap(): return lax.ppermute(value, axis, [(0, 1), (1, 0)])  82.2 us
    ppermute x56, starting transfers between devices, swap(): return lax.ppermute(value, axis, [(0, 1), (1, 0)])  49.4 us
    convert_element_type x17, other arithmetic, add_low(): return total.astype(BF16)  44.6 us
    all_gather x1, waiting for transfers between devices, on_grid(): up_near = lax.all_gather(up_mine, 'z', axis=0, tiled=False)  38.1 us
    all_gather x1, waiting for transfers between devices, on_grid(): down_near = lax.all_gather(down_mine, 'z', axis=0, tiled=False)  20.7 us
    pallas_call x3, Pallas kernels, pair_grads(): pl.pallas_call(kernel, grid=grid, out_shape=[jax.ShapeDtypeStruct((rows,...  17.4 us
    ppermute x9, starting transfers between devices, turn_z(): got = lax.ppermute(entry, 'z', [(i, (i + step) % 4) for i in range(4)])  15.5 us
  transfers between devices with their start and end apart: 76, of which 29 were waited for; matrix products, arithmetic and copies ran while one was open for 17% of the time, Pallas kernels for 32%

profile of v5, /device:TPU:0, one launch (start us, length us, event | category | flops | bytes accessed | tf_op | source)
XLA Modules:
  0.0 532.3 jit_solution(5864260710609160018)
XLA Ops:
  8.8 3.0 collective-permute-start.11
  16.5 7.4 %collective-permute-done.1 = f32[2,4,1152]{2,1,0:T(4,128)S(1)} collective-permute-done((f32[2,4,1152]{2,1,0:T(4,128)S(1)}, f32[2,4,1152]{2,1,0:T(4,128)S(1)}, u32[]{:S(2)}, u32[]{:S(2)}) %collective-permute-start.1) | collective-permute-done | bytes 36896 | tf_op jit(solution)/shard_map/ppermute | solution.py:592
  32.0 2.9 collective-permute-start.4
  38.0 2.9 collective-permute-start.5
  40.9 3.5 collective-permute-start.6
  48.2 5.4 %collective-permute-done.14 = bf16[208,1152]{1,0:T(8,128)(2,1)S(1)} collective-permute-done((bf16[208,1152]{1,0:T(8,128)(2,1)S(1)}, bf16[208,1152]{1,0:T(8,128)(2,1)S(1)}, u32[]{:S(2)}, u32[]{:S(2)}) %collective-permute-start.14) | collective-permute-done | bytes 479264 | tf_op jit(solution)/shard_map/ppermute | solution.py:592
  65.3 3.5 shard_map.490
  68.8 2.6 all-gather.7.cloned.1.call-done
  77.7 38.1 %all-gather.9.cloned.1.call-done = bf16[832,1152]{1,0:T(8,128)(2,1)} async-done(((bf16[208,1152]{1,0:T(8,128)(2,1)}), bf16[832,1152]{1,0:T(8,128)(2,1)}) %all-gather.9.cloned.1.call-update) | async-done | bytes 1916944 | tf_op jit(solution)/shard_map/all_gather | solution.py:745
  121.0 14.5 %collective-permute-done.15.refs_6_.refs_7_.refs_17_.refs_8_ = bf16[4,72,1152]{2,1,0:T(8,128)(2,1)} collective-permute-done((bf16[4,72,1152]{2,1,0:T(8,128)(2,1)S(1)}, bf16[4,72,1152]{2,1,0:T(8,128)(2,1)}, u32[]{:S(2)}, u32[]{:S(2)}) %collective-permute-start.15) | collective-permute-done | bytes 663584 | tf_op jit(solution)/shard_map/ppermute | solution.py:592
  139.0 20.7 %all-gather.11.cloned.1.call-done = bf16[288,3328]{1,0:T(8,128)(2,1)} async-done(((bf16[72,3328]{1,0:T(8,128)(2,1)}), bf16[288,3328]{1,0:T(8,128)(2,1)}) %all-gather.11.cloned.1.call-update) | async-done | bytes 1916944 | tf_op jit(solution)/shard_map/all_gather | solution.py:746
  159.7 14.0 %shard_map.491 = (bf16[512,1152]{1,0:T(8,128)(2,1)}, bf16[48,72,512]{2,1,0:T(8,128)(2,1)}) custom-call(s32[8]{0:T(128)} %stack.32.refs_0_.place_ref, bf16[512,1152]{1,0:T(8,128)(2,1)} %bitcast.535, f32[8,1152]{1,0:T(8,128)} %concatenate.59.refs_2_.refs_3_.refs_5_.refs_4_, bf16[4,72,3456]{2,1,0:T(8,128)(2,1)} %bitcast.527, ...), custom_call_target="tpu_custom_call" | custom-call | flops 12000000000 | bytes 36000000 | tf_op jit(solution)/shard_map/pallas_call | solution.py:118
  178.3 15.4 %shard_map.492 = (bf16[512,1152]{1,0:T(8,128)(2,1)}, f32[512,1152]{1,0:T(8,128)}, bf16[512,1152]{1,0:T(8,128)(2,1)}) custom-call(s32[8]{0:T(128)} %stack.32.refs_0_.place_ref, bf16[48,72,512]{2,1,0:T(8,128)(2,1)} %get-tuple-element.98.refs_1_, bf16[512,1152]{1,0:T(8,128)(2,1)} %bitcast.536, f32[8,1152]{1,0:T(8,128)} %concatenate.59.refs_2_.refs_3_.refs_5_.refs_4_, ...), custom_call_target="tpu_custom_call" | custom-call | flops 12000000000 | bytes 36000000 | tf_op jit(solution)/shard_map/pallas_call | solution.py:118
  199.7 15.0 %shard_map.493 = (bf16[512,4608]{1,0:T(8,128)(2,1)}, bf16[512,4608]{1,0:T(8,128)(2,1)}) custom-call(s32[8]{0:T(128)} %stack.32.refs_0_.place_ref, bf16[512,1152]{1,0:T(8,128)(2,1)} %get-tuple-element.99.refs_1_.right_ref, bf16[4,208,1152]{2,1,0:T(8,128)(2,1)} %bitcast.30.refs_2_.refs_6_, bf16[4,80,1152]{2,1,0:T(8,128)(2,1)} %copy-done.53, ...), custom_call_target="tpu_custom_call" | custom-call | flops 12000000000 | bytes 36000000 | tf_op jit(solution)/shard_map/pallas_call | solution.py:118
  214.7 3.3 collective-permute-done.29.refs_5_.refs_8_
  221.3 2.3 copy-done.12
  223.6 9.2 %shard_map.494 = (bf16[576,4608]{1,0:T(8,128)(2,1)S(1)}, bf16[576,4608]{1,0:T(8,128)(2,1)}) custom-call(bf16[2,576,512]{2,1,0:T(8,128)(2,1)S(1)} %bitcast.501, bf16[2,576,512]{2,1,0:T(8,128)(2,1)S(1)} %bitcast.502, bf16[512,4608]{1,0:T(8,128)(2,1)S(1)} %copy-done.12), custom_call_target="tpu_custom_call" | custom-call | flops 3000000000 | bytes 9000000 | tf_op jit(solution)/shard_map/pallas_call | solution.py:534
  232.8 5.7 %collective-permute-done.30.refs_6_.refs_9_ = bf16[4,72,1280]{2,1,0:T(8,128)(2,1)S(1)} collective-permute-done((bf16[4,72,1280]{2,1,0:T(8,128)(2,1)S(1)}, bf16[4,72,1280]{2,1,0:T(8,128)(2,1)S(1)}, u32[]{:S(2)}, u32[]{:S(2)}) %collective-permute-start.30) | collective-permute-done | bytes 737312 | tf_op jit(solution)/shard_map/ppermute | solution.py:592
  239.3 2.4 collective-permute-done.34.refs_10_.refs_13_
  242.6 15.6 %shard_map.495 = (bf16[512,4608]{1,0:T(8,128)(2,1)}, bf16[4608,512]{1,0:T(8,128)(2,1)}) custom-call(s32[8]{0:T(128)} %stack.32.refs_0_.place_ref, bf16[512,1152]{1,0:T(8,128)(2,1)} %get-tuple-element.115.refs_1_, bf16[512,4608]{1,0:T(8,128)(2,1)} %get-tuple-element.116.refs_2_, bf16[4,72,3328]{2,1,0:T(8,128)(2,1)} %bitcast.520, ...), custom_call_target="tpu_custom_call" | custom-call | flops 96000000000 | bytes 288000000 | tf_op jit(solution)/shard_map/pallas_call | solution.py:118
  258.3 2.8 fusion.29.rest_0_
  262.6 4.5 add_convert_fusion
  268.5 8.9 %shard_map.496 = (bf16[8,288,1152]{2,1,0:T(8,128)(2,1)S(1)}, bf16[8,288,1152]{2,1,0:T(8,128)(2,1)}) custom-call(s32[8]{0:T(128)S(1)} %copy-done.10, bf16[4608,512]{1,0:T(8,128)(2,1)S(1)} %bitcast.504, bf16[4608,512]{1,0:T(8,128)(2,1)S(1)} %bitcast.504, bf16[512,1152]{1,0:T(8,128)(2,1)S(1)} %copy-done.13, bf16[4,72,2048]{2,1,0:T(8,128)(2,1)} %fusion.29.rest_0_, ...), custom_call_target="tpu_custom_call" | custom-call | flops 54000001024 | bytes 162000000 | tf_op jit(solution)/shard_map/pallas_call | solution.py:567
  277.4 2.4 copy-done.3
  279.8 22.6 %shard_map.497 = (f32[512,1152]{1,0:T(8,128)}, bf16[512,1152]{1,0:T(8,128)(2,1)}, bf16[2,8,72,512]{3,2,1,0:T(8,128)(2,1)}, bf16[16,72,512]{2,1,0:T(8,128)(2,1)}, f32[8,1152]{1,0:T(8,128)}) custom-call(s32[8]{0:T(128)} %stack.32.refs_0_.place_ref, bf16[512,4608]{1,0:T(8,128)(2,1)} %get-tuple-element.121.refs_1_, bf16[512,1152]{1,0:T(8,128)(2,1)} %bitcast.537, ...), custom_call_target="tpu_custom_call" | custom-call | flops 143999991808 | bytes 432000000 | tf_op jit(solution)/shard_map/pallas_call | solution.py:118
  302.5 3.8 fusion.3.refs_6_
  309.2 3.0 fusion.30.refs_3_
  313.8 4.6 add_convert_fusion.1
  318.8 24.5 %shard_map.498 = (bf16[512,3456]{1,0:T(8,128)(2,1)}, bf16[2,3,8,72,512]{4,3,2,1,0:T(8,128)(2,1)}) custom-call(s32[8]{0:T(128)} %stack.32.refs_0_.place_ref, bf16[48,72,512]{2,1,0:T(8,128)(2,1)} %get-tuple-element.98.refs_1_, bf16[16,72,512]{2,1,0:T(8,128)(2,1)} %get-tuple-element.122.refs_2_, bf16[4,128,1152]{2,1,0:T(8,128)(2,1)} %fusion.30.refs_3_, ...), custom_call_target="tpu_custom_call" | custom-call | flops 149999992832 | bytes 450000000 | tf_op jit(solution)/shard_map/pallas_call | solution.py:118
  344.9 8.3 %collective-permute-done.42 = bf16[4,128,1152]{2,1,0:T(8,128)(2,1)} collective-permute-done((bf16[4,128,1152]{2,1,0:T(8,128)(2,1)}, bf16[4,128,1152]{2,1,0:T(8,128)(2,1)}, u32[]{:S(2)}, u32[]{:S(2)}) %collective-permute-start.42) | collective-permute-done | bytes 1179680 | tf_op jit(solution)/shard_map/ppermute | solution.py:592
  353.2 2.6 fusion.2.rest_2_
  357.8 6.3 %shard_map.499 = (bf16[1728,1152]{1,0:T(8,128)(2,1)S(1)}, bf16[1728,1152]{1,0:T(8,128)(2,1)}) custom-call(bf16[2,1728,512]{2,1,0:T(8,128)(2,1)S(1)} %bitcast.488, bf16[2,1728,512]{2,1,0:T(8,128)(2,1)S(1)} %bitcast.489, bf16[512,1152]{1,0:T(8,128)(2,1)S(1)} %copy-done.9, bf16[4,72,1280]{2,1,0:T(8,128)(2,1)S(1)} %fusion.14.rest_0_, ...), custom_call_target="tpu_custom_call" | custom-call | flops 120000000 | bytes 360000 | tf_op jit(solution)/shard_map/pallas_call | solution.py:534
  369.7 5.3 %collective-permute-done.45 = bf16[2,4,72,1152]{3,2,1,0:T(8,128)(2,1)} collective-permute-done((bf16[2,4,72,1152]{3,2,1,0:T(8,128)(2,1)S(1)}, bf16[2,4,72,1152]{3,2,1,0:T(8,128)(2,1)}, u32[]{:S(2)}, u32[]{:S(2)}) %collective-permute-start.45) | collective-permute-done | bytes 1327136 | tf_op jit(solution)/shard_map/ppermute | solution.py:592
  379.7 9.1 %reduce-scatter.11.cloned.1.call-done = bf16[72,1280]{1,0:T(8,128)(2,1)} async-done(((bf16[288,1280]{1,0:T(8,128)(2,1)}), bf16[72,1280]{1,0:T(8,128)(2,1)}) %reduce-scatter.11.cloned.1.call-update) | async-done | bytes 184336 | tf_op jit(solution)/shard_map/reduce_scatter | solution.py:674
  395.8 3.7 fusion
  401.1 15.1 %shard_map.500 = (bf16[512,1152]{1,0:T(8,128)(2,1)}, f32[8,1152]{1,0:T(8,128)}) custom-call(s32[8]{0:T(128)} %stack.32.refs_0_.place_ref, bf16[512,3456]{1,0:T(8,128)(2,1)} %get-tuple-element.125.refs_1_, bf16[512,1152]{1,0:T(8,128)(2,1)} %bitcast.538, f32[512,1152]{1,0:T(8,128)} %get-tuple-element.123.refs_3_, ...), custom_call_target="tpu_custom_call" | custom-call | flops 17999998976 | bytes 54000000 | tf_op jit(solution)/shard_map/pallas_call | solution.py:118
  416.3 2.3 fusion.15.refs_14_
  421.9 2.5 collective-permute-done.44
  427.1 16.2 %shard_map.502 = (bf16[512,1152]{1,0:T(8,128)(2,1)}, f32[8,1152]{1,0:T(8,128)}) custom-call(s32[8]{0:T(128)} %stack.32.refs_0_.place_ref, bf16[512,4608]{1,0:T(8,128)(2,1)} %get-tuple-element.107.right_ref.refs_1_, bf16[512,1152]{1,0:T(8,128)(2,1)} %bitcast.539, f32[512,1152]{1,0:T(8,128)} %get-tuple-element.108.refs_4_.refs_3_, ...), custom_call_target="tpu_custom_call" | custom-call | flops 17999998976 | bytes 54000000 | tf_op jit(solution)/shard_map/pallas_call | solution.py:118
  449.5 12.4 %collective-permute-done.48 = bf16[4,72,1152]{2,1,0:T(8,128)(2,1)} collective-permute-done((bf16[4,72,1152]{2,1,0:T(8,128)(2,1)}, bf16[4,72,1152]{2,1,0:T(8,128)(2,1)}, u32[]{:S(2)}, u32[]{:S(2)}) %collective-permute-start.48) | collective-permute-done | bytes 663584 | tf_op jit(solution)/shard_map/ppermute | solution.py:592
  461.9 2.4 fusion.18
  467.8 5.3 %fusion.46 = (bf16[1,4608,72]{1,2,0:T(8,128)(2,1)}, f32[72,4608]{1,0:T(8,128)}, f32[1,4608,72]{1,2,0:T(8,128)}, f32[1,4608,72]{1,2,0:T(8,128)}) fusion(f32[1,4608,72]{1,2,0:T(8,128)} %param.53, f32[72,1280]{1,0:T(8,128)S(1)} %get-tuple-element.197, f32[72,1280]{1,0:T(8,128)S(1)} %get-tuple-element.196, f32[72,2048]{1,0:T(8,128)S(1)} %convert_add_fusion.12, ...), kind=kLoop, calls=%fused_computation.115 | loop fusion | flops 6635520 | bytes 9953281 | tf_op jit(solution)/shard_map/convert_element_type | solution.py:963
  477.5 2.5 collective-permute-done.51
  481.7 2.6 collective-permute-start.54
  492.4 7.8 %convert_bitcast_fusion = (bf16[1,1152,432]{1,2,0:T(8,128)(2,1)}, f32[1152,432]{0,1:T(8,128)}, f32[1,1152,432]{1,2,0:T(8,128)}, f32[1,1152,432]{1,2,0:T(8,128)}) fusion(f32[1,1152,432]{1,2,0:T(8,128)} %param.49, f32[1,1152,432]{1,2,0:T(8,128)} %param.42, f32[1,1152,432]{1,2,0:T(8,128)S(1)} %copy-done.15, pred[]{:T(512)S(6)} %eq.64, ...), kind=kOutput, calls=%fused_computation.105 | convolution fusion | flops 33864192 | bytes 12964609 | tf_op jit(solution)/shard_map/dot_general | solution.py:27
  501.1 3.7 reduce-scatter.19.cloned.1.call-done
  504.8 5.7 %fusion.45 = (bf16[1,1152,288]{1,2,0:T(8,128)(2,1)}, f32[288,1152]{1,0:T(8,128)}, f32[1,1152,288]{1,2,0:T(8,128)}, f32[1,1152,288]{1,2,0:T(8,128)}) fusion(f32[1,1152,288]{1,2,0:T(8,128)} %param.52, f32[80,1152]{1,0:T(8,128)} %get-tuple-element.199, f32[80,1152]{1,0:T(8,128)} %get-tuple-element.198, f32[128,1152]{1,0:T(8,128)} %convert_add_fusion.13, ...), kind=kLoop, calls=%fused_computation.114 | loop fusion | flops 6635520 | bytes 9953281 | tf_op jit(solution)/shard_map/convert_element_type | solution.py:963
  522.8 2.9 fusion.47
  (389 shorter events, 130.9 us)
Async XLA Ops:
  7.2 64.2 %all-gather.7.cloned.1.call-start = ((), (), s32[]{:S(2)}) async-start(), calls=%async_computation.11 | async-start | bytes 2488320 | tf_op jit(solution)/shard_map/all_gather | solution.py:744
  8.8 17.0 %collective-permute-start.11 = (bf16[72,3456]{1,0:T(8,128)(2,1)S(1)}, bf16[72,3456]{1,0:T(8,128)(2,1)S(1)}, u32[]{:S(2)}, u32[]{:S(2)}) collective-permute-start(bf16[72,3456]{1,0:T(8,128)(2,1)S(1)} %pad_maximum_fusion.9), channel_id=1, source_target_pairs={{0,1},{1,0},{2,3},{3,2},{4,5},{5,4},{6,7},{7,6},{8,9},{9,8},{10,11... | collective-permute-start | bytes 1493000 | tf_op jit(solution)/shard_map/ppermute | solution.py:592
  26.7 89.1 %all-gather.9.cloned.1.call-start = ((), (), s32[]{:S(2)}) async-start(), calls=%async_computation.12 | async-start | bytes 2396160 | tf_op jit(solution)/shard_map/all_gather | solution.py:745
  54.6 105.1 %all-gather.11.cloned.1.call-start = ((), (), s32[]{:S(2)}) async-start(), calls=%async_computation.13 | async-start | bytes 2396160 | tf_op jit(solution)/shard_map/all_gather | solution.py:746
  71.4 45.4 %collective-permute-start.13 = (bf16[4,72,3456]{2,1,0:T(8,128)(2,1)}, bf16[4,72,3456]{2,1,0:T(8,128)(2,1)}, u32[]{:S(2)}, u32[]{:S(2)}) collective-permute-start(bf16[4,72,3456]{2,1,0:T(8,128)(2,1)} %bitcast.525), channel_id=1, source_target_pairs={{0,4},{4,0},{1,5},{5,1},{2,6},{6,2},{3,7},{7,3},{8,12},{12,8},{9,1... | collective-permute-start | bytes 5971976 | tf_op jit(solution)/shard_map/ppermute | solution.py:592
  74.5 294.1 %reduce-scatter.9.cloned.1.call-start = ((), (), s32[]{:S(2)}) async-start(), calls=%async_computation.6 | async-start | bytes 1474560 | tf_op jit(solution)/shard_map/reduce_scatter | solution.py:674
  76.2 40.6 %collective-permute-start.12 = (bf16[4,72,1152]{2,1,0:T(8,128)(2,1)S(1)}, bf16[4,72,1152]{2,1,0:T(8,128)(2,1)}, u32[]{:S(2)}, u32[]{:S(2)}) collective-permute-start(bf16[4,72,1152]{2,1,0:T(8,128)(2,1)S(1)} %slice.311), channel_id=1, source_target_pairs={{0,1},{1,0},{2,3},{3,2},{4,5},{5,4},{6,7},{7,6},{8,9},{9,8},{10,11... | collective-permute-start | bytes 1990664 | tf_op jit(solution)/shard_map/ppermute | solution.py:592
  77.7 59.5 %collective-permute-start.16 = (bf16[4,72,3456]{2,1,0:T(8,128)(2,1)S(1)}, bf16[4,72,3456]{2,1,0:T(8,128)(2,1)}, u32[]{:S(2)}, u32[]{:S(2)}) collective-permute-start(bf16[4,72,3456]{2,1,0:T(8,128)(2,1)S(1)} %bitcast.531), channel_id=1, source_target_pairs={{0,2},{2,0},{1,3},{3,1},{4,6},{6,4},{5,7},{7,5},{8,10},{10,8},{9,1... | collective-permute-start | bytes 5971976 | tf_op jit(solution)/shard_map/ppermute | solution.py:592
  116.8 42.8 %collective-permute-start.18 = (bf16[4,72,3456]{2,1,0:T(8,128)(2,1)}, bf16[4,72,3456]{2,1,0:T(8,128)(2,1)}, u32[]{:S(2)}, u32[]{:S(2)}) collective-permute-start(bf16[4,72,3456]{2,1,0:T(8,128)(2,1)} %collective-permute-done.13.refs_5_.refs_6_.refs_16_.refs_7_), channel_id=1, source_target_pairs={{0,2},{2,0},{1,3},{3,1},{4,6},{6,4},{5,7},{7,5},{8,10},{10,8},{9,1... | collective-permute-start | bytes 5971976 | tf_op jit(solution)/shard_map/ppermute | solution.py:592
  118.0 17.5 %collective-permute-start.15 = (bf16[4,72,1152]{2,1,0:T(8,128)(2,1)S(1)}, bf16[4,72,1152]{2,1,0:T(8,128)(2,1)}, u32[]{:S(2)}, u32[]{:S(2)}) collective-permute-start(bf16[4,72,1152]{2,1,0:T(8,128)(2,1)S(1)} %slice.252), channel_id=1, source_target_pairs={{0,1},{1,0},{2,3},{3,2},{4,5},{5,4},{6,7},{7,6},{8,9},{9,8},{10,11... | collective-permute-start | bytes 1990664 | tf_op jit(solution)/shard_map/ppermute | solution.py:592
  119.5 54.2 %collective-permute-start.22 = (bf16[4,208,1152]{2,1,0:T(8,128)(2,1)}, bf16[4,208,1152]{2,1,0:T(8,128)(2,1)}, u32[]{:S(2)}, u32[]{:S(2)}) collective-permute-start(bf16[4,208,1152]{2,1,0:T(8,128)(2,1)} %bitcast.30.refs_2_.refs_6_), channel_id=1, source_target_pairs={{0,4},{4,0},{1,5},{5,1},{2,6},{6,2},{3,7},{7,3},{8,12},{12,8},{9,1... | collective-permute-start | bytes 5750792 | tf_op jit(solution)/shard_map/ppermute | solution.py:592
  121.0 15.7 %collective-permute-start.17 = (bf16[4,72,1152]{2,1,0:T(8,128)(2,1)}, bf16[4,72,1152]{2,1,0:T(8,128)(2,1)S(1)}, u32[]{:S(2)}, u32[]{:S(2)}) collective-permute-start(bf16[4,72,1152]{2,1,0:T(8,128)(2,1)} %collective-permute-done.12.refs_4_.refs_5_.refs_15_.refs_6_), channel_id=1, source_target_pairs={{0,2},{2,0},{1,3},{3,1},{4,6},{6,4},{5,7},{7,5},{8,10},{10,8},{9,1... | collective-permute-start | bytes 1990664 | tf_op jit(solution)/shard_map/ppermute | solution.py:592
  135.5 24.2 %collective-permute-start.19 = (bf16[4,72,1152]{2,1,0:T(8,128)(2,1)}, bf16[4,72,1152]{2,1,0:T(8,128)(2,1)}, u32[]{:S(2)}, u32[]{:S(2)}) collective-permute-start(bf16[4,72,1152]{2,1,0:T(8,128)(2,1)} %collective-permute-done.15.refs_6_.refs_7_.refs_17_.refs_8_), channel_id=1, source_target_pairs={{0,2},{2,0},{1,3},{3,1},{4,6},{6,4},{5,7},{7,5},{8,10},{10,8},{9,1... | collective-permute-start | bytes 1990664 | tf_op jit(solution)/shard_map/ppermute | solution.py:592
  136.7 58.8 %collective-permute-start.24 = (bf16[4,208,1152]{2,1,0:T(8,128)(2,1)}, bf16[4,208,1152]{2,1,0:T(8,128)(2,1)}, u32[]{:S(2)}, u32[]{:S(2)}) collective-permute-start(bf16[4,208,1152]{2,1,0:T(8,128)(2,1)} %bitcast.30.refs_2_.refs_6_), channel_id=1, source_target_pairs={{0,2},{2,0},{1,3},{3,1},{4,6},{6,4},{5,7},{7,5},{8,10},{10,8},{9,1... | collective-permute-start | bytes 5750792 | tf_op jit(solution)/shard_map/ppermute | solution.py:592
  137.5 37.8 %collective-permute-start.21 = (bf16[4,80,1152]{2,1,0:T(8,128)(2,1)S(1)}, bf16[4,80,1152]{2,1,0:T(8,128)(2,1)S(1)}, u32[]{:S(2)}, u32[]{:S(2)}) collective-permute-start(bf16[4,80,1152]{2,1,0:T(8,128)(2,1)S(1)} %slice.257), channel_id=1, source_target_pairs={{0,1},{1,0},{2,3},{3,2},{4,5},{5,4},{6,7},{7,6},{8,9},{9,8},{10,11... | collective-permute-start | bytes 2211848 | tf_op jit(solution)/shard_map/ppermute | solution.py:592
  173.7 23.9 %collective-permute-start.26 = (bf16[4,208,1152]{2,1,0:T(8,128)(2,1)}, bf16[4,208,1152]{2,1,0:T(8,128)(2,1)S(1)}, u32[]{:S(2)}, u32[]{:S(2)}) collective-permute-start(bf16[4,208,1152]{2,1,0:T(8,128)(2,1)} %collective-permute-done.22.refs_4_.refs_8_), channel_id=1, source_target_pairs={{0,2},{2,0},{1,3},{3,1},{4,6},{6,4},{5,7},{7,5},{8,10},{10,8},{9,1... | collective-permute-start | bytes 5750792 | tf_op jit(solution)/shard_map/ppermute | solution.py:592
  173.8 44.3 %collective-permute-start.29 = (bf16[4,72,3328]{2,1,0:T(8,128)(2,1)S(1)}, bf16[4,72,3328]{2,1,0:T(8,128)(2,1)}, u32[]{:S(2)}, u32[]{:S(2)}) collective-permute-start(bf16[4,72,3328]{2,1,0:T(8,128)(2,1)S(1)} %bitcast.522), channel_id=1, source_target_pairs={{0,4},{4,0},{1,5},{5,1},{2,6},{6,2},{3,7},{7,3},{8,12},{12,8},{9,1... | collective-permute-start | bytes 5750792 | tf_op jit(solution)/shard_map/ppermute | solution.py:592
  176.8 18.6 %collective-permute-start.23 = (bf16[4,80,1152]{2,1,0:T(8,128)(2,1)S(1)}, bf16[4,80,1152]{2,1,0:T(8,128)(2,1)S(1)}, u32[]{:S(2)}, u32[]{:S(2)}) collective-permute-start(bf16[4,80,1152]{2,1,0:T(8,128)(2,1)S(1)} %slice.258), channel_id=1, source_target_pairs={{0,1},{1,0},{2,3},{3,2},{4,5},{5,4},{6,7},{7,6},{8,9},{9,8},{10,11... | collective-permute-start | bytes 2211848 | tf_op jit(solution)/shard_map/ppermute | solution.py:592
  178.3 17.7 %collective-permute-start.25 = (bf16[4,80,1152]{2,1,0:T(8,128)(2,1)S(1)}, bf16[4,80,1152]{2,1,0:T(8,128)(2,1)S(1)}, u32[]{:S(2)}, u32[]{:S(2)}) collective-permute-start(bf16[4,80,1152]{2,1,0:T(8,128)(2,1)S(1)} %collective-permute-done.21.refs_3_.refs_7_), channel_id=1, source_target_pairs={{0,2},{2,0},{1,3},{3,1},{4,6},{6,4},{5,7},{7,5},{8,10},{10,8},{9,1... | collective-permute-start | bytes 2211848 | tf_op jit(solution)/shard_map/ppermute | solution.py:592
  195.5 43.5 %collective-permute-start.31 = (bf16[4,72,3328]{2,1,0:T(8,128)(2,1)S(1)}, bf16[4,72,3328]{2,1,0:T(8,128)(2,1)}, u32[]{:S(2)}, u32[]{:S(2)}) collective-permute-start(bf16[4,72,3328]{2,1,0:T(8,128)(2,1)S(1)} %bitcast.524), channel_id=1, source_target_pairs={{0,2},{2,0},{1,3},{3,1},{4,6},{6,4},{5,7},{7,5},{8,10},{10,8},{9,1... | collective-permute-start | bytes 5750792 | tf_op jit(solution)/shard_map/ppermute | solution.py:592
  196.0 22.0 %collective-permute-start.28 = (bf16[4,72,1280]{2,1,0:T(8,128)(2,1)S(1)}, bf16[4,72,1280]{2,1,0:T(8,128)(2,1)S(1)}, u32[]{:S(2)}, u32[]{:S(2)}) collective-permute-start(bf16[4,72,1280]{2,1,0:T(8,128)(2,1)S(1)} %slice.259), channel_id=1, source_target_pairs={{0,1},{1,0},{2,3},{3,2},{4,5},{5,4},{6,7},{7,6},{8,9},{9,8},{10,11... | collective-permute-start | bytes 2211848 | tf_op jit(solution)/shard_map/ppermute | solution.py:592
  218.1 23.6 %collective-permute-start.33 = (bf16[4,72,3328]{2,1,0:T(8,128)(2,1)}, bf16[4,72,3328]{2,1,0:T(8,128)(2,1)}, u32[]{:S(2)}, u32[]{:S(2)}) collective-permute-start(bf16[4,72,3328]{2,1,0:T(8,128)(2,1)} %collective-permute-done.29.refs_5_.refs_8_), channel_id=1, source_target_pairs={{0,2},{2,0},{1,3},{3,1},{4,6},{6,4},{5,7},{7,5},{8,10},{10,8},{9,1... | collective-permute-start | bytes 5750792 | tf_op jit(solution)/shard_map/ppermute | solution.py:592
  219.5 19.0 %collective-permute-start.30 = (bf16[4,72,1280]{2,1,0:T(8,128)(2,1)S(1)}, bf16[4,72,1280]{2,1,0:T(8,128)(2,1)S(1)}, u32[]{:S(2)}, u32[]{:S(2)}) collective-permute-start(bf16[4,72,1280]{2,1,0:T(8,128)(2,1)S(1)} %slice.260), channel_id=1, source_target_pairs={{0,1},{1,0},{2,3},{3,2},{4,5},{5,4},{6,7},{7,6},{8,9},{9,8},{10,11... | collective-permute-start | bytes 2211848 | tf_op jit(solution)/shard_map/ppermute | solution.py:592
  221.0 18.0 %collective-permute-start.32 = (bf16[4,72,1280]{2,1,0:T(8,128)(2,1)S(1)}, bf16[4,72,1280]{2,1,0:T(8,128)(2,1)S(1)}, u32[]{:S(2)}, u32[]{:S(2)}) collective-permute-start(bf16[4,72,1280]{2,1,0:T(8,128)(2,1)S(1)} %collective-permute-done.28.refs_4_.refs_7_), channel_id=1, source_target_pairs={{0,2},{2,0},{1,3},{3,1},{4,6},{6,4},{5,7},{7,5},{8,10},{10,8},{9,1... | collective-permute-start | bytes 2211848 | tf_op jit(solution)/shard_map/ppermute | solution.py:592
  238.5 19.8 %collective-permute-start.35 = (bf16[2,4,72,4608]{3,2,1,0:T(8,128)(2,1)}, bf16[2,4,72,4608]{3,2,1,0:T(8,128)(2,1)}, u32[]{:S(2)}, u32[]{:S(2)}) collective-permute-start(bf16[2,4,72,4608]{3,2,1,0:T(8,128)(2,1)} %bitcast.533), channel_id=1, source_target_pairs={{0,2},{2,0},{1,3},{3,1},{4,6},{6,4},{5,7},{7,5},{8,10},{10,8},{9,1... | collective-permute-start | bytes 15925256 | tf_op jit(solution)/shard_map/ppermute | solution.py:592
  261.1 41.4 %collective-permute-start.39 = (bf16[4,72,2048]{2,1,0:T(8,128)(2,1)}, bf16[4,72,2048]{2,1,0:T(8,128)(2,1)}, u32[]{:S(2)}, u32[]{:S(2)}) collective-permute-start(bf16[4,72,2048]{2,1,0:T(8,128)(2,1)} %fusion.29.rest_0_), channel_id=1, source_target_pairs={{0,4},{4,0},{1,5},{5,1},{2,6},{6,2},{3,7},{7,3},{8,12},{12,8},{9,1... | collective-permute-start | bytes 3538952 | tf_op jit(solution)/shard_map/ppermute | solution.py:592
  267.0 39.3 %collective-permute-start.38 = (bf16[2,4,72,1280]{3,2,1,0:T(8,128)(2,1)}, bf16[2,4,72,1280]{3,2,1,0:T(8,128)(2,1)}, u32[]{:S(2)}, u32[]{:S(2)}) collective-permute-start(bf16[2,4,72,1280]{3,2,1,0:T(8,128)(2,1)} %get-tuple-element.167.rest_1_), channel_id=1, source_target_pairs={{0,1},{1,0},{2,3},{3,2},{4,5},{5,4},{6,7},{7,6},{8,9},{9,8},{10,11... | collective-permute-start | bytes 4423688 | tf_op jit(solution)/shard_map/ppermute | solution.py:592
  279.8 29.4 %collective-permute-start.36 = (bf16[2,4,288,1152]{3,2,1,0:T(8,128)(2,1)}, bf16[2,4,288,1152]{3,2,1,0:T(8,128)(2,1)}, u32[]{:S(2)}, u32[]{:S(2)}) collective-permute-start(bf16[2,4,288,1152]{3,2,1,0:T(8,128)(2,1)} %bitcast.532), channel_id=1, source_target_pairs={{0,2},{2,0},{1,3},{3,1},{4,6},{6,4},{5,7},{7,5},{8,10},{10,8},{9,1... | collective-permute-start | bytes 15925256 | tf_op jit(solution)/shard_map/ppermute | solution.py:592
  306.3 82.5 %reduce-scatter.11.cloned.1.call-start = ((), (), s32[]{:S(2)}) async-start(), calls=%async_computation.7 | async-start | bytes 921600 | tf_op jit(solution)/shard_map/reduce_scatter | solution.py:674
  308.7 34.6 %collective-permute-start.41 = (bf16[4,72,1280]{2,1,0:T(8,128)(2,1)}, bf16[4,72,1280]{2,1,0:T(8,128)(2,1)}, u32[]{:S(2)}, u32[]{:S(2)}) collective-permute-start(bf16[4,72,1280]{2,1,0:T(8,128)(2,1)} %fusion.39.refs_5_), channel_id=1, source_target_pairs={{0,4},{4,0},{1,5},{5,1},{2,6},{6,2},{3,7},{7,3},{8,12},{12,8},{9,1... | collective-permute-start | bytes 2211848 | tf_op jit(solution)/shard_map/ppermute | solution.py:592
  312.2 41.0 %collective-permute-start.42 = (bf16[4,128,1152]{2,1,0:T(8,128)(2,1)}, bf16[4,128,1152]{2,1,0:T(8,128)(2,1)}, u32[]{:S(2)}, u32[]{:S(2)}) collective-permute-start(bf16[4,128,1152]{2,1,0:T(8,128)(2,1)} %fusion.30.refs_3_), channel_id=1, source_target_pairs={{0,4},{4,0},{1,5},{5,1},{2,6},{6,2},{3,7},{7,3},{8,12},{12,8},{9,1... | collective-permute-start | bytes 3538952 | tf_op jit(solution)/shard_map/ppermute | solution.py:592
  318.4 37.4 %collective-permute-start.37 = (bf16[2,4,80,1152]{3,2,1,0:T(8,128)(2,1)}, bf16[2,4,80,1152]{3,2,1,0:T(8,128)(2,1)}, u32[]{:S(2)}, u32[]{:S(2)}) collective-permute-start(bf16[2,4,80,1152]{3,2,1,0:T(8,128)(2,1)} %get-tuple-element.168.refs_4_), channel_id=1, source_target_pairs={{0,1},{1,0},{2,3},{3,2},{4,5},{5,4},{6,7},{7,6},{8,9},{9,8},{10,11... | collective-permute-start | bytes 4423688 | tf_op jit(solution)/shard_map/ppermute | solution.py:592
  366.1 26.1 %collective-permute-start.43 = (bf16[3,2,4,72,1152]{4,3,2,1,0:T(8,128)(2,1)}, bf16[3,2,4,72,1152]{4,3,2,1,0:T(8,128)(2,1)}, u32[]{:S(2)}, u32[]{:S(2)}) collective-permute-start(bf16[3,2,4,72,1152]{4,3,2,1,0:T(8,128)(2,1)} %bitcast.534), channel_id=1, source_target_pairs={{0,2},{2,0},{1,3},{3,1},{4,6},{6,4},{5,7},{7,5},{8,10},{10,8},{9,1... | collective-permute-start | bytes 11943944 | tf_op jit(solution)/shard_map/ppermute | solution.py:592
  368.6 51.3 %reduce-scatter.13.cloned.1.call-start = ((), (), s32[]{:S(2)}) async-start(), calls=%async_computation.8 | async-start | bytes 1474560 | tf_op jit(solution)/shard_map/reduce_scatter | solution.py:674
  377.1 43.2 %collective-permute-start.46 = (bf16[4,72,1152]{2,1,0:T(8,128)(2,1)}, bf16[4,72,1152]{2,1,0:T(8,128)(2,1)}, u32[]{:S(2)}, u32[]{:S(2)}) collective-permute-start(bf16[4,72,1152]{2,1,0:T(8,128)(2,1)} %fusion.19), channel_id=1, source_target_pairs={{0,4},{4,0},{1,5},{5,1},{2,6},{6,2},{3,7},{7,3},{8,12},{12,8},{9,1... | collective-permute-start | bytes 1990664 | tf_op jit(solution)/shard_map/ppermute | solution.py:592
  377.7 68.4 %collective-permute-start.65 = (bf16[72,2048]{1,0:T(8,128)(2,1)}, bf16[72,2048]{1,0:T(8,128)(2,1)}, u32[]{:S(2)}, u32[]{:S(2)}) collective-permute-start(bf16[72,2048]{1,0:T(8,128)(2,1)} %reduce-scatter.9.cloned.1.call-done), channel_id=1, source_target_pairs={{0,1},{1,0},{2,3},{3,2},{4,5},{5,4},{6,7},{7,6},{8,9},{9,8},{10,11... | collective-permute-start | bytes 884744 | tf_op jit(solution)/shard_map/ppermute | solution.py:592
  378.2 38.0 %collective-permute-start.40 = (bf16[4,80,1152]{2,1,0:T(8,128)(2,1)S(1)}, bf16[4,80,1152]{2,1,0:T(8,128)(2,1)S(1)}, u32[]{:S(2)}, u32[]{:S(2)}) collective-permute-start(bf16[4,80,1152]{2,1,0:T(8,128)(2,1)S(1)} %fusion.41.rest_1_), channel_id=1, source_target_pairs={{0,4},{4,0},{1,5},{5,1},{2,6},{6,2},{3,7},{7,3},{8,12},{12,8},{9,1... | collective-permute-start | bytes 2211848 | tf_op jit(solution)/shard_map/ppermute | solution.py:592
  388.8 60.6 %reduce-scatter.15.cloned.1.call-start = ((), (), s32[]{:S(2)}) async-start(), calls=%async_computation.9 | async-start | bytes 921600 | tf_op jit(solution)/shard_map/reduce_scatter | solution.py:674
  394.3 30.1 %collective-permute-start.44 = (bf16[4,72,1152]{2,1,0:T(8,128)(2,1)}, bf16[4,72,1152]{2,1,0:T(8,128)(2,1)}, u32[]{:S(2)}, u32[]{:S(2)}) collective-permute-start(bf16[4,72,1152]{2,1,0:T(8,128)(2,1)} %fusion.22.refs_13_), channel_id=1, source_target_pairs={{0,4},{4,0},{1,5},{5,1},{2,6},{6,2},{3,7},{7,3},{8,12},{12,8},{9,1... | collective-permute-start | bytes 1990664 | tf_op jit(solution)/shard_map/ppermute | solution.py:592
  399.6 43.7 %collective-permute-start.47 = (bf16[2,4,72,1152]{3,2,1,0:T(8,128)(2,1)}, bf16[2,4,72,1152]{3,2,1,0:T(8,128)(2,1)}, u32[]{:S(2)}, u32[]{:S(2)}) collective-permute-start(bf16[2,4,72,1152]{3,2,1,0:T(8,128)(2,1)} %get-tuple-element.173.refs_14_), channel_id=1, source_target_pairs={{0,1},{1,0},{2,3},{3,2},{4,5},{5,4},{6,7},{7,6},{8,9},{9,8},{10,11... | collective-permute-start | bytes 3981320 | tf_op jit(solution)/shard_map/ppermute | solution.py:592
  419.9 64.4 %reduce-scatter.17.cloned.1.call-start = ((), (), s32[]{:S(2)}) async-start(), calls=%async_computation.10 | async-start | bytes 1658880 | tf_op jit(solution)/shard_map/reduce_scatter | solution.py:674
  445.4 16.6 %collective-permute-start.48 = (bf16[4,72,1152]{2,1,0:T(8,128)(2,1)}, bf16[4,72,1152]{2,1,0:T(8,128)(2,1)}, u32[]{:S(2)}, u32[]{:S(2)}) collective-permute-start(bf16[4,72,1152]{2,1,0:T(8,128)(2,1)} %fusion.44), channel_id=1, source_target_pairs={{0,4},{4,0},{1,5},{5,1},{2,6},{6,2},{3,7},{7,3},{8,12},{12,8},{9,1... | collective-permute-start | bytes 1990664 | tf_op jit(solution)/shard_map/ppermute | solution.py:592
  447.2 17.3 %collective-permute-start.66 = (bf16[72,1280]{1,0:T(8,128)(2,1)}, bf16[72,1280]{1,0:T(8,128)(2,1)}, u32[]{:S(2)}, u32[]{:S(2)}) collective-permute-start(bf16[72,1280]{1,0:T(8,128)(2,1)} %reduce-scatter.11.cloned.1.call-done), channel_id=1, source_target_pairs={{0,1},{1,0},{2,3},{3,2},{4,5},{5,4},{6,7},{7,6},{8,9},{9,8},{10,11... | collective-permute-start | bytes 552968 | tf_op jit(solution)/shard_map/ppermute | solution.py:592
  449.5 55.3 %reduce-scatter.19.cloned.1.call-start = ((), (), s32[]{:S(2)}) async-start(), calls=%async_computation.14 | async-start | bytes 829440
  473.1 11.2 %collective-permute-start.64 = (bf16[80,1152]{1,0:T(8,128)(2,1)}, bf16[80,1152]{1,0:T(8,128)(2,1)S(1)}, u32[]{:S(2)}, u32[]{:S(2)}) collective-permute-start(bf16[80,1152]{1,0:T(8,128)(2,1)} %reduce-scatter.15.cloned.1.call-done), channel_id=1, source_target_pairs={{0,1},{1,0},{2,3},{3,2},{4,5},{5,4},{6,7},{7,6},{8,9},{9,8},{10,11... | collective-permute-start | bytes 552968 | tf_op jit(solution)/shard_map/ppermute | solution.py:592
  487.7 13.2 %collective-permute-start.55 = (f32[1,4,288]{2,0,1:T(1,128)S(1)}, f32[1,4,288]{2,0,1:T(1,128)S(1)}, u32[]{:S(2)}, u32[]{:S(2)}) collective-permute-start(f32[1,4,288]{2,0,1:T(1,128)S(1)} %get-tuple-element.212), channel_id=1, source_target_pairs={{0,8},{8,16},{16,24},{24,0},{1,9},{9,17},{17,25},{25,1},{2,10},{10... | collective-permute-start | bytes 13832 | tf_op jit(solution)/shard_map/ppermute | solution.py:614
  489.4 11.5 %collective-permute-start.56 = (f32[1,4,288]{2,0,1:T(1,128)S(1)}, f32[1,4,288]{2,0,1:T(1,128)S(1)}, u32[]{:S(2)}, u32[]{:S(2)}) collective-permute-start(f32[1,4,288]{2,0,1:T(1,128)S(1)} %get-tuple-element.211), channel_id=1, source_target_pairs={{0,16},{8,24},{16,0},{24,8},{1,17},{9,25},{17,1},{25,9},{2,18},{10... | collective-permute-start | bytes 13832 | tf_op jit(solution)/shard_map/ppermute | solution.py:614
  500.3 11.8 %collective-permute-start.61 = (bf16[72,2304]{1,0:T(8,128)(2,1)}, bf16[72,2304]{1,0:T(8,128)(2,1)S(1)}, u32[]{:S(2)}, u32[]{:S(2)}) collective-permute-start(bf16[72,2304]{1,0:T(8,128)(2,1)} %reduce-scatter.17.cloned.1.call-done), channel_id=1, source_target_pairs={{0,1},{1,0},{2,3},{3,2},{4,5},{5,4},{6,7},{7,6},{8,9},{9,8},{10,11... | collective-permute-start | bytes 995336 | tf_op jit(solution)/shard_map/ppermute | solution.py:592
  (99 other events, 668.6 us)
Sparse Core Ops, SparseCore 0:
  26.9 44.4 all-gather.6
  73.5 42.2 all-gather.8
  118.0 41.5 all-gather.10
  306.4 26.4 reduce-scatter.8
  368.7 20.0 reduce-scatter.10
  391.5 28.2 reduce-scatter.12
  422.8 21.6 reduce-scatter.14
  449.6 30.4 reduce-scatter.16
  484.5 20.2 reduce-scatter.18
